TPU v7x, 128 devices: a whole 4x4x4 slice. The times are simulated.
128 devices in a mesh: row: 16 (over y_lo, x, core), col: 8 (over z, y_hi).
Axes of the slice: x: 4, y: 4 (y_hi: 2, y_lo: 2; y = y_hi * 2 + y_lo), z: 4, core: 2. Of those that a mesh axis runs over, the one named last changes fastest.
Arguments:
- passages: float32 [131072, 1024], P('row', 'col'), may hold values from -6 to 6
- list_ids: int32 [131072], P('row'), may hold values from 0 to 4095
- code_ids: int32 [131072, 64], P('row', 'col'), may hold values from 0 to 255
- old_centroids: float32 [4096, 1024], P('row', 'col'), may hold values from -6 to 6
- old_codebook: float32 [256, 1024], P('row', 'col'), may hold values from -5 to 5
Outputs:
- centroids: float32 [4096, 1024], P('row', 'col')
- codebook: float32 [256, 1024], P('row', 'col')
- distortion: float32 [131072], P('row')
All inputs are finite; a program needn't handle non-finite values.
Results may differ from a plain program's by a relative error of at most 0.000082.
Values sent between devices are 32-bit elements; how exact they have to be, the bound alone decides.
No kernel may reach another device: no remote copies, remote signals or barrier semaphores. Data moves between devices by JAX's collectives and lax.ppermute only.
A program may use at most 64 MiB of HBM per device.

v0:
```python
import math

import jax
import jax.numpy as jnp
from jax import lax
from jax.sharding import PartitionSpec as P

D = 1024
SUBS = 64


HIGH = lax.Precision.HIGHEST


def blocked(array, block):
    return array.reshape((array.shape[0] // block, block) + array.shape[1:])


def local(passages, list_ids, code_ids, old_centroids, old_codebook):
    rows, width = passages.shape
    n_row = lax.axis_size("row")
    total = rows * n_row
    owned_lists = old_centroids.shape[0]
    owned_codes = old_codebook.shape[0]
    lists = owned_lists * n_row
    codes = owned_codes * n_row
    sub_dim = D // SUBS
    subs_here = width // sub_dim
    list_prior = float(total // lists)
    code_prior = float(total // codes)
    block = math.gcd(rows, 512)
    pass_blocks = blocked(passages, block)
    id_blocks = blocked(list_ids, block)
    code_blocks = blocked(code_ids, block)
    labels = jnp.arange(owned_lists * lax.axis_size("row"), dtype=jnp.int32)

    def step(acc, pair):
        vectors, ids = pair
        hot = (ids[:, None] == labels[None, :]).astype(jnp.float32)
        return (
            acc + jnp.dot(hot.T, vectors, precision=HIGH, preferred_element_type=jnp.float32),
            None,
        )

    acc, _ = lax.scan(
        step,
        jnp.zeros((owned_lists * lax.axis_size("row"), width), jnp.float32),
        (pass_blocks, id_blocks),
    )
    sums = lax.psum_scatter(acc, "row", scatter_dimension=0, tiled=True)
    list_labels = jnp.arange(owned_lists * lax.axis_size("row"), dtype=jnp.int32)

    def step(acc, ids):
        hot = (ids[:, None] == list_labels[None, :]).astype(jnp.float32)
        return (acc + jnp.sum(hot, axis=0), None)

    acc, _ = lax.scan(
        step, jnp.zeros((owned_lists * lax.axis_size("row"),), jnp.float32), id_blocks
    )
    counts = lax.psum_scatter(acc, "row", scatter_dimension=0, tiled=True)
    centroids = (sums + list_prior * old_centroids) / (counts[:, None] + list_prior)
    every_centroid = lax.all_gather(centroids, "row", axis=0, tiled=True)
    residual = passages - jnp.take(every_centroid, list_ids, axis=0)
    resid_blocks = blocked(residual, block)
    same_sub = (
        jnp.arange(subs_here, dtype=jnp.int32)[:, None]
        == jnp.arange(subs_here, dtype=jnp.int32)[None, :]
    ).astype(jnp.float32)

    def code_terms(count):
        labels = jnp.arange(count, dtype=jnp.int32)

        def step(acc, pair):
            vectors, ids = pair
            hot = (ids[:, :, None] == labels[None, None, :]).astype(jnp.float32)
            flat_hot = hot.reshape(hot.shape[0], subs_here * count)
            return (
                acc
                + jnp.dot(flat_hot.T, vectors, precision=HIGH, preferred_element_type=jnp.float32),
                None,
            )

        acc, _ = lax.scan(
            step, jnp.zeros((subs_here * count, width), jnp.float32), (resid_blocks, code_blocks)
        )
        wide = acc.reshape(subs_here, count, subs_here, sub_dim)
        kept = jnp.sum(wide * same_sub[:, None, :, None], axis=0)
        return kept.reshape(count, width)

    def code_tally():
        labels = jnp.arange(owned_codes * lax.axis_size("row"), dtype=jnp.int32)

        def step(acc, ids):
            hot = (ids[:, :, None] == labels[None, None, :]).astype(jnp.float32)
            return (acc + jnp.sum(hot, axis=0), None)

        acc, _ = lax.scan(
            step,
            jnp.zeros((subs_here, owned_codes * lax.axis_size("row")), jnp.float32),
            code_blocks,
        )
        return jnp.transpose(acc, (1, 0))

    code_sums = lax.psum_scatter(
        code_terms(owned_codes * lax.axis_size("row")), "row", scatter_dimension=0, tiled=True
    )
    code_counts = lax.psum_scatter(code_tally(), "row", scatter_dimension=0, tiled=True)
    spread_counts = jnp.repeat(code_counts, sub_dim, axis=1)
    codebook = (code_sums + code_prior * old_codebook) / (spread_counts + code_prior)
    every_code = lax.all_gather(codebook, "row", axis=0, tiled=True)
    book_subs = jnp.transpose(every_code.reshape(codes, subs_here, sub_dim), (1, 0, 2))
    code_labels = jnp.arange(codes, dtype=jnp.int32)

    def error_step(carry, pair):
        vectors, ids = pair
        hot = (ids[:, :, None] == code_labels[None, None, :]).astype(jnp.float32)
        recon = jnp.einsum(
            "bsc,scd->bsd", hot, book_subs, precision=HIGH, preferred_element_type=jnp.float32
        )
        diff = vectors.reshape(vectors.shape[0], subs_here, sub_dim) - recon
        return (carry, jnp.sum(diff * diff, axis=(1, 2)))

    _, error_blocks = lax.scan(error_step, jnp.zeros((), jnp.float32), (resid_blocks, code_blocks))
    errors = error_blocks.reshape(rows)
    distortion = lax.psum(errors, "col") / D
    return (centroids, codebook, distortion)


def solution(mesh):
    in_specs = (P("row", "col"), P("row"), P("row", "col"), P("row", "col"), P("row", "col"))
    out_specs = (P("row", "col"), P("row", "col"), P("row"))
    return jax.shard_map(local, mesh=mesh, in_specs=in_specs, out_specs=out_specs, check_vma=False)
```

profile of v0, /device:TPU:0, one launch (start us, length us, event | category | flops | bytes accessed | tf_op | source)
XLA Modules:
  0.0 630.4 jit_solution(8052011100374467699)
XLA Ops:
  8.0 138.8 %while.56 = (s32[]{:T(128)}, f32[4096,128]{1,0:T(8,128)S(1)}, s32[16,512]{1,0:T(8,128)S(1)}, f32[16,512,128]{2,1,0:T(8,128)}, s32[]{:T(128)}, /*index=5*/s32[]{:T(128)}) while((s32[]{:T(128)}, f32[4096,128]{1,0:T(8,128)S(1)}, s32[16,512]{1,0:T(8,128)S(1)}, f32[16,512,128]{2,1,0:T(8,128)}, s32[]{:T(128)}, ...), condition=%wide.region_1.2_spmd.clone, body=%wide.region_0.1_spmd.clone.sunk | while | flops 3224371200 | bytes 4463187 | solution.py:45
  8.0 8.7 %fusion.38 = f32[4096,128]{1,0:T(8,128)S(1)} fusion(s32[512]{0:T(512)S(1)} %bitcast.88, f32[4096,128]{1,0:T(8,128)S(1)} %get-tuple-element.410, pred[]{:T(512)S(6)} %compare.12, f32[16,512,128]{2,1,0:T(8,128)} %get-tuple-element.418, s32[]{:T(128)} %get-tuple-element.409), kind=kOutput, calls=%fused_computation.17.clone.1 | convolution fusion | flops 3224371200 | bytes 4459009 | tf_op jit(solution)/shard_map/while/body/eval_jaxpr/dot_general | solution.py:41
  16.7 8.6 %fusion.38 = f32[4096,128]{1,0:T(8,128)S(1)} fusion(s32[512]{0:T(512)S(1)} %bitcast.88, f32[4096,128]{1,0:T(8,128)S(1)} %get-tuple-element.410, pred[]{:T(512)S(6)} %compare.12, f32[16,512,128]{2,1,0:T(8,128)} %get-tuple-element.418, s32[]{:T(128)} %get-tuple-element.409), kind=kOutput, calls=%fused_computation.17.clone.1 | convolution fusion | flops 3224371200 | bytes 4459009 | tf_op jit(solution)/shard_map/while/body/eval_jaxpr/dot_general | solution.py:41
  25.4 8.6 %fusion.38 = f32[4096,128]{1,0:T(8,128)S(1)} fusion(s32[512]{0:T(512)S(1)} %bitcast.88, f32[4096,128]{1,0:T(8,128)S(1)} %get-tuple-element.410, pred[]{:T(512)S(6)} %compare.12, f32[16,512,128]{2,1,0:T(8,128)} %get-tuple-element.418, s32[]{:T(128)} %get-tuple-element.409), kind=kOutput, calls=%fused_computation.17.clone.1 | convolution fusion | flops 3224371200 | bytes 4459009 | tf_op jit(solution)/shard_map/while/body/eval_jaxpr/dot_general | solution.py:41
  34.1 8.6 %fusion.38 = f32[4096,128]{1,0:T(8,128)S(1)} fusion(s32[512]{0:T(512)S(1)} %bitcast.88, f32[4096,128]{1,0:T(8,128)S(1)} %get-tuple-element.410, pred[]{:T(512)S(6)} %compare.12, f32[16,512,128]{2,1,0:T(8,128)} %get-tuple-element.418, s32[]{:T(128)} %get-tuple-element.409), kind=kOutput, calls=%fused_computation.17.clone.1 | convolution fusion | flops 3224371200 | bytes 4459009 | tf_op jit(solution)/shard_map/while/body/eval_jaxpr/dot_general | solution.py:41
  42.7 8.6 %fusion.38 = f32[4096,128]{1,0:T(8,128)S(1)} fusion(s32[512]{0:T(512)S(1)} %bitcast.88, f32[4096,128]{1,0:T(8,128)S(1)} %get-tuple-element.410, pred[]{:T(512)S(6)} %compare.12, f32[16,512,128]{2,1,0:T(8,128)} %get-tuple-element.418, s32[]{:T(128)} %get-tuple-element.409), kind=kOutput, calls=%fused_computation.17.clone.1 | convolution fusion | flops 3224371200 | bytes 4459009 | tf_op jit(solution)/shard_map/while/body/eval_jaxpr/dot_general | solution.py:41
  51.4 8.6 %fusion.38 = f32[4096,128]{1,0:T(8,128)S(1)} fusion(s32[512]{0:T(512)S(1)} %bitcast.88, f32[4096,128]{1,0:T(8,128)S(1)} %get-tuple-element.410, pred[]{:T(512)S(6)} %compare.12, f32[16,512,128]{2,1,0:T(8,128)} %get-tuple-element.418, s32[]{:T(128)} %get-tuple-element.409), kind=kOutput, calls=%fused_computation.17.clone.1 | convolution fusion | flops 3224371200 | bytes 4459009 | tf_op jit(solution)/shard_map/while/body/eval_jaxpr/dot_general | solution.py:41
  60.1 8.6 %fusion.38 = f32[4096,128]{1,0:T(8,128)S(1)} fusion(s32[512]{0:T(512)S(1)} %bitcast.88, f32[4096,128]{1,0:T(8,128)S(1)} %get-tuple-element.410, pred[]{:T(512)S(6)} %compare.12, f32[16,512,128]{2,1,0:T(8,128)} %get-tuple-element.418, s32[]{:T(128)} %get-tuple-element.409), kind=kOutput, calls=%fused_computation.17.clone.1 | convolution fusion | flops 3224371200 | bytes 4459009 | tf_op jit(solution)/shard_map/while/body/eval_jaxpr/dot_general | solution.py:41
  68.8 8.6 %fusion.38 = f32[4096,128]{1,0:T(8,128)S(1)} fusion(s32[512]{0:T(512)S(1)} %bitcast.88, f32[4096,128]{1,0:T(8,128)S(1)} %get-tuple-element.410, pred[]{:T(512)S(6)} %compare.12, f32[16,512,128]{2,1,0:T(8,128)} %get-tuple-element.418, s32[]{:T(128)} %get-tuple-element.409), kind=kOutput, calls=%fused_computation.17.clone.1 | convolution fusion | flops 3224371200 | bytes 4459009 | tf_op jit(solution)/shard_map/while/body/eval_jaxpr/dot_general | solution.py:41
  77.4 8.6 %fusion.38 = f32[4096,128]{1,0:T(8,128)S(1)} fusion(s32[512]{0:T(512)S(1)} %bitcast.88, f32[4096,128]{1,0:T(8,128)S(1)} %get-tuple-element.410, pred[]{:T(512)S(6)} %compare.12, f32[16,512,128]{2,1,0:T(8,128)} %get-tuple-element.418, s32[]{:T(128)} %get-tuple-element.409), kind=kOutput, calls=%fused_computation.17.clone.1 | convolution fusion | flops 3224371200 | bytes 4459009 | tf_op jit(solution)/shard_map/while/body/eval_jaxpr/dot_general | solution.py:41
  86.1 8.6 %fusion.38 = f32[4096,128]{1,0:T(8,128)S(1)} fusion(s32[512]{0:T(512)S(1)} %bitcast.88, f32[4096,128]{1,0:T(8,128)S(1)} %get-tuple-element.410, pred[]{:T(512)S(6)} %compare.12, f32[16,512,128]{2,1,0:T(8,128)} %get-tuple-element.418, s32[]{:T(128)} %get-tuple-element.409), kind=kOutput, calls=%fused_computation.17.clone.1 | convolution fusion | flops 3224371200 | bytes 4459009 | tf_op jit(solution)/shard_map/while/body/eval_jaxpr/dot_general | solution.py:41
  94.8 8.6 %fusion.38 = f32[4096,128]{1,0:T(8,128)S(1)} fusion(s32[512]{0:T(512)S(1)} %bitcast.88, f32[4096,128]{1,0:T(8,128)S(1)} %get-tuple-element.410, pred[]{:T(512)S(6)} %compare.12, f32[16,512,128]{2,1,0:T(8,128)} %get-tuple-element.418, s32[]{:T(128)} %get-tuple-element.409), kind=kOutput, calls=%fused_computation.17.clone.1 | convolution fusion | flops 3224371200 | bytes 4459009 | tf_op jit(solution)/shard_map/while/body/eval_jaxpr/dot_general | solution.py:41
  103.4 8.6 %fusion.38 = f32[4096,128]{1,0:T(8,128)S(1)} fusion(s32[512]{0:T(512)S(1)} %bitcast.88, f32[4096,128]{1,0:T(8,128)S(1)} %get-tuple-element.410, pred[]{:T(512)S(6)} %compare.12, f32[16,512,128]{2,1,0:T(8,128)} %get-tuple-element.418, s32[]{:T(128)} %get-tuple-element.409), kind=kOutput, calls=%fused_computation.17.clone.1 | convolution fusion | flops 3224371200 | bytes 4459009 | tf_op jit(solution)/shard_map/while/body/eval_jaxpr/dot_general | solution.py:41
  112.1 8.6 %fusion.38 = f32[4096,128]{1,0:T(8,128)S(1)} fusion(s32[512]{0:T(512)S(1)} %bitcast.88, f32[4096,128]{1,0:T(8,128)S(1)} %get-tuple-element.410, pred[]{:T(512)S(6)} %compare.12, f32[16,512,128]{2,1,0:T(8,128)} %get-tuple-element.418, s32[]{:T(128)} %get-tuple-element.409), kind=kOutput, calls=%fused_computation.17.clone.1 | convolution fusion | flops 3224371200 | bytes 4459009 | tf_op jit(solution)/shard_map/while/body/eval_jaxpr/dot_general | solution.py:41
  120.8 8.6 %fusion.38 = f32[4096,128]{1,0:T(8,128)S(1)} fusion(s32[512]{0:T(512)S(1)} %bitcast.88, f32[4096,128]{1,0:T(8,128)S(1)} %get-tuple-element.410, pred[]{:T(512)S(6)} %compare.12, f32[16,512,128]{2,1,0:T(8,128)} %get-tuple-element.418, s32[]{:T(128)} %get-tuple-element.409), kind=kOutput, calls=%fused_computation.17.clone.1 | convolution fusion | flops 3224371200 | bytes 4459009 | tf_op jit(solution)/shard_map/while/body/eval_jaxpr/dot_general | solution.py:41
  129.5 8.6 %fusion.38 = f32[4096,128]{1,0:T(8,128)S(1)} fusion(s32[512]{0:T(512)S(1)} %bitcast.88, f32[4096,128]{1,0:T(8,128)S(1)} %get-tuple-element.410, pred[]{:T(512)S(6)} %compare.12, f32[16,512,128]{2,1,0:T(8,128)} %get-tuple-element.418, s32[]{:T(128)} %get-tuple-element.409), kind=kOutput, calls=%fused_computation.17.clone.1 | convolution fusion | flops 3224371200 | bytes 4459009 | tf_op jit(solution)/shard_map/while/body/eval_jaxpr/dot_general | solution.py:41
  138.1 8.6 %fusion.38 = f32[4096,128]{1,0:T(8,128)S(1)} fusion(s32[512]{0:T(512)S(1)} %bitcast.88, f32[4096,128]{1,0:T(8,128)S(1)} %get-tuple-element.410, pred[]{:T(512)S(6)} %compare.12, f32[16,512,128]{2,1,0:T(8,128)} %get-tuple-element.418, s32[]{:T(128)} %get-tuple-element.409), kind=kOutput, calls=%fused_computation.17.clone.1 | convolution fusion | flops 3224371200 | bytes 4459009 | tf_op jit(solution)/shard_map/while/body/eval_jaxpr/dot_general | solution.py:41
  148.2 32.7 %while.57 = (s32[]{:T(128)}, f32[4096]{0:T(1024)S(1)}, s32[16,512]{1,0:T(8,128)S(1)}, s32[]{:T(128)}, s32[]{:T(128)}) while((s32[]{:T(128)}, f32[4096]{0:T(1024)S(1)}, s32[16,512]{1,0:T(8,128)S(1)}, s32[]{:T(128)}, s32[]{:T(128)}) %tuple.131), condition=%wide.region_5.6_spmd.clone, body=%wide.region_3.5_spmd.clone.sunk | while | flops 6295555 | bytes 71755 | solution.py:57
  148.2 2.0 convert_reduce_fusion.4
  152.3 2.0 convert_reduce_fusion.4
  156.4 2.0 convert_reduce_fusion.4
  160.5 2.0 convert_reduce_fusion.4
  164.6 2.0 convert_reduce_fusion.4
  182.2 56.1 %all-reduce = f32[4096]{0:T(1024)S(1)} all-reduce(f32[4096]{0:T(1024)S(1)} %get-tuple-element.134), channel_id=3, replica_groups=mesh['row'=16,'col'=8] {'row'}, use_global_device_ids=true, to_apply=%region_6.7.clone | all-reduce | flops 4096 | bytes 32768
  240.1 35.3 %while.59 = (s32[]{:T(128)}, f32[8,256]{1,0:T(8,128)S(1)}, s32[16,512,8]{1,2,0:T(8,128)}, s32[]{:T(128)}, s32[]{:T(128)}) while((s32[]{:T(128)}, f32[8,256]{1,0:T(8,128)S(1)}, s32[16,512,8]{1,2,0:T(8,128)}, s32[]{:T(128)}, s32[]{:T(128)}) %tuple.127), condition=%wide.region_13.14_spmd.clone, body=%wide.region_11.13_spmd.clone.sunk | while | flops 3147779 | bytes 114763 | solution.py:97
  276.6 29.3 %gather_fusion = f32[8192,128]{1,0:T(8,128)} fusion(f32[4096,128]{1,0:T(8,128)} %all-gather.2.cloned.1.call-done, s32[8192]{0:T(1024)S(1)} %fusion.25), kind=kCustom, calls=%fused_computation | custom fusion | bytes 8421376 | tf_op jit(solution)/shard_map/jit(_take)/gather | solution.py:63
  305.9 8.3 %select_subtract_fusion = f32[8192,128]{1,0:T(8,128)} fusion(f32[8192,128]{1,0:T(8,128)} %bitcast.81, f32[8192,128]{1,0:T(8,128)} %gather_fusion, pred[8192]{0:T(1024)(128)(4,1)S(1)} %compare_and_fusion), kind=kLoop, calls=%fused_computation.37 | loop fusion | flops 2097152 | bytes 12591104 | tf_op jit(solution)/shard_map/sub | solution.py:63
  314.2 123.0 %while.58 = (s32[]{:T(128)}, f32[2048,128]{1,0:T(8,128)S(1)}, s32[16,512,8]{1,2,0:T(8,128)}, f32[16,512,128]{2,1,0:T(8,128)}, s32[]{:T(128)}, /*index=5*/s32[]{:T(128)}) while((s32[]{:T(128)}, f32[2048,128]{1,0:T(8,128)S(1)}, s32[16,512,8]{1,2,0:T(8,128)}, f32[16,512,128]{2,1,0:T(8,128)}, s32[]{:T(128)}, ...), condition=%wide.region_8.9_spmd.clone, body=%wide.region_7.8_spmd.clone.sunk | while | flops 1612185600 | bytes 6636115 | solution.py:83
  317.1 4.8 convolution_add_fusion.2
  324.7 4.8 convolution_add_fusion.2
  332.4 4.8 convolution_add_fusion.2
  340.1 4.8 convolution_add_fusion.2
  347.8 4.8 convolution_add_fusion.2
  355.5 4.8 convolution_add_fusion.2
  363.2 4.8 convolution_add_fusion.2
  370.9 4.8 convolution_add_fusion.2
  378.6 4.8 convolution_add_fusion.2
  386.2 4.8 convolution_add_fusion.2
  393.9 4.8 convolution_add_fusion.2
  401.6 4.8 convolution_add_fusion.2
  409.3 4.8 convolution_add_fusion.2
  417.0 4.8 convolution_add_fusion.2
  424.7 4.8 convolution_add_fusion.2
  432.4 4.8 convolution_add_fusion.2
  440.1 58.8 %reduce-scatter.10.cloned.1.call-done = f32[16,128]{1,0:T(8,128)} async-done(((f32[256,128]{1,0:T(8,128)}), f32[16,128]{1,0:T(8,128)}) %reduce-scatter.10.cloned.1.call-update) | async-done | bytes 8208 | tf_op jit(solution)/shard_map/reduce_scatter | solution.py:104
  499.6 16.3 %all_gather.7 = f32[256,128]{1,0:T(8,128)S(1)} all-gather(f32[16,128]{1,0:T(8,128)S(1)} %add_divide_fusion.1), channel_id=1, replica_groups=mesh['row'=16,'col'=8] {'row'}, dimensions={0}, use_global_device_ids=true | all-gather | bytes 139264 | tf_op jit(solution)/shard_map/all_gather | solution.py:110
  516.0 65.7 %while.55 = (s32[]{:T(128)}, f32[16,512]{1,0:T(8,128)S(1)}, f32[16,512,128]{2,1,0:T(8,128)}, s32[16,512,8]{1,2,0:T(8,128)}, f32[8,256,16]{1,2,0:T(8,128)S(1)}, /*index=5*/s32[]{:T(128)}, s32[]{:T(128)}) while((s32[]{:T(128)}, f32[16,512]{1,0:T(8,128)S(1)}, f32[16,512,128]{2,1,0:T(8,128)}, s32[16,512,8]{1,2,0:T(8,128)}, ...), condition=%wide.region_17.18_spmd.clone, body=%wide.region_15.17_spmd.clone.sunk | while | flops 202571264 | bytes 1497177 | solution.py:123
  517.8 2.2 fusion.36
  522.0 2.2 fusion.36
  526.1 2.2 fusion.36
  530.2 2.2 fusion.36
  534.3 2.2 fusion.36
  538.4 2.2 fusion.36
  542.5 2.2 fusion.36
  546.6 2.2 fusion.36
  550.7 2.2 fusion.36
  554.8 2.2 fusion.36
  558.9 2.2 fusion.36
  563.0 2.2 fusion.36
  567.1 2.2 fusion.36
  571.2 2.2 fusion.36
  575.3 2.2 fusion.36
  579.4 2.2 fusion.36
  581.7 41.6 %psum.7 = f32[8192]{0:T(1024)S(1)} all-reduce(f32[8192]{0:T(1024)S(1)} %bitcast.86), channel_id=1, replica_groups=mesh['row'=16,'col'=8] {'col'}, use_global_device_ids=true, to_apply=%region_18.19 | all-reduce | flops 8192 | bytes 65536 | tf_op jit(solution)/shard_map/psum | solution.py:125
  (300 shorter events, 142.8 us)
Async XLA Ops:
  7.2 231.2 %reduce-scatter.8.cloned.1.call-start = ((), (), s32[]{:S(2)}) async-start(), calls=%async_computation.3 | async-start | bytes 2228224 | tf_op jit(solution)/shard_map/reduce_scatter | solution.py:50
  8.0 173.0 %copy-start.5 = (u32[128]{0:T(128)S(1)}, u32[128]{0:T(128)}, u32[]{:S(2)}) copy-start(u32[128]{0:T(128)} %constant.78) | copy-start | bytes 1540
  8.0 230.4 %copy-start.2 = (f32[256,128]{1,0:T(8,128)S(1)}, f32[256,128]{1,0:T(8,128)}, u32[]{:S(2)}) copy-start(f32[256,128]{1,0:T(8,128)} %param.18) | copy-start | bytes 393220
  146.8 1.4 copy-start
  146.8 129.8 %copy-start.1 = (s32[8192]{0:T(1024)S(1)}, s32[8192]{0:T(1024)}, u32[]{:S(2)}) copy-start(s32[8192]{0:T(1024)} %param.16) | copy-start | bytes 98308
  148.1 128.5 %all-gather.2.cloned.1.call-start = ((), (), s32[]{:S(2)}) async-start(), calls=%async_computation.4 | async-start | bytes 2228224 | tf_op jit(solution)/shard_map/all_gather | solution.py:62
  240.1 199.0 %reduce-scatter.12.cloned.1.call-start = ((), (), s32[]{:S(2)}) async-start(), calls=%async_computation.6 | async-start | bytes 139264
  276.3 222.6 %reduce-scatter.10.cloned.1.call-start = ((), (), s32[]{:S(2)}) async-start(), calls=%async_computation.5 | async-start | bytes 139264 | tf_op jit(solution)/shard_map/reduce_scatter | solution.py:104
  437.2 61.7 %copy-start.4 = (f32[16,128]{1,0:T(8,128)S(1)}, f32[16,128]{1,0:T(8,128)}, u32[]{:S(2)}) copy-start(f32[16,128]{1,0:T(8,128)} %param.19) | copy-start | bytes 24580
  499.6 16.4 %copy-start.3 = (f32[16,128]{1,0:T(8,128)}, f32[16,128]{1,0:T(8,128)S(1)}, u32[]{:S(2)}) copy-start(f32[16,128]{1,0:T(8,128)S(1)} %add_divide_fusion.1) | copy-start | bytes 24580
Sparse Core Ops, SparseCore 0:
  148.3 65.8 reduce-scatter.7
  240.2 33.6 all-gather.1
  276.4 59.6 reduce-scatter.11
  439.1 59.6 reduce-scatter.9
where the time goes:
time: 636 us; the launch traced here: 630 us
  matrix products  249 us (39%)
  blocking collectives  114 us (18%)
  local copies, waits for them, and re-layouts  103 us (16%)
  other arithmetic  86.8 us (14%)
  waiting for transfers between devices  58.9 us (9%)
  between operations  14.6 us (2%)
    dot_general x16, matrix products, step(): jnp.dot(hot.T, vectors, precision=HIGH, preferred_element_type=jnp.float32)  138 us
    dot_general x16, matrix products, step(): jnp.dot(flat_hot.T, vectors, precision=HIGH, preferred_element_type=jnp.f...  76.6 us
    reduce_scatter x1, waiting for transfers between devices, local(): lax.psum_scatter(code_terms(owned_codes * lax.axis_size('row')), 'row', s...  58.8 us
    unnamed x1, blocking collectives  56.1 us
    reduce_sum x32, other arithmetic, step(): return (acc + jnp.sum(hot, axis=0), None)  52.9 us
    psum x1, blocking collectives, local(): distortion = lax.psum(errors, 'col') / D  41.6 us
    dot_general x16, matrix products, error_step(): jnp.einsum('bsc,scd->bsd', hot, book_subs, precision=HIGH, preferred_elem...  34.8 us
    gather x1, local copies, waits for them, and re-layouts, local(): residual = passages - jnp.take(every_centroid, list_ids, axis=0)  29.3 us
  transfers between devices with their start and end apart: 4, of which 1 were waited for; matrix products, arithmetic and copies ran while one was open for 37% of the time, Pallas kernels for 0%

commit v1 on v0

v1 whole, which is shorter than its diff:
```python
import functools
import jax
import jax.numpy as jnp
from jax import lax
from jax.experimental import pallas as pl
from jax.experimental.pallas import tpu as pltpu

from jax.sharding import PartitionSpec as P

HIGH = lax.Precision.HIGHEST
D = 1024
LANES = 128
SUB_DIM = 16
NACC = 8
SLAB = 8


def sums_kernel(core_ref, ids_ref, idv_ref, codes_ref, x_ref, keep_ref, send_ref, lcnt, ccnt, *accs):
    step = pl.program_id(0)
    block = x_ref.shape[0]
    lists = accs[0].shape[0]
    pieces = keep_ref.shape[0]
    owned = lists // (2 * pieces)

    @pl.when(step == 0)
    def _():
        zero = jnp.zeros((256, LANES), jnp.float32)

        @pl.loop(0, lists // 256)
        def _(i):
            for acc in accs:
                acc[pl.ds(i * 256, 256), :] = zero

        lcnt[...] = jnp.zeros_like(lcnt)
        ccnt[...] = jnp.zeros_like(ccnt)

    base = step * block

    @pl.loop(0, block // UNROLL1)
    def _(i):
        r0 = i * UNROLL1
        for u in range(0, UNROLL1, NACC):
            ids = [ids_ref[base + r0 + u + j] for j in range(NACC)]
            old = [accs[j][pl.ds(ids[j], 1), :] for j in range(NACC)]
            new = [x_ref[pl.ds(r0 + u + j, 1), :] for j in range(NACC)]
            for j in range(NACC):
                accs[j][pl.ds(ids[j], 1), :] = old[j] + new[j]

    nhi = lists // LANES
    hi_iota = lax.broadcasted_iota(jnp.int32, (nhi, LANES), 0)
    lo_iota = lax.broadcasted_iota(jnp.int32, (LANES, LANES), 0)
    his, los = [], []
    for t in range(block // LANES):
        row = idv_ref[pl.ds(step * (block // LANES) + t, 1), :]
        his.append((row // LANES == hi_iota).astype(jnp.bfloat16))
        los.append((row % LANES == lo_iota).astype(jnp.bfloat16))
    nt = (((1,), (1,)), ((), ()))
    lcnt[...] += lax.dot_general(
        jnp.concatenate(his, 1), jnp.concatenate(los, 1), nt, preferred_element_type=jnp.float32
    )
    dig = lax.broadcasted_iota(jnp.int32, (SUB_DIM, block), 0)
    his, los = [], []
    for m in range(codes_ref.shape[0]):
        row = codes_ref[pl.ds(m, 1), :]
        his.append((row // SUB_DIM == dig).astype(jnp.bfloat16))
        los.append((row % SUB_DIM == dig).astype(jnp.bfloat16))
    ccnt[...] += lax.dot_general(
        jnp.concatenate(his, 0), jnp.concatenate(los, 0), nt, preferred_element_type=jnp.float32
    )

    @pl.when(step == pl.num_programs(0) - 1)
    def _():
        core = core_ref[0]
        cc = ccnt[...]
        r = lax.broadcasted_iota(jnp.int32, cc.shape, 0) // SUB_DIM
        c = lax.broadcasted_iota(jnp.int32, cc.shape, 1) // SUB_DIM
        cc = jnp.where(r == c, cc, 0.0)
        crow = cc[0:SUB_DIM, :]
        for m in range(1, codes_ref.shape[0]):
            crow = crow + cc[m * SUB_DIM:(m + 1) * SUB_DIM, :]
        ccnt[0:SUB_DIM, :] = crow
        for out, par in ((keep_ref, core), (send_ref, 1 - core)):
            @pl.loop(0, pieces)
            def _(k):
                owner = 2 * k + par
                start = pl.multiple_of(owner * owned, owned)
                total = accs[0][pl.ds(start, owned), :]
                for acc in accs[1:]:
                    total = total + acc[pl.ds(start, owned), :]
                out[k, 0:owned, :] = total
                out[k, pl.ds(owned, SLAB), :] = jnp.concatenate(
                    [
                        lcnt[pl.ds(owner * (owned // LANES), owned // LANES), :],
                        ccnt[pl.ds(owner, 1), :],
                        jnp.zeros((SLAB - owned // LANES - 1, LANES), jnp.float32),
                    ],
                    0,
                )


UNROLL1 = 32


def list_sums(core, ids, codes_t, x, pieces, lists, block=1024):
    rows, width = x.shape
    owned = lists // (2 * pieces)
    out = jax.ShapeDtypeStruct((pieces, owned + SLAB, width), jnp.float32)
    full = pl.BlockSpec((pieces, owned + SLAB, width), lambda i: (0, 0, 0))
    return pl.pallas_call(
        sums_kernel,
        grid=(rows // block,),
        in_specs=[
            pl.BlockSpec(memory_space=pltpu.SMEM),
            pl.BlockSpec(memory_space=pltpu.SMEM),
            pl.BlockSpec((rows // LANES, LANES), lambda i: (0, 0)),
            pl.BlockSpec((codes_t.shape[0], block), lambda i: (0, i)),
            pl.BlockSpec((block, width), lambda i: (i, 0)),
        ],
        out_specs=[full, full],
        out_shape=[out, out],
        scratch_shapes=[
            pltpu.VMEM((lists // LANES, LANES), jnp.float32),
            pltpu.VMEM((LANES, LANES), jnp.float32),
        ]
        + [pltpu.VMEM((lists, width), jnp.float32)] * NACC,
        compiler_params=pltpu.CompilerParams(vmem_limit_bytes=48 * 2**20),
        name="list_sums",
    )(core, ids, ids.reshape(rows // LANES, LANES), codes_t, x)


def centroid_kernel(prior, part_ref, old_ref, cent_ref, copies_ref, tail_ref):
    owned = old_ref.shape[0]
    total = part_ref[0]
    for k in range(1, part_ref.shape[0]):
        total = total + part_ref[k]
    eye = (
        lax.broadcasted_iota(jnp.int32, (LANES, LANES), 0)
        == lax.broadcasted_iota(jnp.int32, (LANES, LANES), 1)
    )
    for h in range(owned // LANES):
        row = total[owned + h : owned + h + 1, :]
        col = jnp.sum(jnp.where(eye, row, 0.0), axis=1, keepdims=True)
        sl = slice(h * LANES, (h + 1) * LANES)
        cent = (total[sl, :] + prior * old_ref[sl, :]) / (col + prior)
        cent_ref[sl, :] = cent
        for k in range(copies_ref.shape[0]):
            copies_ref[k, sl, :] = cent
    tail_ref[...] = total[owned:, :]


def new_centroids(parts, old, prior):
    n, _, width = parts.shape
    return pl.pallas_call(
        functools.partial(centroid_kernel, prior),
        out_shape=[
            jax.ShapeDtypeStruct(old.shape, jnp.float32),
            jax.ShapeDtypeStruct((n,) + old.shape, jnp.float32),
            jax.ShapeDtypeStruct((SLAB, width), jnp.float32),
        ],
        compiler_params=pltpu.CompilerParams(vmem_limit_bytes=32 * 2**20),
        name="centroids",
    )(parts, old)


UNROLL3 = 32


def resid_kernel(core_ref, ids_ref, codes_ref, x_ref, own_ref, other_ref, rest_ref, sums_ref, table, got):
    step = pl.program_id(0)
    block = x_ref.shape[0]
    pieces, owned, _ = own_ref.shape
    subs = codes_ref.shape[0]
    codes = sums_ref.shape[0]

    @pl.when(step == 0)
    def _():
        core = core_ref[0]
        for k in range(pieces):
            table[pl.ds(pl.multiple_of((2 * k + core) * owned, owned), owned), :] = own_ref[k]
            table[pl.ds(pl.multiple_of((2 * k + 1 - core) * owned, owned), owned), :] = other_ref[k]
        sums_ref[...] = jnp.zeros_like(sums_ref)

    base = step * block

    @pl.loop(0, block // UNROLL3)
    def _(i):
        r0 = i * UNROLL3
        rows = [table[pl.ds(ids_ref[base + r0 + j], 1), :] for j in range(UNROLL3)]
        for j in range(UNROLL3):
            got[pl.ds(r0 + j, 1), :] = rows[j]

    res = x_ref[...] - got[...]
    rest_ref[...] = res.T
    hi = res.astype(jnp.bfloat16)
    lo = (res - hi.astype(jnp.float32)).astype(jnp.bfloat16)
    both = jnp.concatenate([hi, lo], 1)
    lane_sub = lax.broadcasted_iota(jnp.int32, (codes, LANES), 1) // SUB_DIM
    label = lax.broadcasted_iota(jnp.int32, (codes, block), 0)
    total = sums_ref[...]
    for m in range(subs):
        hot = (codes_ref[pl.ds(m, 1), :] == label).astype(jnp.bfloat16)
        part = jnp.dot(hot, both, preferred_element_type=jnp.float32)
        total = total + jnp.where(lane_sub == m, part[:, :LANES] + part[:, LANES:], 0.0)
    sums_ref[...] = total


def residuals(core, ids, codes_t, x, own, other, codes, block=1024):
    rows, width = x.shape
    pieces, owned, _ = own.shape
    whole = pl.BlockSpec(own.shape, lambda i: (0, 0, 0))
    return pl.pallas_call(
        resid_kernel,
        grid=(rows // block,),
        in_specs=[
            pl.BlockSpec(memory_space=pltpu.SMEM),
            pl.BlockSpec(memory_space=pltpu.SMEM),
            pl.BlockSpec((codes_t.shape[0], block), lambda i: (0, i)),
            pl.BlockSpec((block, width), lambda i: (i, 0)),
            whole,
            whole,
        ],
        out_specs=[
            pl.BlockSpec((width, block), lambda i: (0, i)),
            pl.BlockSpec((codes, width), lambda i: (0, 0)),
        ],
        out_shape=[
            jax.ShapeDtypeStruct((width, rows), jnp.float32),
            jax.ShapeDtypeStruct((codes, width), jnp.float32),
        ],
        scratch_shapes=[
            pltpu.VMEM((2 * pieces * owned, width), jnp.float32),
            pltpu.VMEM((block, width), jnp.float32),
        ],
        compiler_params=pltpu.CompilerParams(vmem_limit_bytes=48 * 2**20),
        name="residuals",
    )(core, ids, codes_t, x, own, other)


def errors_kernel(book_ref, codes_ref, rest_ref, out_ref, table):
    width, block = rest_ref.shape
    subs = codes_ref.shape[0]

    @pl.when(pl.program_id(0) == 0)
    def _():
        table[...] = book_ref[...].T

    for t in range(block // LANES):
        cols = slice(t * LANES, (t + 1) * LANES)
        acc = jnp.zeros((8, LANES), jnp.float32)
        for m in range(subs):
            idx = jnp.broadcast_to(codes_ref[m:m + 1, cols], (8, LANES))
            low = idx % LANES
            first = idx < LANES
            for g in range(SUB_DIM // 8):
                f = slice(m * SUB_DIM + g * 8, m * SUB_DIM + g * 8 + 8)
                a = jnp.take_along_axis(table[f, 0:LANES], low, axis=1)
                b = jnp.take_along_axis(table[f, LANES:2 * LANES], low, axis=1)
                d = rest_ref[f, cols] - jnp.where(first, a, b)
                acc = acc + d * d
        out_ref[t:t + 1, :] = jnp.sum(acc, axis=0, keepdims=True)


def errors(book, codes_t, rest, block=1024):
    width, rows = rest.shape
    return pl.pallas_call(
        errors_kernel,
        grid=(rows // block,),
        in_specs=[
            pl.BlockSpec(book.shape, lambda i: (0, 0)),
            pl.BlockSpec((codes_t.shape[0], block), lambda i: (0, i)),
            pl.BlockSpec((width, block), lambda i: (0, i)),
        ],
        out_specs=pl.BlockSpec((block // LANES, LANES), lambda i: (i, 0)),
        out_shape=jax.ShapeDtypeStruct((rows // LANES, LANES), jnp.float32),
        scratch_shapes=[pltpu.VMEM((width, book.shape[0]), jnp.float32)],
        compiler_params=pltpu.CompilerParams(vmem_limit_bytes=48 * 2**20),
        name="errors",
    )(book, codes_t, rest)


def book_kernel(prior, part_ref, tail_ref, old_ref, book_ref, copies_ref):
    total = part_ref[0]
    for k in range(1, part_ref.shape[0]):
        total = total + part_ref[k]
    shape = total.shape
    row = jnp.broadcast_to(tail_ref[2:3, :], shape)
    lane = lax.broadcasted_iota(jnp.int32, shape, 1)
    code = lax.broadcasted_iota(jnp.int32, shape, 0)
    picked = jnp.where(lane % SUB_DIM == code, row, 0.0)
    r = lax.broadcasted_iota(jnp.int32, (LANES, LANES), 0) // SUB_DIM
    c = lax.broadcasted_iota(jnp.int32, (LANES, LANES), 1) // SUB_DIM
    ones = (r == c).astype(jnp.float32)
    counts = jnp.dot(picked, ones, precision=HIGH, preferred_element_type=jnp.float32)
    book = (total + prior * old_ref[...]) / (counts + prior)
    book_ref[...] = book
    for k in range(copies_ref.shape[0]):
        copies_ref[k] = book


def new_codebook(parts, tail, old, prior):
    return pl.pallas_call(
        functools.partial(book_kernel, prior),
        out_shape=[
            jax.ShapeDtypeStruct(old.shape, jnp.float32),
            jax.ShapeDtypeStruct(parts.shape, jnp.float32),
        ],
        name="codebook",
    )(parts, tail, old)


def swap(x, axis, n, bit):
    return lax.ppermute(x, axis, [(i, i ^ bit) for i in range(n)])


def local(passages, list_ids, code_ids, old_centroids, old_codebook):
    rows, width = passages.shape
    n_row = lax.axis_size("row")
    n_col = lax.axis_size("col")
    total = rows * n_row
    owned_lists = old_centroids.shape[0]
    owned_codes = old_codebook.shape[0]
    lists = owned_lists * n_row
    codes = owned_codes * n_row
    list_prior = float(total // lists)
    code_prior = float(total // codes)
    pieces = n_row // 2
    same_core = [[2 * k + c for k in range(pieces)] for c in range(2)]
    core = (lax.axis_index("row") % 2).astype(jnp.int32).reshape(1)
    codes_t = code_ids.T

    keep, send = list_sums(core, list_ids, codes_t, passages, pieces, lists)
    pair = keep + swap(send, "row", n_row, 1)
    parts = lax.all_to_all(pair, "row", 0, 0, axis_index_groups=same_core, tiled=True)
    centroids, copies, tail = new_centroids(parts, old_centroids, list_prior)
    own = lax.all_to_all(copies, "row", 0, 0, axis_index_groups=same_core, tiled=True)
    other = swap(own, "row", n_row, 1)
    rest, sums = residuals(core, list_ids, codes_t, passages, own, other, codes)
    parts = lax.all_to_all(sums.reshape(n_row, owned_codes, width), "row", 0, 0, tiled=True)
    codebook, copies = new_codebook(parts, tail, old_codebook, code_prior)
    book = lax.all_to_all(copies, "row", 0, 0, tiled=True).reshape(codes, width)
    err = errors(book, codes_t, rest)
    bit = 1
    while bit < n_col:
        err = err + swap(err, "col", n_col, bit)
        bit *= 2
    return centroids, codebook, err.reshape(rows) / D


def solution(mesh):
    in_specs = (P("row", "col"), P("row"), P("row", "col"), P("row", "col"), P("row", "col"))
    out_specs = (P("row", "col"), P("row", "col"), P("row"))
    return jax.shard_map(local, mesh=mesh, in_specs=in_specs, out_specs=out_specs, check_vma=False)
```

time: 636 us -> 128 us (0.20)
  matrix products: 249 us -> 0 us
  local copies, waits for them, and re-layouts: 103 us -> 3.9 us
  other arithmetic: 86.8 us -> 0.75 us
  blocking collectives: 114 us -> 59.4 us
  waiting for transfers between devices: 58.9 us -> 11.7 us
  Pallas kernels: 0 us -> 41.6 us
  between operations: 14.6 us -> 0.7 us
  starting transfers between devices: 0.34 us -> 8.87 us
    dot_general x48 -> x0, matrix products: 249 us -> none  [the longest x16 138 us: step(): jnp.dot(hot.T, vectors, precision=HIGH, preferred_element_type=jnp.float32)]
    all_to_all x0 -> x4, blocking collectives: none -> 59.4 us  [the longest x1 21.9 us: local(): lax.all_to_all(pair, 'row', 0, 0, axis_index_groups=same_core, tiled=True)]
    reduce_scatter x2 -> x0, waiting for transfers between devices: 58.8 us -> none  [the longest x1 58.8 us: local(): lax.psum_scatter(code_terms(owned_codes * lax.axis_size('row')), 'row', s...]
    unnamed x1 -> x0, blocking collectives: 56.1 us -> none
    reduce_sum x33 -> x0, other arithmetic: 53.3 us -> none  [the longest x32 52.9 us: step(): return (acc + jnp.sum(hot, axis=0), None)]
    pallas_call x0 -> x5, Pallas kernels: none -> 41.6 us  [the longest x1 20.1 us: residuals(): pl.pallas_call(resid_kernel, grid=(rows // block,), in_specs=[pl.BlockSpe...]
    psum x1 -> x0, blocking collectives: 41.6 us -> none  [local(): distortion = lax.psum(errors, 'col') / D]
    eq x80 -> x0, local copies, waits for them, and re-layouts: 38.7 us -> none  [the longest x64 27.1 us: step(): hot = (ids[:, :, None] == labels[None, None, :]).astype(jnp.float32)]
  transfers between devices with their start and end apart: 4 -> 5, of which waited for: 1 -> 5; matrix products, arithmetic and copies ran while one was open for 37% -> 0% of each run, Pallas kernels for 0% -> 0%
where the time goes in v1:
time: 128 us; the launch traced here: 127 us
  blocking collectives  59.4 us (46%)
  Pallas kernels  41.6 us (32%)
  waiting for transfers between devices  11.7 us (9%)
  starting transfers between devices  8.87 us (7%)
  local copies, waits for them, and re-layouts  3.9 us (3%)
    all_to_all x1, blocking collectives, local(): lax.all_to_all(pair, 'row', 0, 0, axis_index_groups=same_core, tiled=True)  21.9 us
    pallas_call x1, Pallas kernels, residuals(): pl.pallas_call(resid_kernel, grid=(rows // block,), in_specs=[pl.BlockSpe...  20.1 us
    all_to_all x1, blocking collectives, local(): lax.all_to_all(copies, 'row', 0, 0, axis_index_groups=same_core, tiled=True)  18 us
    pallas_call x1, Pallas kernels, list_sums(): pl.pallas_call(sums_kernel, grid=(rows // block,), in_specs=[pl.BlockSpec...  14.1 us
    ppermute x5, waiting for transfers between devices, swap(): return lax.ppermute(x, axis, [(i, i ^ bit) for i in range(n)])  11.7 us
    all_to_all x1, blocking collectives, local(): book = lax.all_to_all(copies, 'row', 0, 0, tiled=True).reshape(codes, width)  9.91 us
    all_to_all x1, blocking collectives, local(): lax.all_to_all(sums.reshape(n_row, owned_codes, width), 'row', 0, 0, tile...  9.7 us
    ppermute x5, starting transfers between devices, swap(): return lax.ppermute(x, axis, [(i, i ^ bit) for i in range(n)])  8.87 us
  transfers between devices with their start and end apart: 5, of which 5 were waited for; matrix products, arithmetic and copies ran while one was open for 0% of the time, Pallas kernels for 0%

profile of v1, /device:TPU:0, one launch (start us, length us, event | category | flops | bytes accessed | tf_op | source)
XLA Modules:
  0.0 127.1 jit_solution(3528542904367502409)
XLA Ops:
  0.6 0.0 copy-start.1
  0.7 0.9 copy-done.1
  1.6 0.0 copy-start.3
  1.6 0.8 copy-done.3
  2.4 14.1 %list_sums.1 = (f32[8,264,128]{2,1,0:T(8,128)S(1)}, f32[8,264,128]{2,1,0:T(8,128)S(1)}) custom-call(s32[1]{0:T(128)} %bitcast.core_ref, s32[8192]{0:T(1024)S(1)} %copy-done.3, s32[64,128]{1,0:T(8,128)S(1)} %bitcast.11, s32[8,8192]{1,0:T(8,128)S(1)} %bitcast.7, f32[8192,128]{1,0:T(8,128)} %x_ref.3), custom_call_target="tpu_custom_call" | custom-call | tf_op jit(solution)/shard_map/list_sums/pallas_call | solution.py:109
  16.4 0.1 collective-permute-start
  16.5 2.7 %collective-permute-done = f32[8,264,128]{2,1,0:T(8,128)S(1)} collective-permute-done((f32[8,264,128]{2,1,0:T(8,128)S(1)}, f32[8,264,128]{2,1,0:T(8,128)S(1)}, u32[]{:S(2)}, u32[]{:S(2)}) %collective-permute-start) | collective-permute-done | bytes 1081376 | tf_op jit(solution)/shard_map/ppermute | solution.py:312
  19.2 0.1 add.17
  19.4 0.0 copy-start.4
  19.4 21.9 %all_to_all.20.part_ref = f32[8,264,128]{2,1,0:T(8,128)S(1)} all-to-all(f32[8,264,128]{2,1,0:T(8,128)S(1)} %add.17), channel_id=1, replica_groups={{0,16,32,48,64,80,96,112},{8,24,40,56,72,88,104,120},{1,17,33,49,65,81,..., dimensions={0} | all-to-all | bytes 2162688 | tf_op jit(solution)/shard_map/all_to_all | solution.py:333
  41.2 0.0 copy-done.4
  41.2 0.8 centroids.1
  42.1 0.0 copy-start.5
  42.1 18.0 %all_to_all.21.own_ref = f32[8,256,128]{2,1,0:T(8,128)S(1)} all-to-all(f32[8,256,128]{2,1,0:T(8,128)S(1)} %get-tuple-element.15), channel_id=1, replica_groups={{0,16,32,48,64,80,96,112},{8,24,40,56,72,88,104,120},{1,17,33,49,65,81,..., dimensions={0} | all-to-all | bytes 2097152 | tf_op jit(solution)/shard_map/all_to_all | solution.py:335
  60.0 0.0 copy-start.2
  60.1 0.0 collective-permute-start.1
  60.1 0.0 copy-done.5
  60.1 2.7 %collective-permute-done.1.other_ref = f32[8,256,128]{2,1,0:T(8,128)S(1)} collective-permute-done((f32[8,256,128]{2,1,0:T(8,128)S(1)}, f32[8,256,128]{2,1,0:T(8,128)S(1)}, u32[]{:S(2)}, u32[]{:S(2)}) %collective-permute-start.1) | collective-permute-done | bytes 1048608 | tf_op jit(solution)/shard_map/ppermute | solution.py:312
  62.7 20.1 %residuals.1 = (f32[128,8192]{1,0:T(8,128)}, f32[256,128]{1,0:T(8,128)S(1)}) custom-call(s32[1]{0:T(128)} %bitcast.core_ref, s32[8192]{0:T(1024)S(1)} %copy-done.3, s32[8,8192]{1,0:T(8,128)S(1)} %bitcast.8, f32[8192,128]{1,0:T(8,128)} %x_ref.3, f32[8,256,128]{2,1,0:T(8,128)S(1)} %all_to_all.21.own_ref, f32[8,256,128]{2,1,0:T(8,128)S(1)} %collective-permute-done.1.other_ref), custom_call_target="tpu_custom_call" | custom-call | tf_op jit(solution)/shard_map/residuals/pallas_call | solution.py:211
  82.8 9.7 %all_to_all.22.part_ref = f32[16,16,128]{2,1,0:T(8,128)} all-to-all(f32[16,16,128]{2,1,0:T(8,128)S(1)} %bitcast.12), channel_id=1, replica_groups=mesh['row'=16,'col'=8] {'row'}, dimensions={0} | all-to-all | bytes 262144 | tf_op jit(solution)/shard_map/all_to_all | solution.py:338
  92.5 1.8 %codebook.1 = (f32[16,128]{1,0:T(8,128)}, f32[16,16,128]{2,1,0:T(8,128)}) custom-call(f32[16,16,128]{2,1,0:T(8,128)} %all_to_all.22.part_ref, f32[8,128]{1,0:T(8,128)} %copy-done.5, f32[16,128]{1,0:T(8,128)} %old_ref.3), custom_call_target="tpu_custom_call" | custom-call | tf_op jit(solution)/shard_map/codebook/pallas_call | solution.py:301
  94.2 9.9 %all_to_all.23 = f32[16,16,128]{2,1,0:T(8,128)S(1)} all-to-all(f32[16,16,128]{2,1,0:T(8,128)} %get-tuple-element.19), channel_id=1, replica_groups=mesh['row'=16,'col'=8] {'row'}, dimensions={0} | all-to-all | bytes 262144 | tf_op jit(solution)/shard_map/all_to_all | solution.py:340
  104.2 0.0 copy-done.2
  104.2 0.0 copy-start
  104.2 2.2 %copy-done = f32[128,8192]{1,0:T(8,128)S(1)} copy-done((f32[128,8192]{1,0:T(8,128)S(1)}, f32[128,8192]{1,0:T(8,128)}, u32[]{:S(2)}) %copy-start) | copy-done | bytes 4194328
  106.3 4.9 %errors.1 = f32[64,128]{1,0:T(8,128)S(1)} custom-call(f32[256,128]{1,0:T(8,128)S(1)} %bitcast.10, s32[8,8192]{1,0:T(8,128)S(1)} %bitcast.9, f32[128,8192]{1,0:T(8,128)S(1)} %copy-done), custom_call_target="tpu_custom_call" | custom-call | tf_op jit(solution)/shard_map/errors/pallas_call | solution.py:265
  111.2 3.0 %collective-permute-start.2 = (f32[64,128]{1,0:T(8,128)S(1)}, f32[64,128]{1,0:T(8,128)S(1)}, u32[]{:S(2)}, u32[]{:S(2)}) collective-permute-start(f32[64,128]{1,0:T(8,128)S(1)} %errors.1), channel_id=1, source_target_pairs={{0,1},{1,0},{2,3},{3,2},{4,5},{5,4},{6,7},{7,6},{8,9},{9,8},{10,11... | collective-permute-start | bytes 98312 | tf_op jit(solution)/shard_map/ppermute | solution.py:312
  114.2 2.5 %collective-permute-done.2 = f32[64,128]{1,0:T(8,128)S(1)} collective-permute-done((f32[64,128]{1,0:T(8,128)S(1)}, f32[64,128]{1,0:T(8,128)S(1)}, u32[]{:S(2)}, u32[]{:S(2)}) %collective-permute-start.2) | collective-permute-done | bytes 32800 | tf_op jit(solution)/shard_map/ppermute | solution.py:312
  116.7 1.9 %collective-permute-start.3 = (f32[64,128]{1,0:T(8,128)S(1)}, f32[64,128]{1,0:T(8,128)S(1)}, u32[]{:S(2)}, u32[]{:S(2)}) collective-permute-start(f32[64,128]{1,0:T(8,128)S(1)} %add.18), channel_id=1, source_target_pairs={{0,2},{1,3},{2,0},{3,1},{4,6},{5,7},{6,4},{7,5},{8,10},{9,11},{10,... | collective-permute-start | bytes 98312 | tf_op jit(solution)/shard_map/ppermute | solution.py:312
  118.7 2.0 %collective-permute-done.3 = f32[64,128]{1,0:T(8,128)S(1)} collective-permute-done((f32[64,128]{1,0:T(8,128)S(1)}, f32[64,128]{1,0:T(8,128)S(1)}, u32[]{:S(2)}, u32[]{:S(2)}) %collective-permute-start.3) | collective-permute-done | bytes 32800 | tf_op jit(solution)/shard_map/ppermute | solution.py:312
  120.7 3.9 %collective-permute-start.4 = (f32[64,128]{1,0:T(8,128)S(1)}, f32[64,128]{1,0:T(8,128)S(1)}, u32[]{:S(2)}, u32[]{:S(2)}) collective-permute-start(f32[64,128]{1,0:T(8,128)S(1)} %add.19), channel_id=1, source_target_pairs={{0,4},{1,5},{2,6},{3,7},{4,0},{5,1},{6,2},{7,3},{8,12},{9,13},{10,... | collective-permute-start | bytes 98312 | tf_op jit(solution)/shard_map/ppermute | solution.py:312
  124.6 1.9 %collective-permute-done.4 = f32[64,128]{1,0:T(8,128)S(1)} collective-permute-done((f32[64,128]{1,0:T(8,128)S(1)}, f32[64,128]{1,0:T(8,128)S(1)}, u32[]{:S(2)}, u32[]{:S(2)}) %collective-permute-start.4) | collective-permute-done | bytes 32800 | tf_op jit(solution)/shard_map/ppermute | solution.py:312
  126.4 0.6 multiply_bitcast_fusion
  (2 shorter events, 0.0 us)
Async XLA Ops:
  0.6 1.0 copy-start.1
  1.6 0.8 copy-start.3
  16.4 2.8 %collective-permute-start = (f32[8,264,128]{2,1,0:T(8,128)S(1)}, f32[8,264,128]{2,1,0:T(8,128)S(1)}, u32[]{:S(2)}, u32[]{:S(2)}) collective-permute-start(f32[8,264,128]{2,1,0:T(8,128)S(1)} %get-tuple-element.13), channel_id=1, source_target_pairs={{0,8},{8,0},{16,24},{24,16},{32,40},{40,32},{48,56},{56,48},{64,72... | collective-permute-start | bytes 3244040 | tf_op jit(solution)/shard_map/ppermute | solution.py:312
  19.4 21.9 %copy-start.4 = (f32[256,128]{1,0:T(8,128)S(1)}, f32[256,128]{1,0:T(8,128)}, u32[]{:S(2)}) copy-start(f32[256,128]{1,0:T(8,128)} %old_ref.2) | copy-start | bytes 393220
  42.1 18.0 %copy-start.5 = (f32[8,128]{1,0:T(8,128)}, f32[8,128]{1,0:T(8,128)S(1)}, u32[]{:S(2)}) copy-start(f32[8,128]{1,0:T(8,128)S(1)} %get-tuple-element.17.tail_ref) | copy-start | bytes 12292
  60.0 44.1 %copy-start.2 = (s32[8192,8]{0,1:T(8,128)S(1)}, s32[8192,8]{0,1:T(8,128)}, u32[]{:S(2)}) copy-start(s32[8192,8]{0,1:T(8,128)} %param.7) | copy-start | bytes 786436
  60.1 2.7 %collective-permute-start.1 = (f32[8,256,128]{2,1,0:T(8,128)S(1)}, f32[8,256,128]{2,1,0:T(8,128)S(1)}, u32[]{:S(2)}, u32[]{:S(2)}) collective-permute-start(f32[8,256,128]{2,1,0:T(8,128)S(1)} %all_to_all.21.own_ref), channel_id=1, source_target_pairs={{0,8},{8,0},{16,24},{24,16},{32,40},{40,32},{48,56},{56,48},{64,72... | collective-permute-start | bytes 3145736 | tf_op jit(solution)/shard_map/ppermute | solution.py:312
  104.2 2.2 %copy-start = (f32[128,8192]{1,0:T(8,128)S(1)}, f32[128,8192]{1,0:T(8,128)}, u32[]{:S(2)}) copy-start(f32[128,8192]{1,0:T(8,128)} %get-tuple-element.20.rest_ref) | copy-start | bytes 12582916
  111.2 5.5 %collective-permute-start.2 = (f32[64,128]{1,0:T(8,128)S(1)}, f32[64,128]{1,0:T(8,128)S(1)}, u32[]{:S(2)}, u32[]{:S(2)}) collective-permute-start(f32[64,128]{1,0:T(8,128)S(1)} %errors.1), channel_id=1, source_target_pairs={{0,1},{1,0},{2,3},{3,2},{4,5},{5,4},{6,7},{7,6},{8,9},{9,8},{10,11... | collective-permute-start | bytes 98312 | tf_op jit(solution)/shard_map/ppermute | solution.py:312
  116.7 3.9 %collective-permute-start.3 = (f32[64,128]{1,0:T(8,128)S(1)}, f32[64,128]{1,0:T(8,128)S(1)}, u32[]{:S(2)}, u32[]{:S(2)}) collective-permute-start(f32[64,128]{1,0:T(8,128)S(1)} %add.18), channel_id=1, source_target_pairs={{0,2},{1,3},{2,0},{3,1},{4,6},{5,7},{6,4},{7,5},{8,10},{9,11},{10,... | collective-permute-start | bytes 98312 | tf_op jit(solution)/shard_map/ppermute | solution.py:312
  120.7 5.8 %collective-permute-start.4 = (f32[64,128]{1,0:T(8,128)S(1)}, f32[64,128]{1,0:T(8,128)S(1)}, u32[]{:S(2)}, u32[]{:S(2)}) collective-permute-start(f32[64,128]{1,0:T(8,128)S(1)} %add.19), channel_id=1, source_target_pairs={{0,4},{1,5},{2,6},{3,7},{4,0},{5,1},{6,2},{7,3},{8,12},{9,13},{10,... | collective-permute-start | bytes 98312 | tf_op jit(solution)/shard_map/ppermute | solution.py:312

commit v2 on v1

v2 whole, which is shorter than its diff:
```python
import functools
import jax
import jax.numpy as jnp
from jax import lax
from jax.experimental import pallas as pl
from jax.experimental.pallas import tpu as pltpu

from jax.sharding import PartitionSpec as P

HIGH = lax.Precision.HIGHEST
D = 1024
LANES = 128
SUB_DIM = 16
NACC = 8
SLAB = 8
RBLOCK = 512
ETILE = 1024
VLIM = 20 * 2**20


def sums_kernel(core_ref, ids_hbm, idv_hbm, codes_hbm, x_hbm, keep_ref, send_ref, ids, idv, codes_ref, x_ref, lcnt, ccnt, sems, *accs):
    rows, _ = x_ref.shape
    lists = accs[0].shape[0]
    pieces = keep_ref.shape[0]
    owned = lists // (2 * pieces)
    subs = codes_ref.shape[0]
    nchunk = sems.shape[0] - 3
    chunk = rows // nchunk

    def part(c):
        here = pl.ds(c * chunk, chunk)
        return pltpu.make_async_copy(x_hbm.at[here, :], x_ref.at[here, :], sems.at[c])

    fetch_ids = pltpu.make_async_copy(ids_hbm, ids, sems.at[nchunk])
    fetch_idv = pltpu.make_async_copy(idv_hbm, idv, sems.at[nchunk + 1])
    fetch_codes = pltpu.make_async_copy(codes_hbm, codes_ref, sems.at[nchunk + 2])
    fetch_ids.start()
    part(0).start()
    fetch_idv.start()
    fetch_codes.start()
    for c in range(1, nchunk):
        part(c).start()

    zero = jnp.zeros((ZROWS, LANES), jnp.float32)

    @pl.loop(0, lists // ZROWS)
    def _(i):
        for acc in accs:
            acc[pl.ds(pl.multiple_of(i * ZROWS, ZROWS), ZROWS), :] = zero

    lcnt[...] = jnp.zeros_like(lcnt)
    ccnt[...] = jnp.zeros_like(ccnt)
    fetch_idv.wait()
    fetch_codes.wait()
    fetch_ids.wait()
    nhi = lists // LANES
    nt = (((1,), (1,)), ((), ()))

    def counts(start):
        hi_iota = lax.broadcasted_iota(jnp.int32, (nhi, LANES), 0)
        lo_iota = lax.broadcasted_iota(jnp.int32, (LANES, LANES), 0)
        his, los = [], []
        group = idv[pl.ds(pl.multiple_of(start // LANES, CBLOCK // LANES), CBLOCK // LANES), :]
        for t in range(CBLOCK // LANES):
            row = group[t : t + 1, :]
            his.append((lax.shift_right_logical(row, 7) == hi_iota).astype(jnp.bfloat16))
            los.append(((row & (LANES - 1)) == lo_iota).astype(jnp.bfloat16))
        lcnt[...] += lax.dot_general(
            jnp.concatenate(his, 1), jnp.concatenate(los, 1), nt, preferred_element_type=jnp.float32
        )
        dig = lax.broadcasted_iota(jnp.int32, (SUB_DIM, CBLOCK), 0)
        his, los = [], []
        for m in range(subs):
            row = codes_ref[pl.ds(m, 1), pl.ds(start, CBLOCK)]
            his.append((lax.shift_right_logical(row, 4) == dig).astype(jnp.bfloat16))
            los.append(((row & (SUB_DIM - 1)) == dig).astype(jnp.bfloat16))
        ccnt[...] += lax.dot_general(
            jnp.concatenate(his, 0), jnp.concatenate(los, 0), nt, preferred_element_type=jnp.float32
        )

    def scatter(start):
        for u in range(0, CBLOCK, NACC):
            row = [ids.at[pl.ds(u + j, rows - CBLOCK + 1)][start] for j in range(NACC)]
            old = [accs[j][pl.ds(row[j], 1), :] for j in range(NACC)]
            new = [x_ref[pl.ds(start + u + j, 1), :] for j in range(NACC)]
            for j in range(NACC):
                accs[j][pl.ds(row[j], 1), :] = old[j] + new[j]

    @pl.loop(0, nchunk)
    def _(c):
        part(c).wait()

        @pl.loop(0, chunk // CBLOCK)
        def _(i):
            start = pl.multiple_of(c * chunk + i * CBLOCK, CBLOCK)
            scatter(start)
            counts(start)

    cc = ccnt[...]
    r = lax.broadcasted_iota(jnp.int32, cc.shape, 0) // SUB_DIM
    c = lax.broadcasted_iota(jnp.int32, cc.shape, 1) // SUB_DIM
    cc = jnp.where(r == c, cc, 0.0)
    crow = cc[0:SUB_DIM, :]
    for m in range(1, subs):
        crow = crow + cc[m * SUB_DIM:(m + 1) * SUB_DIM, :]
    ccnt[0:SUB_DIM, :] = crow
    core = core_ref[0]
    for out, par in ((send_ref, 1 - core), (keep_ref, core)):
        @pl.loop(0, pieces)
        def _(k):
            owner = 2 * k + par
            start = pl.multiple_of(owner * owned, owned)
            total = accs[0][pl.ds(start, owned), :]
            for acc in accs[1:]:
                total = total + acc[pl.ds(start, owned), :]
            out[k, 0:owned, :] = total
            out[k, pl.ds(owned, SLAB), :] = jnp.concatenate(
                [
                    lcnt[pl.ds(owner * (owned // LANES), owned // LANES), :],
                    ccnt[pl.ds(owner, 1), :],
                    jnp.zeros((SLAB - owned // LANES - 1, LANES), jnp.float32),
                ],
                0,
            )


CBLOCK = 1024
ZROWS = 64
NCHUNK = 8


def list_sums(core, ids, codes_t, x, pieces, lists):
    rows, width = x.shape
    owned = lists // (2 * pieces)
    out = jax.ShapeDtypeStruct((pieces, owned + SLAB, width), jnp.float32)
    hbm = pl.BlockSpec(memory_space=pl.ANY)
    vmem = pl.BlockSpec(memory_space=pltpu.VMEM)
    return pl.pallas_call(
        sums_kernel,
        in_specs=[pl.BlockSpec(memory_space=pltpu.SMEM)] + [hbm] * 4,
        out_specs=[vmem, vmem],
        out_shape=[out, out],
        scratch_shapes=[
            pltpu.SMEM((rows,), jnp.int32),
            pltpu.VMEM((rows // LANES, LANES), jnp.int32),
            pltpu.VMEM(codes_t.shape, jnp.int32),
            pltpu.VMEM((rows, width), jnp.float32),
            pltpu.VMEM((lists // LANES, LANES), jnp.float32),
            pltpu.VMEM((LANES, LANES), jnp.float32),
            pltpu.SemaphoreType.DMA((NCHUNK + 3,)),
        ]
        + [pltpu.VMEM((lists, width), jnp.float32)] * NACC,
        compiler_params=pltpu.CompilerParams(vmem_limit_bytes=60 * 2**20),
        name="list_sums",
    )(core, ids, ids.reshape(rows // LANES, LANES), codes_t, x)


def centroid_kernel(prior, part_ref, old_ref, cent_ref, copies_ref, tail_ref):
    owned = old_ref.shape[0]
    total = part_ref[0]
    for k in range(1, part_ref.shape[0]):
        total = total + part_ref[k]
    eye = (
        lax.broadcasted_iota(jnp.int32, (LANES, LANES), 0)
        == lax.broadcasted_iota(jnp.int32, (LANES, LANES), 1)
    )
    for h in range(owned // LANES):
        row = total[owned + h : owned + h + 1, :]
        col = jnp.sum(jnp.where(eye, row, 0.0), axis=1, keepdims=True)
        sl = slice(h * LANES, (h + 1) * LANES)
        cent = (total[sl, :] + prior * old_ref[sl, :]) / (col + prior)
        cent_ref[sl, :] = cent
        for k in range(copies_ref.shape[0]):
            copies_ref[k, sl, :] = cent
    tail_ref[...] = total[owned:, :]


def new_centroids(parts, old, prior):
    n, _, width = parts.shape
    return pl.pallas_call(
        functools.partial(centroid_kernel, prior),
        out_shape=[
            jax.ShapeDtypeStruct(old.shape, jnp.float32),
            jax.ShapeDtypeStruct((n,) + old.shape, jnp.float32),
            jax.ShapeDtypeStruct((SLAB, width), jnp.float32),
        ],
        compiler_params=pltpu.CompilerParams(vmem_limit_bytes=32 * 2**20),
        name="centroids",
    )(parts, old)


NT = (((1,), (1,)), ((), ()))


def resid_kernel(
    core_ref, ids_ref, codes_ref, x_ref, own_ref, other_ref, rest_ref, sums_ref, ids, table, got0, got1, sumst, sem
):
    block = got0.shape[0]
    rows = x_ref.shape[0]
    pieces, owned, _ = own_ref.shape
    subs = codes_ref.shape[0]
    half = sums_ref.shape[0] // 2
    fetch = pltpu.make_async_copy(ids_ref, ids, sem)
    fetch.start()
    core = core_ref[0]
    for k in range(pieces):
        table[pl.ds(pl.multiple_of((2 * k + core) * owned, owned), owned), :] = own_ref[k]
        table[pl.ds(pl.multiple_of((2 * k + 1 - core) * owned, owned), owned), :] = other_ref[k]
    sumst[...] = jnp.zeros_like(sumst)
    fetch.wait()

    def gather(start, got):
        for j in range(block):
            row = ids.at[pl.ds(j, rows - block + 1)][start]
            got[pl.ds(j, 1), :] = table[pl.ds(row, 1), :]

    def work(start, got):
        here = pl.ds(start, block)
        rest = (x_ref[here, :] - got[...]).T
        rest_ref[:, here] = rest
        hi = rest.astype(jnp.bfloat16)
        lo = (rest - hi.astype(jnp.float32)).astype(jnp.bfloat16)
        label = lax.broadcasted_iota(jnp.int32, (half, block), 0)
        for p in range(subs // 2):
            left, right = [], []
            for m in (2 * p, 2 * p + 1):
                code = codes_ref[pl.ds(m, 1), here]
                right.append(((code & (half - 1)) == label).astype(jnp.bfloat16))
                f = slice(m * SUB_DIM, (m + 1) * SUB_DIM)
                both = jnp.concatenate([hi[f], lo[f]], 0)
                top = jnp.broadcast_to((code < half).astype(jnp.bfloat16), both.shape)
                first = both * top
                left += [first, both - first]
            part = lax.dot_general(
                jnp.concatenate(left, 0), jnp.concatenate(right, 0), NT, preferred_element_type=jnp.float32
            )
            for s in range(2):
                f = slice((2 * p + s) * SUB_DIM, (2 * p + s + 1) * SUB_DIM)
                for h in range(2):
                    band = part[(4 * s + 2 * h) * SUB_DIM : (4 * s + 2 * h + 2) * SUB_DIM, s * half : (s + 1) * half]
                    sumst[f, h * half : (h + 1) * half] += band[:SUB_DIM] + band[SUB_DIM:]

    gather(0, got0)

    @pl.loop(0, rows // (2 * block))
    def _(i):
        first = pl.multiple_of(2 * i * block, block)
        second = pl.multiple_of(first + block, block)
        third = pl.multiple_of(jnp.minimum(second + block, rows - block), block)
        gather(second, got1)
        work(first, got0)
        gather(third, got0)
        work(second, got1)

    sums_ref[...] = sumst[...].T


def residuals(core, ids, codes_t, x, own, other, codes, block=RBLOCK):
    rows, width = x.shape
    pieces, owned, _ = own.shape
    vmem = pl.BlockSpec(memory_space=pltpu.VMEM)
    return pl.pallas_call(
        resid_kernel,
        in_specs=[pl.BlockSpec(memory_space=pltpu.SMEM)] + [vmem] * 5,
        out_specs=[vmem, vmem],
        out_shape=[
            jax.ShapeDtypeStruct((width, rows), jnp.float32),
            jax.ShapeDtypeStruct((codes, width), jnp.float32),
        ],
        scratch_shapes=[
            pltpu.SMEM((rows,), jnp.int32),
            pltpu.VMEM((2 * pieces * owned, width), jnp.float32),
            pltpu.VMEM((block, width), jnp.float32),
            pltpu.VMEM((block, width), jnp.float32),
            pltpu.VMEM((width, codes), jnp.float32),
            pltpu.SemaphoreType.DMA(()),
        ],
        compiler_params=pltpu.CompilerParams(vmem_limit_bytes=VLIM),
        name="residuals",
    )(core, ids, codes_t, x, own, other)


def errors_kernel(book_ref, codes_ref, rest_ref, out_ref, table):
    subs, rows = codes_ref.shape
    half = book_ref.shape[0] // 2
    table[...] = book_ref[...].T

    @pl.loop(0, rows // ETILE)
    def _(i):
        sums = []
        for t in range(ETILE // LANES):
            cols = pl.ds(pl.multiple_of(i * ETILE, ETILE) + t * LANES, LANES)
            acc = jnp.zeros((8, LANES), jnp.float32)
            for m in range(subs):
                idx = jnp.broadcast_to(codes_ref[pl.ds(m, 1), cols], (8, LANES))
                low = idx & (half - 1)
                first = idx < half
                for g in range(SUB_DIM // 8):
                    f = slice(m * SUB_DIM + g * 8, m * SUB_DIM + g * 8 + 8)
                    a = jnp.take_along_axis(table[f, 0:half], low, axis=1)
                    b = jnp.take_along_axis(table[f, half:2 * half], low, axis=1)
                    d = rest_ref[f, cols] - jnp.where(first, a, b)
                    acc = acc + d * d
            sums.append(jnp.sum(acc, axis=0, keepdims=True))
        out_ref[pl.ds(pl.multiple_of(i * (ETILE // LANES), ETILE // LANES), ETILE // LANES), :] = jnp.concatenate(sums, 0)


def errors(book, codes_t, rest):
    width, rows = rest.shape
    vmem = pl.BlockSpec(memory_space=pltpu.VMEM)
    return pl.pallas_call(
        errors_kernel,
        in_specs=[vmem] * 3,
        out_specs=vmem,
        out_shape=jax.ShapeDtypeStruct((rows // LANES, LANES), jnp.float32),
        scratch_shapes=[pltpu.VMEM((width, book.shape[0]), jnp.float32)],
        compiler_params=pltpu.CompilerParams(vmem_limit_bytes=VLIM),
        name="errors",
    )(book, codes_t, rest)


def book_kernel(prior, part_ref, tail_ref, old_ref, book_ref, copies_ref):
    total = part_ref[0]
    for k in range(1, part_ref.shape[0]):
        total = total + part_ref[k]
    shape = total.shape
    row = jnp.broadcast_to(tail_ref[2:3, :], shape)
    lane = lax.broadcasted_iota(jnp.int32, shape, 1)
    code = lax.broadcasted_iota(jnp.int32, shape, 0)
    picked = jnp.where(lane % SUB_DIM == code, row, 0.0)
    r = lax.broadcasted_iota(jnp.int32, (LANES, LANES), 0) // SUB_DIM
    c = lax.broadcasted_iota(jnp.int32, (LANES, LANES), 1) // SUB_DIM
    ones = (r == c).astype(jnp.float32)
    counts = jnp.dot(picked, ones, precision=HIGH, preferred_element_type=jnp.float32)
    book = (total + prior * old_ref[...]) / (counts + prior)
    book_ref[...] = book
    for k in range(copies_ref.shape[0]):
        copies_ref[k] = book


def new_codebook(parts, tail, old, prior):
    return pl.pallas_call(
        functools.partial(book_kernel, prior),
        out_shape=[
            jax.ShapeDtypeStruct(old.shape, jnp.float32),
            jax.ShapeDtypeStruct(parts.shape, jnp.float32),
        ],
        name="codebook",
    )(parts, tail, old)


def swap(x, axis, n, bit):
    return lax.ppermute(x, axis, [(i, i ^ bit) for i in range(n)])


def local(passages, list_ids, code_ids, old_centroids, old_codebook):
    rows, width = passages.shape
    n_row = lax.axis_size("row")
    n_col = lax.axis_size("col")
    total = rows * n_row
    owned_lists = old_centroids.shape[0]
    owned_codes = old_codebook.shape[0]
    lists = owned_lists * n_row
    codes = owned_codes * n_row
    list_prior = float(total // lists)
    code_prior = float(total // codes)
    pieces = n_row // 2
    same_core = [[2 * k + c for k in range(pieces)] for c in range(2)]
    core = (lax.axis_index("row") % 2).astype(jnp.int32).reshape(1)
    codes_t = code_ids.T

    keep, send = list_sums(core, list_ids, codes_t, passages, pieces, lists)
    pair = keep + swap(send, "row", n_row, 1)
    parts = lax.all_to_all(pair, "row", 0, 0, axis_index_groups=same_core, tiled=True)
    centroids, copies, tail = new_centroids(parts, old_centroids, list_prior)
    own = lax.all_to_all(copies, "row", 0, 0, axis_index_groups=same_core, tiled=True)
    other = swap(own, "row", n_row, 1)
    rest, sums = residuals(core, list_ids, codes_t, passages, own, other, codes)
    parts = lax.all_to_all(sums.reshape(n_row, owned_codes, width), "row", 0, 0, tiled=True)
    codebook, copies = new_codebook(parts, tail, old_codebook, code_prior)
    book = lax.all_to_all(copies, "row", 0, 0, tiled=True).reshape(codes, width)
    err = errors(book, codes_t, rest)
    bit = 1
    while bit < n_col:
        err = err + swap(err, "col", n_col, bit)
        bit *= 2
    return centroids, codebook, err.reshape(rows) / D


def solution(mesh):
    in_specs = (P("row", "col"), P("row"), P("row", "col"), P("row", "col"), P("row", "col"))
    out_specs = (P("row", "col"), P("row", "col"), P("row"))
    return jax.shard_map(local, mesh=mesh, in_specs=in_specs, out_specs=out_specs, check_vma=False)
```

time: 128 us -> 117 us (0.914)
  Pallas kernels: 41.6 us -> 29 us
    pallas_call x3, Pallas kernels: 39 us -> 26.4 us  [the longest x1 11.4 us: list_sums(): pl.pallas_call(sums_kernel, in_specs=[pl.BlockSpec(memory_space=pltpu.SME...]
    unnamed x12 -> x14, local copies, waits for them, and re-layouts: 3.9 us -> 4.16 us
where the time goes in v2:
time: 117 us; the launch traced here: 116 us
  blocking collectives  59.7 us (51%)
  Pallas kernels  29 us (25%)
  waiting for transfers between devices  12 us (10%)
  starting transfers between devices  8.86 us (8%)
  local copies, waits for them, and re-layouts  4.16 us (4%)
  other arithmetic  2.02 us (2%)
    all_to_all x1, blocking collectives, local(): lax.all_to_all(pair, 'row', 0, 0, axis_index_groups=same_core, tiled=True)  22 us
    all_to_all x1, blocking collectives, local(): lax.all_to_all(copies, 'row', 0, 0, axis_index_groups=same_core, tiled=True)  18.1 us
    ppermute x5, waiting for transfers between devices, swap(): return lax.ppermute(x, axis, [(i, i ^ bit) for i in range(n)])  12 us
    pallas_call x1, Pallas kernels, list_sums(): pl.pallas_call(sums_kernel, in_specs=[pl.BlockSpec(memory_space=pltpu.SME...  11.4 us
    pallas_call x1, Pallas kernels, residuals(): pl.pallas_call(resid_kernel, in_specs=[pl.BlockSpec(memory_space=pltpu.SM...  10.5 us
    all_to_all x1, blocking collectives, local(): book = lax.all_to_all(copies, 'row', 0, 0, tiled=True).reshape(codes, width)  9.91 us
    all_to_all x1, blocking collectives, local(): lax.all_to_all(sums.reshape(n_row, owned_codes, width), 'row', 0, 0, tile...  9.69 us
    ppermute x5, starting transfers between devices, swap(): return lax.ppermute(x, axis, [(i, i ^ bit) for i in range(n)])  8.86 us
  transfers between devices with their start and end apart: 5, of which 5 were waited for; matrix products, arithmetic and copies ran while one was open for 0% of the time, Pallas kernels for 0%

profile of v2, /device:TPU:0, one launch (start us, length us, event | category | flops | bytes accessed | tf_op | source)
XLA Modules:
  0.0 116.4 jit_solution(7250854883463574054)
XLA Ops:
  0.6 11.4 %list_sums.1 = (f32[8,264,128]{2,1,0:T(8,128)}, f32[8,264,128]{2,1,0:T(8,128)}) custom-call(s32[1]{0:T(128)} %bitcast.core_ref, s32[8192]{0:T(1024)} %ids_ref.1, s32[64,128]{1,0:T(8,128)} %bitcast.11, s32[8,8192]{1,0:T(8,128)} %bitcast.7, f32[8192,128]{1,0:T(8,128)} %x_ref.1), custom_call_target="tpu_custom_call" | custom-call | tf_op jit(solution)/shard_map/list_sums/pallas_call | solution.py:138
  12.0 0.1 collective-permute-start
  12.1 2.9 %collective-permute-done = f32[8,264,128]{2,1,0:T(8,128)S(1)} collective-permute-done((f32[8,264,128]{2,1,0:T(8,128)}, f32[8,264,128]{2,1,0:T(8,128)S(1)}, u32[]{:S(2)}, u32[]{:S(2)}) %collective-permute-start) | collective-permute-done | bytes 1081376 | tf_op jit(solution)/shard_map/ppermute | solution.py:353
  15.0 0.0 copy-start.5
  15.0 1.4 %add.17 = f32[8,264,128]{2,1,0:T(8,128)S(1)} add(f32[8,264,128]{2,1,0:T(8,128)} %get-tuple-element.12, f32[8,264,128]{2,1,0:T(8,128)S(1)} %collective-permute-done) | non-fusion elementwise | flops 270336 | bytes 3244032 | tf_op jit(solution)/shard_map/add | solution.py:373
  16.4 0.0 copy-start
  16.4 22.0 %all_to_all.20.part_ref = f32[8,264,128]{2,1,0:T(8,128)S(1)} all-to-all(f32[8,264,128]{2,1,0:T(8,128)S(1)} %add.17), channel_id=1, replica_groups={{0,16,32,48,64,80,96,112},{8,24,40,56,72,88,104,120},{1,17,33,49,65,81,..., dimensions={0} | all-to-all | bytes 2162688 | tf_op jit(solution)/shard_map/all_to_all | solution.py:374
  38.4 0.0 copy-done.5
  38.4 0.8 centroids.1
  39.3 0.0 copy-start.6
  39.3 0.0 copy-start.3
  39.3 0.0 copy-start.4
  39.3 18.1 %all_to_all.21.own_ref = f32[8,256,128]{2,1,0:T(8,128)S(1)} all-to-all(f32[8,256,128]{2,1,0:T(8,128)S(1)} %get-tuple-element.15), channel_id=1, replica_groups={{0,16,32,48,64,80,96,112},{8,24,40,56,72,88,104,120},{1,17,33,49,65,81,..., dimensions={0} | all-to-all | bytes 2097152 | tf_op jit(solution)/shard_map/all_to_all | solution.py:376
  57.4 0.0 collective-permute-start.1
  57.4 2.7 %collective-permute-done.1.other_ref = f32[8,256,128]{2,1,0:T(8,128)S(1)} collective-permute-done((f32[8,256,128]{2,1,0:T(8,128)S(1)}, f32[8,256,128]{2,1,0:T(8,128)S(1)}, u32[]{:S(2)}, u32[]{:S(2)}) %collective-permute-start.1) | collective-permute-done | bytes 1048608 | tf_op jit(solution)/shard_map/ppermute | solution.py:353
  60.0 0.0 copy-done
  60.0 0.0 copy-done.3
  60.0 0.0 copy-done.4
  60.0 10.5 %residuals.1 = (f32[128,8192]{1,0:T(8,128)S(1)}, f32[256,128]{1,0:T(8,128)S(1)}) custom-call(s32[1]{0:T(128)} %bitcast.core_ref, s32[8192]{0:T(1024)S(1)} %copy-done.4, s32[8,8192]{1,0:T(8,128)S(1)} %bitcast.8, f32[8192,128]{1,0:T(8,128)S(1)} %copy-done, f32[8,256,128]{2,1,0:T(8,128)S(1)} %all_to_all.21.own_ref, ...), custom_call_target="tpu_custom_call" | custom-call | tf_op jit(solution)/shard_map/residuals/pallas_call | solution.py:262
  70.5 0.0 copy-done.6
  70.5 0.0 copy-start.1
  70.6 1.9 %copy-done.1 = f32[128,8192]{1,0:T(8,128)} copy-done((f32[128,8192]{1,0:T(8,128)}, f32[128,8192]{1,0:T(8,128)S(1)}, u32[]{:S(2)}) %copy-start.1) | copy-done | bytes 4194328
  72.5 9.7 %all_to_all.22.part_ref = f32[16,16,128]{2,1,0:T(8,128)} all-to-all(f32[16,16,128]{2,1,0:T(8,128)S(1)} %bitcast.12), channel_id=1, replica_groups=mesh['row'=16,'col'=8] {'row'}, dimensions={0} | all-to-all | bytes 262144 | tf_op jit(solution)/shard_map/all_to_all | solution.py:379
  82.2 1.8 %codebook.1 = (f32[16,128]{1,0:T(8,128)}, f32[16,16,128]{2,1,0:T(8,128)}) custom-call(f32[16,16,128]{2,1,0:T(8,128)} %all_to_all.22.part_ref, f32[8,128]{1,0:T(8,128)} %copy-done.6, f32[16,128]{1,0:T(8,128)} %old_ref.3), custom_call_target="tpu_custom_call" | custom-call | tf_op jit(solution)/shard_map/codebook/pallas_call | solution.py:342
  84.0 9.9 %all_to_all.23 = f32[16,16,128]{2,1,0:T(8,128)S(1)} all-to-all(f32[16,16,128]{2,1,0:T(8,128)} %get-tuple-element.19), channel_id=1, replica_groups=mesh['row'=16,'col'=8] {'row'}, dimensions={0} | all-to-all | bytes 262144 | tf_op jit(solution)/shard_map/all_to_all | solution.py:381
  93.9 0.0 copy-start.2
  93.9 2.2 %copy-done.2 = f32[128,8192]{1,0:T(8,128)S(1)} copy-done((f32[128,8192]{1,0:T(8,128)S(1)}, f32[128,8192]{1,0:T(8,128)}, u32[]{:S(2)}) %copy-start.2) | copy-done | bytes 4194328
  96.1 4.5 %errors.1 = f32[64,128]{1,0:T(8,128)S(1)} custom-call(f32[256,128]{1,0:T(8,128)S(1)} %bitcast.10, s32[8,8192]{1,0:T(8,128)S(1)} %bitcast.9, f32[128,8192]{1,0:T(8,128)S(1)} %copy-done.2), custom_call_target="tpu_custom_call" | custom-call | tf_op jit(solution)/shard_map/errors/pallas_call | solution.py:311
  100.6 3.0 %collective-permute-start.2 = (f32[64,128]{1,0:T(8,128)S(1)}, f32[64,128]{1,0:T(8,128)S(1)}, u32[]{:S(2)}, u32[]{:S(2)}) collective-permute-start(f32[64,128]{1,0:T(8,128)S(1)} %errors.1), channel_id=1, source_target_pairs={{0,1},{1,0},{2,3},{3,2},{4,5},{5,4},{6,7},{7,6},{8,9},{9,8},{10,11... | collective-permute-start | bytes 98312 | tf_op jit(solution)/shard_map/ppermute | solution.py:353
  103.6 2.5 %collective-permute-done.2 = f32[64,128]{1,0:T(8,128)S(1)} collective-permute-done((f32[64,128]{1,0:T(8,128)S(1)}, f32[64,128]{1,0:T(8,128)S(1)}, u32[]{:S(2)}, u32[]{:S(2)}) %collective-permute-start.2) | collective-permute-done | bytes 32800 | tf_op jit(solution)/shard_map/ppermute | solution.py:353
  106.1 1.9 %collective-permute-start.3 = (f32[64,128]{1,0:T(8,128)S(1)}, f32[64,128]{1,0:T(8,128)S(1)}, u32[]{:S(2)}, u32[]{:S(2)}) collective-permute-start(f32[64,128]{1,0:T(8,128)S(1)} %add.18), channel_id=1, source_target_pairs={{0,2},{1,3},{2,0},{3,1},{4,6},{5,7},{6,4},{7,5},{8,10},{9,11},{10,... | collective-permute-start | bytes 98312 | tf_op jit(solution)/shard_map/ppermute | solution.py:353
  108.0 2.0 %collective-permute-done.3 = f32[64,128]{1,0:T(8,128)S(1)} collective-permute-done((f32[64,128]{1,0:T(8,128)S(1)}, f32[64,128]{1,0:T(8,128)S(1)}, u32[]{:S(2)}, u32[]{:S(2)}) %collective-permute-start.3) | collective-permute-done | bytes 32800 | tf_op jit(solution)/shard_map/ppermute | solution.py:353
  110.0 3.9 %collective-permute-start.4 = (f32[64,128]{1,0:T(8,128)S(1)}, f32[64,128]{1,0:T(8,128)S(1)}, u32[]{:S(2)}, u32[]{:S(2)}) collective-permute-start(f32[64,128]{1,0:T(8,128)S(1)} %add.19), channel_id=1, source_target_pairs={{0,4},{1,5},{2,6},{3,7},{4,0},{5,1},{6,2},{7,3},{8,12},{9,13},{10,... | collective-permute-start | bytes 98312 | tf_op jit(solution)/shard_map/ppermute | solution.py:353
  113.9 1.9 %collective-permute-done.4 = f32[64,128]{1,0:T(8,128)S(1)} collective-permute-done((f32[64,128]{1,0:T(8,128)S(1)}, f32[64,128]{1,0:T(8,128)S(1)}, u32[]{:S(2)}, u32[]{:S(2)}) %collective-permute-start.4) | collective-permute-done | bytes 32800 | tf_op jit(solution)/shard_map/ppermute | solution.py:353
  115.8 0.6 multiply_bitcast_fusion
  (2 shorter events, 0.0 us)
Async XLA Ops:
  12.0 3.0 %collective-permute-start = (f32[8,264,128]{2,1,0:T(8,128)}, f32[8,264,128]{2,1,0:T(8,128)S(1)}, u32[]{:S(2)}, u32[]{:S(2)}) collective-permute-start(f32[8,264,128]{2,1,0:T(8,128)} %get-tuple-element.13), channel_id=1, source_target_pairs={{0,8},{8,0},{16,24},{24,16},{32,40},{40,32},{48,56},{56,48},{64,72... | collective-permute-start | bytes 3244040 | tf_op jit(solution)/shard_map/ppermute | solution.py:353
  15.0 23.4 %copy-start.5 = (f32[256,128]{1,0:T(8,128)S(1)}, f32[256,128]{1,0:T(8,128)}, u32[]{:S(2)}) copy-start(f32[256,128]{1,0:T(8,128)} %old_ref.2) | copy-start | bytes 393220
  16.4 43.6 %copy-start = (f32[8192,128]{1,0:T(8,128)S(1)}, f32[8192,128]{1,0:T(8,128)}, u32[]{:S(2)}) copy-start(f32[8192,128]{1,0:T(8,128)} %x_ref.1) | copy-start | bytes 12582916
  39.3 31.3 %copy-start.6 = (f32[8,128]{1,0:T(8,128)}, f32[8,128]{1,0:T(8,128)S(1)}, u32[]{:S(2)}) copy-start(f32[8,128]{1,0:T(8,128)S(1)} %get-tuple-element.17.tail_ref) | copy-start | bytes 12292
  39.3 20.8 %copy-start.3 = (s32[8192,8]{0,1:T(8,128)S(1)}, s32[8192,8]{0,1:T(8,128)}, u32[]{:S(2)}) copy-start(s32[8192,8]{0,1:T(8,128)} %param.7) | copy-start | bytes 786436
  39.3 20.8 %copy-start.4 = (s32[8192]{0:T(1024)S(1)}, s32[8192]{0:T(1024)}, u32[]{:S(2)}) copy-start(s32[8192]{0:T(1024)} %ids_ref.1) | copy-start | bytes 98308
  57.4 2.7 %collective-permute-start.1 = (f32[8,256,128]{2,1,0:T(8,128)S(1)}, f32[8,256,128]{2,1,0:T(8,128)S(1)}, u32[]{:S(2)}, u32[]{:S(2)}) collective-permute-start(f32[8,256,128]{2,1,0:T(8,128)S(1)} %all_to_all.21.own_ref), channel_id=1, source_target_pairs={{0,8},{8,0},{16,24},{24,16},{32,40},{40,32},{48,56},{56,48},{64,72... | collective-permute-start | bytes 3145736 | tf_op jit(solution)/shard_map/ppermute | solution.py:353
  70.5 2.0 %copy-start.1 = (f32[128,8192]{1,0:T(8,128)}, f32[128,8192]{1,0:T(8,128)S(1)}, u32[]{:S(2)}) copy-start(f32[128,8192]{1,0:T(8,128)S(1)} %get-tuple-element.20.rest_ref) | copy-start | bytes 12582916
  93.9 2.2 %copy-start.2 = (f32[128,8192]{1,0:T(8,128)S(1)}, f32[128,8192]{1,0:T(8,128)}, u32[]{:S(2)}) copy-start(f32[128,8192]{1,0:T(8,128)} %copy-done.1) | copy-start | bytes 12582916
  100.6 5.5 %collective-permute-start.2 = (f32[64,128]{1,0:T(8,128)S(1)}, f32[64,128]{1,0:T(8,128)S(1)}, u32[]{:S(2)}, u32[]{:S(2)}) collective-permute-start(f32[64,128]{1,0:T(8,128)S(1)} %errors.1), channel_id=1, source_target_pairs={{0,1},{1,0},{2,3},{3,2},{4,5},{5,4},{6,7},{7,6},{8,9},{9,8},{10,11... | collective-permute-start | bytes 98312 | tf_op jit(solution)/shard_map/ppermute | solution.py:353
  106.1 3.9 %collective-permute-start.3 = (f32[64,128]{1,0:T(8,128)S(1)}, f32[64,128]{1,0:T(8,128)S(1)}, u32[]{:S(2)}, u32[]{:S(2)}) collective-permute-start(f32[64,128]{1,0:T(8,128)S(1)} %add.18), channel_id=1, source_target_pairs={{0,2},{1,3},{2,0},{3,1},{4,6},{5,7},{6,4},{7,5},{8,10},{9,11},{10,... | collective-permute-start | bytes 98312 | tf_op jit(solution)/shard_map/ppermute | solution.py:353
  110.0 5.8 %collective-permute-start.4 = (f32[64,128]{1,0:T(8,128)S(1)}, f32[64,128]{1,0:T(8,128)S(1)}, u32[]{:S(2)}, u32[]{:S(2)}) collective-permute-start(f32[64,128]{1,0:T(8,128)S(1)} %add.19), channel_id=1, source_target_pairs={{0,4},{1,5},{2,6},{3,7},{4,0},{5,1},{6,2},{7,3},{8,12},{9,13},{10,... | collective-permute-start | bytes 98312 | tf_op jit(solution)/shard_map/ppermute | solution.py:353

commit v3 on v2

v3 whole, which is shorter than its diff:
```python
import functools
import jax
import jax.numpy as jnp
from jax import lax
from jax.experimental import pallas as pl
from jax.experimental.pallas import tpu as pltpu

from jax.sharding import PartitionSpec as P

HIGH = lax.Precision.HIGHEST
D = 1024
LANES = 128
SUB_DIM = 16
NACC = 8
SLAB = 8
K1LIM = 50 * 2**20
SPARE = 5
RBLOCK = 512
EBLOCK = 2048
VLIM = 40 * 2**20


def sums_kernel(core_ref, ids_hbm, idv_hbm, x_hbm, keep_ref, send_ref, ids, idv, x_ref, lcnt, sems, *accs):
    rows, _ = x_ref.shape
    lists = accs[0].shape[0]
    pieces = keep_ref.shape[0]
    owned = lists // (2 * pieces)
    nchunk = sems.shape[0] - 2
    chunk = rows // nchunk

    def part(c):
        here = pl.ds(c * chunk, chunk)
        return pltpu.make_async_copy(x_hbm.at[here, :], x_ref.at[here, :], sems.at[c])

    fetch_ids = pltpu.make_async_copy(ids_hbm, ids, sems.at[nchunk])
    fetch_idv = pltpu.make_async_copy(idv_hbm, idv, sems.at[nchunk + 1])
    fetch_ids.start()
    part(0).start()
    fetch_idv.start()
    for c in range(1, nchunk):
        part(c).start()

    zero = jnp.zeros((ZROWS, LANES), jnp.float32)

    @pl.loop(0, lists // ZROWS)
    def _(i):
        for acc in accs:
            acc[pl.ds(pl.multiple_of(i * ZROWS, ZROWS), ZROWS), :] = zero

    lcnt[...] = jnp.zeros_like(lcnt)
    fetch_idv.wait()
    fetch_ids.wait()
    nhi = lists // LANES
    nt = (((1,), (1,)), ((), ()))

    def counts(start):
        hi_iota = lax.broadcasted_iota(jnp.int32, (nhi, LANES), 0)
        lo_iota = lax.broadcasted_iota(jnp.int32, (LANES, LANES), 0)
        his, los = [], []
        group = idv[pl.ds(pl.multiple_of(start // LANES, CBLOCK // LANES), CBLOCK // LANES), :]
        for t in range(CBLOCK // LANES):
            row = group[t : t + 1, :]
            his.append((lax.shift_right_logical(row, 7) == hi_iota).astype(jnp.bfloat16))
            los.append(((row & (LANES - 1)) == lo_iota).astype(jnp.bfloat16))
        lcnt[...] += lax.dot_general(
            jnp.concatenate(his, 1), jnp.concatenate(los, 1), nt, preferred_element_type=jnp.float32
        )

    def scatter(start):
        for u in range(0, CBLOCK, NACC):
            row = [ids.at[pl.ds(u + j, rows - CBLOCK + 1)][start] for j in range(NACC)]
            old = [accs[j][pl.ds(row[j], 1), :] for j in range(NACC)]
            new = [x_ref[pl.ds(start + u + j, 1), :] for j in range(NACC)]
            for j in range(NACC):
                accs[j][pl.ds(row[j], 1), :] = old[j] + new[j]

    @pl.loop(0, nchunk)
    def _(c):
        part(c).wait()

        @pl.loop(0, chunk // CBLOCK)
        def _(i):
            start = pl.multiple_of(c * chunk + i * CBLOCK, CBLOCK)
            scatter(start)
            counts(start)

    core = core_ref[0]
    for out, par in ((send_ref, 1 - core), (keep_ref, core)):
        @pl.loop(0, pieces)
        def _(k):
            owner = 2 * k + par
            start = pl.multiple_of(owner * owned, owned)
            total = accs[0][pl.ds(start, owned), :]
            for acc in accs[1:]:
                total = total + acc[pl.ds(start, owned), :]
            out[k, 0:owned, :] = total
            out[k, pl.ds(owned, SLAB), :] = jnp.concatenate(
                [
                    lcnt[pl.ds(owner * (owned // LANES), owned // LANES), :],
                    jnp.zeros((SLAB - owned // LANES, LANES), jnp.float32),
                ],
                0,
            )


CBLOCK = 1024
ZROWS = 64
NCHUNK = 8


def list_sums(core, ids, x, pieces, lists):
    rows, width = x.shape
    owned = lists // (2 * pieces)
    out = jax.ShapeDtypeStruct((pieces, owned + SLAB, width), jnp.float32)
    hbm = pl.BlockSpec(memory_space=pltpu.HBM)
    vmem = pl.BlockSpec(memory_space=pltpu.VMEM)
    return pl.pallas_call(
        sums_kernel,
        in_specs=[pl.BlockSpec(memory_space=pltpu.SMEM)] + [hbm] * 3,
        out_specs=[vmem, vmem],
        out_shape=[out, out],
        scratch_shapes=[
            pltpu.SMEM((rows,), jnp.int32),
            pltpu.VMEM((rows // LANES, LANES), jnp.int32),
            pltpu.VMEM((rows, width), jnp.float32),
            pltpu.VMEM((lists // LANES, LANES), jnp.float32),
            pltpu.SemaphoreType.DMA((NCHUNK + 2,)),
        ]
        + [pltpu.VMEM((lists, width), jnp.float32)] * NACC,
        compiler_params=pltpu.CompilerParams(vmem_limit_bytes=K1LIM),
        name="list_sums",
    )(core, ids, ids.reshape(rows // LANES, LANES), x)


def centroid_kernel(prior, part_ref, old_ref, cent_ref, copies_ref):
    owned = old_ref.shape[0]
    total = part_ref[0]
    for k in range(1, part_ref.shape[0]):
        total = total + part_ref[k]
    eye = (
        lax.broadcasted_iota(jnp.int32, (LANES, LANES), 0)
        == lax.broadcasted_iota(jnp.int32, (LANES, LANES), 1)
    )
    for h in range(owned // LANES):
        row = total[owned + h : owned + h + 1, :]
        col = jnp.sum(jnp.where(eye, row, 0.0), axis=1, keepdims=True)
        sl = slice(h * LANES, (h + 1) * LANES)
        cent = (total[sl, :] + prior * old_ref[sl, :]) / (col + prior)
        cent_ref[sl, :] = cent
        for k in range(copies_ref.shape[0]):
            copies_ref[k, sl, :] = cent


def new_centroids(parts, old, prior):
    n = parts.shape[0]
    return pl.pallas_call(
        functools.partial(centroid_kernel, prior),
        out_shape=[
            jax.ShapeDtypeStruct(old.shape, jnp.float32),
            jax.ShapeDtypeStruct((n,) + old.shape, jnp.float32),
        ],
        compiler_params=pltpu.CompilerParams(vmem_limit_bytes=16 * 2**20),
        name="centroids",
    )(parts, old)


NT = (((1,), (1,)), ((), ()))


def resid_kernel(
    core_ref, ids_ref, codes_ref, x_ref, own_ref, other_ref, rest_hbm, sums_ref, ids, table, got0, got1, sumst, ccnt, rest_ref, sem, out_sems
):
    block = got0.shape[0]
    rows = x_ref.shape[0]
    pieces, owned, _ = own_ref.shape
    subs = codes_ref.shape[0]
    owners, slab, _ = sums_ref.shape
    each = slab - SLAB
    half = owners * each // 2
    fetch = pltpu.make_async_copy(ids_ref, ids, sem)
    fetch.start()
    core = core_ref[0]
    for k in range(pieces):
        table[pl.ds(pl.multiple_of((2 * k + core) * owned, owned), owned), :] = own_ref[k]
        table[pl.ds(pl.multiple_of((2 * k + 1 - core) * owned, owned), owned), :] = other_ref[k]
    sumst[...] = jnp.zeros_like(sumst)
    ccnt[...] = jnp.zeros_like(ccnt)
    fetch.wait()

    def gather(start, got):
        for j in range(block):
            row = ids.at[pl.ds(j, rows - block + 1)][start]
            got[pl.ds(j, 1), :] = table[pl.ds(row, 1), :]

    def work(start, got):
        here = pl.ds(start, block)
        rest = (x_ref[here, :] - got[...]).T
        rest_ref[:, here] = rest
        hi = rest.astype(jnp.bfloat16)
        lo = (rest - hi.astype(jnp.float32)).astype(jnp.bfloat16)
        label = lax.broadcasted_iota(jnp.int32, (half, block), 0)
        digit = lax.broadcasted_iota(jnp.int32, (SUB_DIM, block), 0)
        left, right = [], []
        for m in range(subs):
            code = codes_ref[pl.ds(m, 1), here]
            left.append((lax.shift_right_logical(code, 4) == digit).astype(jnp.bfloat16))
            right.append(((code & (SUB_DIM - 1)) == digit).astype(jnp.bfloat16))
        ccnt[...] += lax.dot_general(
            jnp.concatenate(left, 0), jnp.concatenate(right, 0), NT, preferred_element_type=jnp.float32
        )
        for p in range(subs // 2):
            left, right = [], []
            for m in (2 * p, 2 * p + 1):
                code = codes_ref[pl.ds(m, 1), here]
                right.append(((code & (half - 1)) == label).astype(jnp.bfloat16))
                f = slice(m * SUB_DIM, (m + 1) * SUB_DIM)
                both = jnp.concatenate([hi[f], lo[f]], 0)
                top = jnp.broadcast_to((code < half).astype(jnp.bfloat16), both.shape)
                first = both * top
                left += [first, both - first]
            part = lax.dot_general(
                jnp.concatenate(left, 0), jnp.concatenate(right, 0), NT, preferred_element_type=jnp.float32
            )
            for s in range(2):
                f = slice((2 * p + s) * SUB_DIM, (2 * p + s + 1) * SUB_DIM)
                for h in range(2):
                    band = part[(4 * s + 2 * h) * SUB_DIM : (4 * s + 2 * h + 2) * SUB_DIM, s * half : (s + 1) * half]
                    sumst[f, h * half : (h + 1) * half] += band[:SUB_DIM] + band[SUB_DIM:]

    def store(start):
        here = pl.ds(start, block)
        return pltpu.make_async_copy(rest_ref.at[:, here], rest_hbm.at[0, :, here], out_sems.at[start // block])

    gather(0, got0)

    @pl.loop(0, rows // (2 * block))
    def _(i):
        first = pl.multiple_of(2 * i * block, block)
        second = pl.multiple_of(first + block, block)
        third = pl.multiple_of(jnp.minimum(second + block, rows - block), block)
        gather(second, got1)
        work(first, got0)
        gather(third, got0)
        work(second, got1)
        store(first).start()
        store(second).start()

    total = sumst[...].T
    cc = ccnt[...]
    r = lax.broadcasted_iota(jnp.int32, cc.shape, 0) // SUB_DIM
    c = lax.broadcasted_iota(jnp.int32, cc.shape, 1) // SUB_DIM
    cc = jnp.where(r == c, cc, 0.0)
    crow = cc[0:SUB_DIM, :]
    for m in range(1, subs):
        crow = crow + cc[m * SUB_DIM : (m + 1) * SUB_DIM, :]
    fill = jnp.zeros((SLAB - 1, LANES), jnp.float32)
    for o in range(owners):
        sums_ref[o, 0:each, :] = total[o * each : (o + 1) * each, :]
        sums_ref[o, each:slab, :] = jnp.concatenate([crow[o : o + 1, :], fill], 0)
    for c in range(rows // block):
        store(c * block).wait()


def residuals(core, ids, codes_t, x, own, other, owners, codes, block=RBLOCK):
    rows, width = x.shape
    pieces, owned, _ = own.shape
    vmem = pl.BlockSpec(memory_space=pltpu.VMEM)
    return pl.pallas_call(
        resid_kernel,
        in_specs=[pl.BlockSpec(memory_space=pltpu.SMEM)] + [vmem] * 5,
        out_specs=[pl.BlockSpec(memory_space=pltpu.HBM), vmem],
        out_shape=[
            jax.ShapeDtypeStruct((SPARE, width, rows), jnp.float32),
            jax.ShapeDtypeStruct((owners, codes // owners + SLAB, width), jnp.float32),
        ],
        scratch_shapes=[
            pltpu.SMEM((rows,), jnp.int32),
            pltpu.VMEM((2 * pieces * owned, width), jnp.float32),
            pltpu.VMEM((block, width), jnp.float32),
            pltpu.VMEM((block, width), jnp.float32),
            pltpu.VMEM((width, codes), jnp.float32),
            pltpu.VMEM((LANES, LANES), jnp.float32),
            pltpu.VMEM((width, rows), jnp.float32),
            pltpu.SemaphoreType.DMA(()),
            pltpu.SemaphoreType.DMA((rows // block,)),
        ],
        compiler_params=pltpu.CompilerParams(vmem_limit_bytes=VLIM),
        name="residuals",
    )(core, ids, codes_t, x, own, other)


def errors_kernel(book_ref, codes_ref, rest_ref, out_ref, table):
    subs = codes_ref.shape[0]
    half = book_ref.shape[0] // 2

    @pl.when(pl.program_id(0) == 0)
    def _():
        table[...] = book_ref[...].T

    for t in range(rest_ref.shape[2] // LANES):
        cols = slice(t * LANES, (t + 1) * LANES)
        acc = jnp.zeros((8, LANES), jnp.float32)
        for m in range(subs):
            idx = jnp.broadcast_to(codes_ref[m : m + 1, cols], (8, LANES))
            low = idx & (half - 1)
            first = idx < half
            for g in range(SUB_DIM // 8):
                f = slice(m * SUB_DIM + g * 8, m * SUB_DIM + g * 8 + 8)
                a = jnp.take_along_axis(table[f, 0:half], low, axis=1)
                b = jnp.take_along_axis(table[f, half : 2 * half], low, axis=1)
                d = rest_ref[0, f, cols] - jnp.where(first, a, b)
                acc = acc + d * d
        row = jnp.sum(acc, axis=0, keepdims=True)
        for k in range(out_ref.shape[0]):
            out_ref[k, t : t + 1, :] = row


def errors(book, codes_t, rest, copies, block=EBLOCK):
    _, width, rows = rest.shape
    return pl.pallas_call(
        errors_kernel,
        grid=(rows // block,),
        in_specs=[
            pl.BlockSpec(book.shape, lambda i: (0, 0)),
            pl.BlockSpec((codes_t.shape[0], block), lambda i: (0, i)),
            pl.BlockSpec((1, width, block), lambda i: (0, 0, i)),
        ],
        out_specs=pl.BlockSpec((copies, block // LANES, LANES), lambda i: (0, i, 0)),
        out_shape=jax.ShapeDtypeStruct((copies, rows // LANES, LANES), jnp.float32),
        scratch_shapes=[pltpu.VMEM((width, book.shape[0]), jnp.float32)],
        compiler_params=pltpu.CompilerParams(vmem_limit_bytes=58 * 2**20),
        name="errors",
    )(book, codes_t, rest)


def book_kernel(prior, part_ref, old_ref, book_ref, copies_ref):
    total = part_ref[0]
    for k in range(1, part_ref.shape[0]):
        total = total + part_ref[k]
    shape = old_ref.shape
    row = jnp.broadcast_to(total[shape[0] : shape[0] + 1, :], shape)
    lane = lax.broadcasted_iota(jnp.int32, shape, 1)
    code = lax.broadcasted_iota(jnp.int32, shape, 0)
    picked = jnp.where(lane % SUB_DIM == code, row, 0.0)
    r = lax.broadcasted_iota(jnp.int32, (LANES, LANES), 0) // SUB_DIM
    c = lax.broadcasted_iota(jnp.int32, (LANES, LANES), 1) // SUB_DIM
    ones = (r == c).astype(jnp.float32)
    counts = jnp.dot(picked, ones, precision=HIGH, preferred_element_type=jnp.float32)
    book = (total[: shape[0], :] + prior * old_ref[...]) / (counts + prior)
    book_ref[...] = book
    for k in range(copies_ref.shape[0]):
        copies_ref[k] = book


def new_codebook(parts, old, prior):
    return pl.pallas_call(
        functools.partial(book_kernel, prior),
        out_shape=[
            jax.ShapeDtypeStruct(old.shape, jnp.float32),
            jax.ShapeDtypeStruct((parts.shape[0],) + old.shape, jnp.float32),
        ],
        compiler_params=pltpu.CompilerParams(vmem_limit_bytes=4 * 2**20),
        name="codebook",
    )(parts, old)


def swap(x, axis, n, bit):
    return lax.ppermute(x, axis, [(i, i ^ bit) for i in range(n)])


def local(passages, list_ids, code_ids, old_centroids, old_codebook):
    rows, width = passages.shape
    n_row = lax.axis_size("row")
    n_col = lax.axis_size("col")
    total = rows * n_row
    owned_lists = old_centroids.shape[0]
    owned_codes = old_codebook.shape[0]
    lists = owned_lists * n_row
    codes = owned_codes * n_row
    list_prior = float(total // lists)
    code_prior = float(total // codes)
    pieces = n_row // 2
    same_core = [[2 * k + c for k in range(pieces)] for c in range(2)]
    core = (lax.axis_index("row") % 2).astype(jnp.int32).reshape(1)
    codes_t = code_ids.T

    keep, send = list_sums(core, list_ids, passages, pieces, lists)
    pair = keep + swap(send, "row", n_row, 1)
    parts = lax.all_to_all(pair, "row", 0, 0, axis_index_groups=same_core, tiled=True)
    centroids, copies = new_centroids(parts, old_centroids, list_prior)
    own = lax.all_to_all(copies, "row", 0, 0, axis_index_groups=same_core, tiled=True)
    other = swap(own, "row", n_row, 1)
    rest, sums = residuals(core, list_ids, codes_t, passages, own, other, n_row, codes)
    parts = lax.all_to_all(sums, "row", 0, 0, tiled=True)
    codebook, copies = new_codebook(parts, old_codebook, code_prior)
    book = lax.all_to_all(copies, "row", 0, 0, tiled=True).reshape(codes, width)
    err = errors(book, codes_t, rest, n_col)
    err = lax.all_to_all(err, "col", 0, 0, tiled=True)
    return centroids, codebook, jnp.sum(err, axis=0).reshape(rows) / D


def solution(mesh):
    in_specs = (P("row", "col"), P("row"), P("row", "col"), P("row", "col"), P("row", "col"))
    out_specs = (P("row", "col"), P("row", "col"), P("row"))
    return jax.shard_map(local, mesh=mesh, in_specs=in_specs, out_specs=out_specs, check_vma=False)
```

time: 117 us -> 113 us (0.966)
  blocking collectives: 59.7 us -> 76.2 us
  starting transfers between devices: 8.86 us -> 0.09 us
  waiting for transfers between devices: 12 us -> 5.35 us
  local copies, waits for them, and re-layouts: 4.16 us -> 0.77 us
  other arithmetic: 2.02 us -> 0.75 us
    all_to_all x1 -> x2, blocking collectives: 9.69 us -> 26.4 us  [the longest x1 16.6 us: local(): err = lax.all_to_all(err, 'col', 0, 0, tiled=True)]
    ppermute x5 -> x2, starting transfers between devices: 8.86 us -> 0.09 us  [swap(): return lax.ppermute(x, axis, [(i, i ^ bit) for i in range(n)])]
    ppermute x5 -> x2, waiting for transfers between devices: 12 us -> 5.35 us  [swap(): return lax.ppermute(x, axis, [(i, i ^ bit) for i in range(n)])]
    unnamed x14 -> x10, local copies, waits for them, and re-layouts: 4.16 us -> 0.77 us
    pallas_call x1, Pallas kernels: 11.4 us -> 9.05 us  [list_sums(): pl.pallas_call(sums_kernel, in_specs=[pl.BlockSpec(memory_space=pltpu.SME...]
    pallas_call x1, Pallas kernels: 4.52 us -> 6.45 us  [errors(): pl.pallas_call(errors_kernel, grid=(rows // block,), in_specs=[pl.BlockSp...]
    add x1, other arithmetic: 1.39 us -> 0.12 us  [local(): pair = keep + swap(send, 'row', n_row, 1)]
  transfers between devices with their start and end apart: 5 -> 2, of which waited for: 5 -> 2; matrix products, arithmetic and copies ran while one was open for 0% -> 0% of each run, Pallas kernels for 0% -> 0%
where the time goes in v3:
time: 113 us; the launch traced here: 112 us
  blocking collectives  76.2 us (67%)
  Pallas kernels  28.7 us (25%)
  waiting for transfers between devices  5.35 us (5%)
    all_to_all x1, blocking collectives, local(): lax.all_to_all(pair, 'row', 0, 0, axis_index_groups=same_core, tiled=True)  22 us
    all_to_all x1, blocking collectives, local(): lax.all_to_all(copies, 'row', 0, 0, axis_index_groups=same_core, tiled=True)  18.1 us
    all_to_all x1, blocking collectives, local(): err = lax.all_to_all(err, 'col', 0, 0, tiled=True)  16.6 us
    pallas_call x1, Pallas kernels, residuals(): pl.pallas_call(resid_kernel, in_specs=[pl.BlockSpec(memory_space=pltpu.SM...  11.5 us
    all_to_all x1, blocking collectives, local(): parts = lax.all_to_all(sums, 'row', 0, 0, tiled=True)  9.73 us
    all_to_all x1, blocking collectives, local(): book = lax.all_to_all(copies, 'row', 0, 0, tiled=True).reshape(codes, width)  9.7 us
    pallas_call x1, Pallas kernels, list_sums(): pl.pallas_call(sums_kernel, in_specs=[pl.BlockSpec(memory_space=pltpu.SME...  9.05 us
    pallas_call x1, Pallas kernels, errors(): pl.pallas_call(errors_kernel, grid=(rows // block,), in_specs=[pl.BlockSp...  6.45 us
  transfers between devices with their start and end apart: 2, of which 2 were waited for; matrix products, arithmetic and copies ran while one was open for 0% of the time, Pallas kernels for 0%

profile of v3, /device:TPU:0, one launch (start us, length us, event | category | flops | bytes accessed | tf_op | source)
XLA Modules:
  0.0 112.5 jit_solution(4527741864558054870)
XLA Ops:
  0.6 0.0 copy-start.2
  0.7 0.7 copy-done.2
  1.4 9.0 %list_sums.1 = (f32[8,264,128]{2,1,0:T(8,128)S(1)}, f32[8,264,128]{2,1,0:T(8,128)S(1)}) custom-call(s32[1]{0:T(128)} %bitcast.core_ref, s32[8192]{0:T(1024)S(1)} %copy-done.2, s32[64,128]{1,0:T(8,128)S(1)} %bitcast.8, f32[8192,128]{1,0:T(8,128)} %x_ref.1), custom_call_target="tpu_custom_call" | custom-call | tf_op jit(solution)/shard_map/list_sums/pallas_call | solution.py:117
  10.5 0.1 collective-permute-start
  10.5 2.7 %collective-permute-done = f32[8,264,128]{2,1,0:T(8,128)S(1)} collective-permute-done((f32[8,264,128]{2,1,0:T(8,128)S(1)}, f32[8,264,128]{2,1,0:T(8,128)S(1)}, u32[]{:S(2)}, u32[]{:S(2)}) %collective-permute-start) | collective-permute-done | bytes 1081376 | tf_op jit(solution)/shard_map/ppermute | solution.py:368
  13.2 0.0 copy-start.3
  13.2 0.1 add.8
  13.4 0.0 copy-start
  13.4 22.0 %all_to_all.25.part_ref = f32[8,264,128]{2,1,0:T(8,128)S(1)} all-to-all(f32[8,264,128]{2,1,0:T(8,128)S(1)} %add.8), channel_id=1, replica_groups={{0,16,32,48,64,80,96,112},{8,24,40,56,72,88,104,120},{1,17,33,49,65,81,..., dimensions={0} | all-to-all | bytes 2162688 | tf_op jit(solution)/shard_map/all_to_all | solution.py:389
  35.4 0.0 copy-done.3
  35.4 0.8 centroids.1
  36.2 0.0 copy-start.1
  36.2 18.1 %all_to_all.26.own_ref = f32[8,256,128]{2,1,0:T(8,128)S(1)} all-to-all(f32[8,256,128]{2,1,0:T(8,128)S(1)} %get-tuple-element.14), channel_id=1, replica_groups={{0,16,32,48,64,80,96,112},{8,24,40,56,72,88,104,120},{1,17,33,49,65,81,..., dimensions={0} | all-to-all | bytes 2097152 | tf_op jit(solution)/shard_map/all_to_all | solution.py:391
  54.3 0.0 collective-permute-start.1
  54.3 2.7 %collective-permute-done.1.other_ref = f32[8,256,128]{2,1,0:T(8,128)S(1)} collective-permute-done((f32[8,256,128]{2,1,0:T(8,128)S(1)}, f32[8,256,128]{2,1,0:T(8,128)S(1)}, u32[]{:S(2)}, u32[]{:S(2)}) %collective-permute-start.1) | collective-permute-done | bytes 1048608 | tf_op jit(solution)/shard_map/ppermute | solution.py:368
  57.0 0.0 copy-done
  57.0 0.0 copy-done.1
  57.0 0.0 copy-start.4
  57.0 11.5 %residuals.1 = (f32[5,128,8192]{2,1,0:T(8,128)}, f32[16,24,128]{2,1,0:T(8,128)S(1)}) custom-call(s32[1]{0:T(128)} %bitcast.core_ref, s32[8192]{0:T(1024)S(1)} %copy-done.2, s32[8,8192]{1,0:T(8,128)S(1)} %bitcast.7, f32[8192,128]{1,0:T(8,128)S(1)} %copy-done, f32[8,256,128]{2,1,0:T(8,128)S(1)} %all_to_all.26.own_ref, ...), custom_call_target="tpu_custom_call" | custom-call | tf_op jit(solution)/shard_map/residuals/pallas_call | solution.py:268
  68.5 9.7 %all_to_all.27.part_ref = f32[16,24,128]{2,1,0:T(8,128)S(1)} all-to-all(f32[16,24,128]{2,1,0:T(8,128)S(1)} %get-tuple-element.15), channel_id=1, replica_groups=mesh['row'=16,'col'=8] {'row'}, dimensions={0} | all-to-all | bytes 393216 | tf_op jit(solution)/shard_map/all_to_all | solution.py:394
  78.3 0.0 copy-done.4
  78.3 0.8 codebook.1
  79.1 9.7 %all_to_all.28 = f32[16,16,128]{2,1,0:T(8,128)} all-to-all(f32[16,16,128]{2,1,0:T(8,128)S(1)} %get-tuple-element.17), channel_id=1, replica_groups=mesh['row'=16,'col'=8] {'row'}, dimensions={0} | all-to-all | bytes 262144 | tf_op jit(solution)/shard_map/all_to_all | solution.py:396
  88.8 6.4 %errors.1 = f32[8,64,128]{2,1,0:T(8,128)} custom-call(f32[256,128]{1,0:T(8,128)} %bitcast.9, s32[8,8192]{1,0:T(8,128)} %bitcast.6, f32[5,128,8192]{2,1,0:T(8,128)} %get-tuple-element.18.rest_ref), custom_call_target="tpu_custom_call" | custom-call | tf_op jit(solution)/shard_map/errors/pallas_call | solution.py:320
  95.2 16.6 %all_to_all.29 = f32[8,64,128]{2,1,0:T(8,128)S(1)} all-to-all(f32[8,64,128]{2,1,0:T(8,128)} %errors.1), channel_id=1, replica_groups=mesh['row'=16,'col'=8] {'col'}, dimensions={0} | all-to-all | bytes 524288 | tf_op jit(solution)/shard_map/all_to_all | solution.py:398
  111.9 0.6 multiply_bitcast_fusion
  (1 shorter events, 0.0 us)
Async XLA Ops:
  0.6 0.8 copy-start.2
  10.5 2.8 %collective-permute-start = (f32[8,264,128]{2,1,0:T(8,128)S(1)}, f32[8,264,128]{2,1,0:T(8,128)S(1)}, u32[]{:S(2)}, u32[]{:S(2)}) collective-permute-start(f32[8,264,128]{2,1,0:T(8,128)S(1)} %get-tuple-element.12), channel_id=1, source_target_pairs={{0,8},{8,0},{16,24},{24,16},{32,40},{40,32},{48,56},{56,48},{64,72... | collective-permute-start | bytes 3244040 | tf_op jit(solution)/shard_map/ppermute | solution.py:368
  13.2 22.2 %copy-start.3 = (f32[256,128]{1,0:T(8,128)S(1)}, f32[256,128]{1,0:T(8,128)}, u32[]{:S(2)}) copy-start(f32[256,128]{1,0:T(8,128)} %old_ref.2) | copy-start | bytes 393220
  13.4 43.6 %copy-start = (f32[8192,128]{1,0:T(8,128)S(1)}, f32[8192,128]{1,0:T(8,128)}, u32[]{:S(2)}) copy-start(f32[8192,128]{1,0:T(8,128)} %x_ref.1) | copy-start | bytes 12582916
  36.2 20.8 %copy-start.1 = (s32[8192,8]{0,1:T(8,128)S(1)}, s32[8192,8]{0,1:T(8,128)}, u32[]{:S(2)}) copy-start(s32[8192,8]{0,1:T(8,128)} %param.7) | copy-start | bytes 786436
  54.3 2.7 %collective-permute-start.1 = (f32[8,256,128]{2,1,0:T(8,128)S(1)}, f32[8,256,128]{2,1,0:T(8,128)S(1)}, u32[]{:S(2)}, u32[]{:S(2)}) collective-permute-start(f32[8,256,128]{2,1,0:T(8,128)S(1)} %all_to_all.26.own_ref), channel_id=1, source_target_pairs={{0,8},{8,0},{16,24},{24,16},{32,40},{40,32},{48,56},{56,48},{64,72... | collective-permute-start | bytes 3145736 | tf_op jit(solution)/shard_map/ppermute | solution.py:368
  57.0 21.3 %copy-start.4 = (f32[16,128]{1,0:T(8,128)S(1)}, f32[16,128]{1,0:T(8,128)}, u32[]{:S(2)}) copy-start(f32[16,128]{1,0:T(8,128)} %old_ref.3) | copy-start | bytes 24580

commit v4 on v3

--- a/solution.py
+++ b/solution.py
@@ -16,7 +16,8 @@
 K1LIM = 50 * 2**20
 SPARE = 5
 RBLOCK = 512
-EBLOCK = 2048
+EBLOCK = 512
+EPAIRS = 2
 VLIM = 40 * 2**20
 
 
@@ -40,29 +41,19 @@
     for c in range(1, nchunk):
         part(c).start()
 
-    zero = jnp.zeros((ZROWS, LANES), jnp.float32)
-
-    @pl.loop(0, lists // ZROWS)
-    def _(i):
-        for acc in accs:
-            acc[pl.ds(pl.multiple_of(i * ZROWS, ZROWS), ZROWS), :] = zero
-
-    lcnt[...] = jnp.zeros_like(lcnt)
     fetch_idv.wait()
-    fetch_ids.wait()
     nhi = lists // LANES
     nt = (((1,), (1,)), ((), ()))
 
-    def counts(start):
+    def counts():
         hi_iota = lax.broadcasted_iota(jnp.int32, (nhi, LANES), 0)
         lo_iota = lax.broadcasted_iota(jnp.int32, (LANES, LANES), 0)
         his, los = [], []
-        group = idv[pl.ds(pl.multiple_of(start // LANES, CBLOCK // LANES), CBLOCK // LANES), :]
-        for t in range(CBLOCK // LANES):
-            row = group[t : t + 1, :]
+        for t in range(rows // LANES):
+            row = idv[t : t + 1, :]
             his.append((lax.shift_right_logical(row, 7) == hi_iota).astype(jnp.bfloat16))
             los.append(((row & (LANES - 1)) == lo_iota).astype(jnp.bfloat16))
-        lcnt[...] += lax.dot_general(
+        lcnt[...] = lax.dot_general(
             jnp.concatenate(his, 1), jnp.concatenate(los, 1), nt, preferred_element_type=jnp.float32
         )
 
@@ -74,6 +65,11 @@
             for j in range(NACC):
                 accs[j][pl.ds(row[j], 1), :] = old[j] + new[j]
 
+    for acc in accs:
+        acc[...] = jnp.zeros_like(acc)
+    counts()
+    fetch_ids.wait()
+
     @pl.loop(0, nchunk)
     def _(c):
         part(c).wait()
@@ -82,7 +78,6 @@
         def _(i):
             start = pl.multiple_of(c * chunk + i * CBLOCK, CBLOCK)
             scatter(start)
-            counts(start)
 
     core = core_ref[0]
     for out, par in ((send_ref, 1 - core), (keep_ref, core)):
@@ -104,7 +99,6 @@
 
 
 CBLOCK = 1024
-ZROWS = 64
 NCHUNK = 8
 
 
@@ -187,10 +181,16 @@
     ccnt[...] = jnp.zeros_like(ccnt)
     fetch.wait()
 
+    sublane = lax.broadcasted_iota(jnp.int32, (8, LANES), 0)
+
     def gather(start, got):
-        for j in range(block):
-            row = ids.at[pl.ds(j, rows - block + 1)][start]
-            got[pl.ds(j, 1), :] = table[pl.ds(row, 1), :]
+        for g in range(0, block, 8):
+            tile = None
+            for j in range(8):
+                row = ids.at[pl.ds(g + j, rows - block + 1)][start]
+                line = jnp.broadcast_to(table[pl.ds(row, 1), :], (8, LANES))
+                tile = line if j == 0 else jnp.where(sublane == j, line, tile)
+            got[g : g + 8, :] = tile
 
     def work(start, got):
         here = pl.ds(start, block)
@@ -289,46 +289,99 @@
     )(core, ids, codes_t, x, own, other)
 
 
-def errors_kernel(book_ref, codes_ref, rest_ref, out_ref, table):
-    subs = codes_ref.shape[0]
+def book_bands(book_t, pair):
+    half = book_t.shape[1] // 2
+    bands = []
+    for s in range(2):
+        f = slice((2 * pair + s) * SUB_DIM, (2 * pair + s + 1) * SUB_DIM)
+        for h in range(2):
+            words = book_t[f, h * half : (h + 1) * half]
+            hi = words.astype(jnp.bfloat16)
+            lo = (words - hi.astype(jnp.float32)).astype(jnp.bfloat16)
+            none = jnp.zeros_like(hi)
+            bands += [jnp.concatenate([p, none] if s == 0 else [none, p], 1) for p in (hi, lo)]
+    return jnp.concatenate(bands, 0)
+
+
+def errors_kernel(book_ref, codes_ref, rest_hbm, out_ref, table, bands, rest_ref, sems):
+    subs, rows = codes_ref.shape
     half = book_ref.shape[0] // 2
-
-    @pl.when(pl.program_id(0) == 0)
-    def _():
-        table[...] = book_ref[...].T
-
-    for t in range(rest_ref.shape[2] // LANES):
-        cols = slice(t * LANES, (t + 1) * LANES)
+    nchunk = sems.shape[0]
+    chunk = rows // nchunk
+    by_product = bands.shape[0]
+    looked_up = subs - 2 * by_product
+
+    def load(c):
+        here = pl.ds(c * chunk, chunk)
+        return pltpu.make_async_copy(rest_hbm.at[0, :, here], rest_ref.at[:, here], sems.at[c])
+
+    load(0).start()
+    load(1).start()
+    table[...] = book_ref[...].T
+    for q in range(by_product):
+        bands[q] = book_bands(table[...], looked_up // 2 + q)
+    label = lax.broadcasted_iota(jnp.int32, (half, EBLOCK), 0)
+
+    def product(here):
+        acc = jnp.zeros((8, EBLOCK), jnp.float32)
+        for q in range(by_product):
+            m0 = looked_up + 2 * q
+            code = [codes_ref[m : m + 1, here] for m in (m0, m0 + 1)]
+            hot = [((c & (half - 1)) == label).astype(jnp.bfloat16) for c in code]
+            part = jnp.dot(bands[q], jnp.concatenate(hot, 0), preferred_element_type=jnp.float32)
+            for s in range(2):
+                p = [part[(4 * s + b) * SUB_DIM : (4 * s + b + 1) * SUB_DIM, :] for b in range(4)]
+                word = jnp.where(jnp.broadcast_to(code[s] < half, p[0].shape), p[0] + p[1], p[2] + p[3])
+                d = rest_ref[(m0 + s) * SUB_DIM : (m0 + s + 1) * SUB_DIM, here] - word
+                d = d * d
+                for g in range(0, SUB_DIM, 8):
+                    acc = acc + d[g : g + 8, :]
+        return acc
+
+    def lookup(cols):
         acc = jnp.zeros((8, LANES), jnp.float32)
-        for m in range(subs):
+        for m in range(looked_up):
             idx = jnp.broadcast_to(codes_ref[m : m + 1, cols], (8, LANES))
             low = idx & (half - 1)
             first = idx < half
-            for g in range(SUB_DIM // 8):
-                f = slice(m * SUB_DIM + g * 8, m * SUB_DIM + g * 8 + 8)
+            for g in range(0, SUB_DIM, 8):
+                f = slice(m * SUB_DIM + g, m * SUB_DIM + g + 8)
                 a = jnp.take_along_axis(table[f, 0:half], low, axis=1)
                 b = jnp.take_along_axis(table[f, half : 2 * half], low, axis=1)
-                d = rest_ref[0, f, cols] - jnp.where(first, a, b)
+                d = rest_ref[f, cols] - jnp.where(first, a, b)
                 acc = acc + d * d
-        row = jnp.sum(acc, axis=0, keepdims=True)
-        for k in range(out_ref.shape[0]):
-            out_ref[k, t : t + 1, :] = row
-
-
-def errors(book, codes_t, rest, copies, block=EBLOCK):
+        return acc
+
+    for c in range(nchunk):
+        load(c).wait()
+        if c + 2 < nchunk:
+            load(c + 2).start()
+        for b in range(c * chunk, (c + 1) * chunk, EBLOCK):
+            wide = product(slice(b, b + EBLOCK))
+            for t in range(0, EBLOCK, LANES):
+                acc = wide[:, t : t + LANES] + lookup(slice(b + t, b + t + LANES))
+                row = jnp.sum(acc, axis=0, keepdims=True)
+                at = (b + t) // LANES
+                for k in range(out_ref.shape[0]):
+                    out_ref[k, at : at + 1, :] = row
+
+
+def errors(book, codes_t, rest, copies):
     _, width, rows = rest.shape
+    codes = book.shape[0]
+    vmem = pl.BlockSpec(memory_space=pltpu.VMEM)
     return pl.pallas_call(
         errors_kernel,
-        grid=(rows // block,),
-        in_specs=[
-            pl.BlockSpec(book.shape, lambda i: (0, 0)),
-            pl.BlockSpec((codes_t.shape[0], block), lambda i: (0, i)),
-            pl.BlockSpec((1, width, block), lambda i: (0, 0, i)),
+        in_specs=[vmem, vmem, pl.BlockSpec(memory_space=pl.ANY)],
+        out_specs=vmem,
+        out_shape=jax.ShapeDtypeStruct((copies, rows // LANES, LANES), jnp.float32),
+        scratch_shapes=[
+            pltpu.VMEM((width, codes), jnp.float32),
+            pltpu.VMEM((EPAIRS, LANES, codes), jnp.bfloat16),
+            pltpu.VMEM((width, rows), jnp.float32),
+            pltpu.SemaphoreType.DMA((4,)),
         ],
-        out_specs=pl.BlockSpec((copies, block // LANES, LANES), lambda i: (0, i, 0)),
-        out_shape=jax.ShapeDtypeStruct((copies, rows // LANES, LANES), jnp.float32),
-        scratch_shapes=[pltpu.VMEM((width, book.shape[0]), jnp.float32)],
-        compiler_params=pltpu.CompilerParams(vmem_limit_bytes=58 * 2**20),
+        compiler_params=pltpu.CompilerParams(vmem_limit_bytes=40 * 2**20),
         name="errors",
     )(book, codes_t, rest)
 

time: 113 us -> 109 us (0.965)
  Pallas kernels: 28.7 us -> 25.5 us
    pallas_call x1, Pallas kernels: 6.45 us -> 4.18 us  [errors(): pl.pallas_call(errors_kernel, in_specs=[vmem, vmem, pl.BlockSpec(memory_s...]
where the time goes in v4:
time: 109 us
  blocking collectives  75.3 us (69%)
  Pallas kernels  25.5 us (23%)
  waiting for transfers between devices  5.35 us (5%)
    all_to_all x1, blocking collectives, local(): lax.all_to_all(pair, 'row', 0, 0, axis_index_groups=same_core, tiled=True)  22 us
    all_to_all x1, blocking collectives, local(): lax.all_to_all(copies, 'row', 0, 0, axis_index_groups=same_core, tiled=True)  18.1 us
    all_to_all x1, blocking collectives, local(): err = lax.all_to_all(err, 'col', 0, 0, tiled=True)  16.4 us
    pallas_call x1, Pallas kernels, residuals(): pl.pallas_call(resid_kernel, in_specs=[pl.BlockSpec(memory_space=pltpu.SM...  11.4 us
    all_to_all x1, blocking collectives, local(): parts = lax.all_to_all(sums, 'row', 0, 0, tiled=True)  9.76 us
    all_to_all x1, blocking collectives, local(): book = lax.all_to_all(copies, 'row', 0, 0, tiled=True).reshape(codes, width)  9.02 us
    pallas_call x1, Pallas kernels, list_sums(): pl.pallas_call(sums_kernel, in_specs=[pl.BlockSpec(memory_space=pltpu.SME...  8.37 us
    ppermute x2, waiting for transfers between devices, swap(): return lax.ppermute(x, axis, [(i, i ^ bit) for i in range(n)])  5.35 us
  transfers between devices with their start and end apart: 2, of which 2 were waited for; matrix products, arithmetic and copies ran while one was open for 0% of the time, Pallas kernels for 0%

profile of v4, /device:TPU:0, one launch (start us, length us, event | category | flops | bytes accessed | tf_op | source)
XLA Modules:
  0.0 108.5 jit_solution(10961803684002841363)
XLA Ops:
  0.6 0.0 copy-start.2
  0.7 0.7 copy-done.2
  1.4 8.4 %list_sums.1 = (f32[8,264,128]{2,1,0:T(8,128)S(1)}, f32[8,264,128]{2,1,0:T(8,128)S(1)}) custom-call(s32[1]{0:T(128)} %bitcast.core_ref, s32[8192]{0:T(1024)S(1)} %copy-done.2, s32[64,128]{1,0:T(8,128)S(1)} %bitcast.9, f32[8192,128]{1,0:T(8,128)} %x_ref.1), custom_call_target="tpu_custom_call" | custom-call | tf_op jit(solution)/shard_map/list_sums/pallas_call | solution.py:111
  9.8 0.1 collective-permute-start
  9.9 2.7 %collective-permute-done = f32[8,264,128]{2,1,0:T(8,128)S(1)} collective-permute-done((f32[8,264,128]{2,1,0:T(8,128)S(1)}, f32[8,264,128]{2,1,0:T(8,128)S(1)}, u32[]{:S(2)}, u32[]{:S(2)}) %collective-permute-start) | collective-permute-done | bytes 1081376 | tf_op jit(solution)/shard_map/ppermute | solution.py:421
  12.6 0.0 copy-start.3
  12.6 0.1 add.8
  12.7 0.0 copy-start
  12.7 22.0 %all_to_all.25.part_ref = f32[8,264,128]{2,1,0:T(8,128)S(1)} all-to-all(f32[8,264,128]{2,1,0:T(8,128)S(1)} %add.8), channel_id=1, replica_groups={{0,16,32,48,64,80,96,112},{8,24,40,56,72,88,104,120},{1,17,33,49,65,81,..., dimensions={0} | all-to-all | bytes 2162688 | tf_op jit(solution)/shard_map/all_to_all | solution.py:442
  34.7 0.0 copy-done.3
  34.7 0.8 centroids.1
  35.5 0.0 copy-start.1
  35.6 18.1 %all_to_all.26.own_ref = f32[8,256,128]{2,1,0:T(8,128)S(1)} all-to-all(f32[8,256,128]{2,1,0:T(8,128)S(1)} %get-tuple-element.14), channel_id=1, replica_groups={{0,16,32,48,64,80,96,112},{8,24,40,56,72,88,104,120},{1,17,33,49,65,81,..., dimensions={0} | all-to-all | bytes 2097152 | tf_op jit(solution)/shard_map/all_to_all | solution.py:444
  53.6 0.0 collective-permute-start.1
  53.6 2.7 %collective-permute-done.1.other_ref = f32[8,256,128]{2,1,0:T(8,128)S(1)} collective-permute-done((f32[8,256,128]{2,1,0:T(8,128)S(1)}, f32[8,256,128]{2,1,0:T(8,128)S(1)}, u32[]{:S(2)}, u32[]{:S(2)}) %collective-permute-start.1) | collective-permute-done | bytes 1048608 | tf_op jit(solution)/shard_map/ppermute | solution.py:421
  56.3 0.0 copy-done
  56.3 0.0 copy-done.1
  56.3 0.0 copy-start.4
  56.3 11.4 %residuals.1 = (f32[5,128,8192]{2,1,0:T(8,128)}, f32[16,24,128]{2,1,0:T(8,128)S(1)}) custom-call(s32[1]{0:T(128)} %bitcast.core_ref, s32[8192]{0:T(1024)S(1)} %copy-done.2, s32[8,8192]{1,0:T(8,128)S(1)} %bitcast.6, f32[8192,128]{1,0:T(8,128)S(1)} %copy-done, f32[8,256,128]{2,1,0:T(8,128)S(1)} %all_to_all.26.own_ref, ...), custom_call_target="tpu_custom_call" | custom-call | tf_op jit(solution)/shard_map/residuals/pallas_call | solution.py:268
  67.7 9.8 %all_to_all.27.part_ref = f32[16,24,128]{2,1,0:T(8,128)S(1)} all-to-all(f32[16,24,128]{2,1,0:T(8,128)S(1)} %get-tuple-element.15), channel_id=1, replica_groups=mesh['row'=16,'col'=8] {'row'}, dimensions={0} | all-to-all | bytes 393216 | tf_op jit(solution)/shard_map/all_to_all | solution.py:447
  77.4 0.0 copy-done.4
  77.4 0.8 codebook.1
  78.2 9.0 %all_to_all.28 = f32[16,16,128]{2,1,0:T(8,128)S(1)} all-to-all(f32[16,16,128]{2,1,0:T(8,128)S(1)} %get-tuple-element.17), channel_id=1, replica_groups=mesh['row'=16,'col'=8] {'row'}, dimensions={0} | all-to-all | bytes 262144 | tf_op jit(solution)/shard_map/all_to_all | solution.py:449
  87.3 4.2 %errors.1 = f32[8,64,128]{2,1,0:T(8,128)S(1)} custom-call(f32[256,128]{1,0:T(8,128)S(1)} %bitcast.8, s32[8,8192]{1,0:T(8,128)S(1)} %bitcast.7, f32[5,128,8192]{2,1,0:T(8,128)} %get-tuple-element.18.rest_hbm), custom_call_target="tpu_custom_call" | custom-call | tf_op jit(solution)/shard_map/errors/pallas_call | solution.py:373
  91.4 16.4 %all_to_all.29 = f32[8,64,128]{2,1,0:T(8,128)S(1)} all-to-all(f32[8,64,128]{2,1,0:T(8,128)S(1)} %errors.1), channel_id=1, replica_groups=mesh['row'=16,'col'=8] {'col'}, dimensions={0} | all-to-all | bytes 524288 | tf_op jit(solution)/shard_map/all_to_all | solution.py:451
  107.9 0.6 multiply_bitcast_fusion
  (1 shorter events, 0.0 us)
Async XLA Ops:
  0.6 0.8 copy-start.2
  9.8 2.8 %collective-permute-start = (f32[8,264,128]{2,1,0:T(8,128)S(1)}, f32[8,264,128]{2,1,0:T(8,128)S(1)}, u32[]{:S(2)}, u32[]{:S(2)}) collective-permute-start(f32[8,264,128]{2,1,0:T(8,128)S(1)} %get-tuple-element.12), channel_id=1, source_target_pairs={{0,8},{8,0},{16,24},{24,16},{32,40},{40,32},{48,56},{56,48},{64,72... | collective-permute-start | bytes 3244040 | tf_op jit(solution)/shard_map/ppermute | solution.py:421
  12.6 22.1 %copy-start.3 = (f32[256,128]{1,0:T(8,128)S(1)}, f32[256,128]{1,0:T(8,128)}, u32[]{:S(2)}) copy-start(f32[256,128]{1,0:T(8,128)} %old_ref.2) | copy-start | bytes 393220
  12.7 43.6 %copy-start = (f32[8192,128]{1,0:T(8,128)S(1)}, f32[8192,128]{1,0:T(8,128)}, u32[]{:S(2)}) copy-start(f32[8192,128]{1,0:T(8,128)} %x_ref.1) | copy-start | bytes 12582916
  35.5 20.8 %copy-start.1 = (s32[8192,8]{0,1:T(8,128)S(1)}, s32[8192,8]{0,1:T(8,128)}, u32[]{:S(2)}) copy-start(s32[8192,8]{0,1:T(8,128)} %param.7) | copy-start | bytes 786436
  53.6 2.7 %collective-permute-start.1 = (f32[8,256,128]{2,1,0:T(8,128)S(1)}, f32[8,256,128]{2,1,0:T(8,128)S(1)}, u32[]{:S(2)}, u32[]{:S(2)}) collective-permute-start(f32[8,256,128]{2,1,0:T(8,128)S(1)} %all_to_all.26.own_ref), channel_id=1, source_target_pairs={{0,8},{8,0},{16,24},{24,16},{32,40},{40,32},{48,56},{56,48},{64,72... | collective-permute-start | bytes 3145736 | tf_op jit(solution)/shard_map/ppermute | solution.py:421
  56.3 21.1 %copy-start.4 = (f32[16,128]{1,0:T(8,128)S(1)}, f32[16,128]{1,0:T(8,128)}, u32[]{:S(2)}) copy-start(f32[16,128]{1,0:T(8,128)} %old_ref.3) | copy-start | bytes 24580

commit v5 on v4

--- a/solution.py
+++ b/solution.py
@@ -14,11 +14,10 @@
 NACC = 8
 SLAB = 8
 K1LIM = 50 * 2**20
-SPARE = 5
-RBLOCK = 512
+RBLOCK = 1024
 EBLOCK = 512
 EPAIRS = 2
-VLIM = 40 * 2**20
+VLIM = 24 * 2**20
 
 
 def sums_kernel(core_ref, ids_hbm, idv_hbm, x_hbm, keep_ref, send_ref, ids, idv, x_ref, lcnt, sems, *accs):
@@ -35,13 +34,12 @@
 
     fetch_ids = pltpu.make_async_copy(ids_hbm, ids, sems.at[nchunk])
     fetch_idv = pltpu.make_async_copy(idv_hbm, idv, sems.at[nchunk + 1])
+    fetch_idv.start()
     fetch_ids.start()
     part(0).start()
-    fetch_idv.start()
     for c in range(1, nchunk):
         part(c).start()
 
-    fetch_idv.wait()
     nhi = lists // LANES
     nt = (((1,), (1,)), ((), ()))
 
@@ -65,7 +63,10 @@
             for j in range(NACC):
                 accs[j][pl.ds(row[j], 1), :] = old[j] + new[j]
 
-    for acc in accs:
+    for acc in accs[: NACC // 2]:
+        acc[...] = jnp.zeros_like(acc)
+    fetch_idv.wait()
+    for acc in accs[NACC // 2 :]:
         acc[...] = jnp.zeros_like(acc)
     counts()
     fetch_ids.wait()
@@ -104,6 +105,9 @@
 
 def list_sums(core, ids, x, pieces, lists):
     rows, width = x.shape
+    idv = ids.reshape(rows // LANES, LANES)
+    ids = pltpu.with_memory_space_constraint(ids, pltpu.HBM)
+    idv = pltpu.with_memory_space_constraint(idv, pltpu.HBM)
     owned = lists // (2 * pieces)
     out = jax.ShapeDtypeStruct((pieces, owned + SLAB, width), jnp.float32)
     hbm = pl.BlockSpec(memory_space=pltpu.HBM)
@@ -123,7 +127,7 @@
         + [pltpu.VMEM((lists, width), jnp.float32)] * NACC,
         compiler_params=pltpu.CompilerParams(vmem_limit_bytes=K1LIM),
         name="list_sums",
-    )(core, ids, ids.reshape(rows // LANES, LANES), x)
+    )(core, ids, idv, x)
 
 
 def centroid_kernel(prior, part_ref, old_ref, cent_ref, copies_ref):
@@ -162,7 +166,7 @@
 
 
 def resid_kernel(
-    core_ref, ids_ref, codes_ref, x_ref, own_ref, other_ref, rest_hbm, sums_ref, ids, table, got0, got1, sumst, ccnt, rest_ref, sem, out_sems
+    core_ref, ids_ref, codes_ref, x_ref, own_ref, other_ref, rest_ref, sums_ref, ids, table, got0, got1, sumst, ccnt, sems
 ):
     block = got0.shape[0]
     rows = x_ref.shape[0]
@@ -171,15 +175,17 @@
     owners, slab, _ = sums_ref.shape
     each = slab - SLAB
     half = owners * each // 2
-    fetch = pltpu.make_async_copy(ids_ref, ids, sem)
-    fetch.start()
+    early, late = pl.ds(0, 2 * block), pl.ds(2 * block, rows - 2 * block)
+    fetch = [pltpu.make_async_copy(ids_ref.at[p], ids.at[p], sems.at[n]) for n, p in enumerate((early, late))]
+    for f in fetch:
+        f.start()
     core = core_ref[0]
     for k in range(pieces):
         table[pl.ds(pl.multiple_of((2 * k + core) * owned, owned), owned), :] = own_ref[k]
         table[pl.ds(pl.multiple_of((2 * k + 1 - core) * owned, owned), owned), :] = other_ref[k]
     sumst[...] = jnp.zeros_like(sumst)
     ccnt[...] = jnp.zeros_like(ccnt)
-    fetch.wait()
+    fetch[0].wait()
 
     sublane = lax.broadcasted_iota(jnp.int32, (8, LANES), 0)
 
@@ -227,11 +233,8 @@
                     band = part[(4 * s + 2 * h) * SUB_DIM : (4 * s + 2 * h + 2) * SUB_DIM, s * half : (s + 1) * half]
                     sumst[f, h * half : (h + 1) * half] += band[:SUB_DIM] + band[SUB_DIM:]
 
-    def store(start):
-        here = pl.ds(start, block)
-        return pltpu.make_async_copy(rest_ref.at[:, here], rest_hbm.at[0, :, here], out_sems.at[start // block])
-
     gather(0, got0)
+    fetch[1].wait()
 
     @pl.loop(0, rows // (2 * block))
     def _(i):
@@ -242,8 +245,6 @@
         work(first, got0)
         gather(third, got0)
         work(second, got1)
-        store(first).start()
-        store(second).start()
 
     total = sumst[...].T
     cc = ccnt[...]
@@ -257,8 +258,6 @@
     for o in range(owners):
         sums_ref[o, 0:each, :] = total[o * each : (o + 1) * each, :]
         sums_ref[o, each:slab, :] = jnp.concatenate([crow[o : o + 1, :], fill], 0)
-    for c in range(rows // block):
-        store(c * block).wait()
 
 
 def residuals(core, ids, codes_t, x, own, other, owners, codes, block=RBLOCK):
@@ -268,9 +267,9 @@
     return pl.pallas_call(
         resid_kernel,
         in_specs=[pl.BlockSpec(memory_space=pltpu.SMEM)] + [vmem] * 5,
-        out_specs=[pl.BlockSpec(memory_space=pltpu.HBM), vmem],
+        out_specs=[vmem, vmem],
         out_shape=[
-            jax.ShapeDtypeStruct((SPARE, width, rows), jnp.float32),
+            jax.ShapeDtypeStruct((width, rows), jnp.float32),
             jax.ShapeDtypeStruct((owners, codes // owners + SLAB, width), jnp.float32),
         ],
         scratch_shapes=[
@@ -280,9 +279,7 @@
             pltpu.VMEM((block, width), jnp.float32),
             pltpu.VMEM((width, codes), jnp.float32),
             pltpu.VMEM((LANES, LANES), jnp.float32),
-            pltpu.VMEM((width, rows), jnp.float32),
-            pltpu.SemaphoreType.DMA(()),
-            pltpu.SemaphoreType.DMA((rows // block,)),
+            pltpu.SemaphoreType.DMA((2,)),
         ],
         compiler_params=pltpu.CompilerParams(vmem_limit_bytes=VLIM),
         name="residuals",
@@ -303,20 +300,12 @@
     return jnp.concatenate(bands, 0)
 
 
-def errors_kernel(book_ref, codes_ref, rest_hbm, out_ref, table, bands, rest_ref, sems):
+def errors_kernel(book_ref, codes_ref, rest_ref, out_ref, table, bands):
     subs, rows = codes_ref.shape
     half = book_ref.shape[0] // 2
-    nchunk = sems.shape[0]
-    chunk = rows // nchunk
     by_product = bands.shape[0]
     looked_up = subs - 2 * by_product
 
-    def load(c):
-        here = pl.ds(c * chunk, chunk)
-        return pltpu.make_async_copy(rest_hbm.at[0, :, here], rest_ref.at[:, here], sems.at[c])
-
-    load(0).start()
-    load(1).start()
     table[...] = book_ref[...].T
     for q in range(by_product):
         bands[q] = book_bands(table[...], looked_up // 2 + q)
@@ -352,36 +341,30 @@
                 acc = acc + d * d
         return acc
 
-    for c in range(nchunk):
-        load(c).wait()
-        if c + 2 < nchunk:
-            load(c + 2).start()
-        for b in range(c * chunk, (c + 1) * chunk, EBLOCK):
-            wide = product(slice(b, b + EBLOCK))
-            for t in range(0, EBLOCK, LANES):
-                acc = wide[:, t : t + LANES] + lookup(slice(b + t, b + t + LANES))
-                row = jnp.sum(acc, axis=0, keepdims=True)
-                at = (b + t) // LANES
-                for k in range(out_ref.shape[0]):
-                    out_ref[k, at : at + 1, :] = row
+    for b in range(0, rows, EBLOCK):
+        wide = product(slice(b, b + EBLOCK))
+        for t in range(0, EBLOCK, LANES):
+            acc = wide[:, t : t + LANES] + lookup(slice(b + t, b + t + LANES))
+            row = jnp.sum(acc, axis=0, keepdims=True)
+            at = (b + t) // LANES
+            for k in range(out_ref.shape[0]):
+                out_ref[k, at : at + 1, :] = row
 
 
 def errors(book, codes_t, rest, copies):
-    _, width, rows = rest.shape
+    width, rows = rest.shape
     codes = book.shape[0]
     vmem = pl.BlockSpec(memory_space=pltpu.VMEM)
     return pl.pallas_call(
         errors_kernel,
-        in_specs=[vmem, vmem, pl.BlockSpec(memory_space=pl.ANY)],
+        in_specs=[vmem] * 3,
         out_specs=vmem,
         out_shape=jax.ShapeDtypeStruct((copies, rows // LANES, LANES), jnp.float32),
         scratch_shapes=[
             pltpu.VMEM((width, codes), jnp.float32),
             pltpu.VMEM((EPAIRS, LANES, codes), jnp.bfloat16),
-            pltpu.VMEM((width, rows), jnp.float32),
-            pltpu.SemaphoreType.DMA((4,)),
         ],
-        compiler_params=pltpu.CompilerParams(vmem_limit_bytes=40 * 2**20),
+        compiler_params=pltpu.CompilerParams(vmem_limit_bytes=24 * 2**20),
         name="errors",
     )(book, codes_t, rest)
 

time: 109 us -> 106 us (0.972)
  Pallas kernels: 25.5 us -> 23.1 us
    pallas_call x1, Pallas kernels: 11.4 us -> 9.77 us  [residuals(): pl.pallas_call(resid_kernel, in_specs=[pl.BlockSpec(memory_space=pltpu.SM...]
where the time goes in v5:
time: 106 us; the launch traced here: 105 us
  blocking collectives  75.3 us (71%)
  Pallas kernels  23.1 us (22%)
  waiting for transfers between devices  5.35 us (5%)
    all_to_all x1, blocking collectives, local(): lax.all_to_all(pair, 'row', 0, 0, axis_index_groups=same_core, tiled=True)  22 us
    all_to_all x1, blocking collectives, local(): lax.all_to_all(copies, 'row', 0, 0, axis_index_groups=same_core, tiled=True)  18.1 us
    all_to_all x1, blocking collectives, local(): err = lax.all_to_all(err, 'col', 0, 0, tiled=True)  16.4 us
    pallas_call x1, Pallas kernels, residuals(): pl.pallas_call(resid_kernel, in_specs=[pl.BlockSpec(memory_space=pltpu.SM...  9.77 us
    all_to_all x1, blocking collectives, local(): parts = lax.all_to_all(sums, 'row', 0, 0, tiled=True)  9.76 us
    all_to_all x1, blocking collectives, local(): book = lax.all_to_all(copies, 'row', 0, 0, tiled=True).reshape(codes, width)  9.02 us
    pallas_call x1, Pallas kernels, list_sums(): pl.pallas_call(sums_kernel, in_specs=[pl.BlockSpec(memory_space=pltpu.SME...  8.57 us
    ppermute x2, waiting for transfers between devices, swap(): return lax.ppermute(x, axis, [(i, i ^ bit) for i in range(n)])  5.35 us
  transfers between devices with their start and end apart: 2, of which 2 were waited for; matrix products, arithmetic and copies ran while one was open for 0% of the time, Pallas kernels for 0%

profile of v5, /device:TPU:0, one launch (start us, length us, event | category | flops | bytes accessed | tf_op | source)
XLA Modules:
  0.0 105.3 jit_solution(11136338683604696521)
XLA Ops:
  0.6 8.6 %list_sums.1 = (f32[8,264,128]{2,1,0:T(8,128)S(1)}, f32[8,264,128]{2,1,0:T(8,128)S(1)}) custom-call(s32[1]{0:T(128)} %bitcast.core_ref, s32[8192]{0:T(1024)} %ids_ref.1, s32[64,128]{1,0:T(8,128)} %bitcast.9, f32[8192,128]{1,0:T(8,128)} %x_ref.1), custom_call_target="tpu_custom_call" | custom-call | tf_op jit(solution)/shard_map/list_sums/pallas_call | solution.py:115
  9.2 0.1 collective-permute-start
  9.3 2.7 %collective-permute-done = f32[8,264,128]{2,1,0:T(8,128)S(1)} collective-permute-done((f32[8,264,128]{2,1,0:T(8,128)S(1)}, f32[8,264,128]{2,1,0:T(8,128)S(1)}, u32[]{:S(2)}, u32[]{:S(2)}) %collective-permute-start) | collective-permute-done | bytes 1081376 | tf_op jit(solution)/shard_map/ppermute | solution.py:404
  12.0 0.0 copy-start.3
  12.0 0.1 add.8
  12.1 0.0 copy-start
  12.1 22.0 %all_to_all.25.part_ref = f32[8,264,128]{2,1,0:T(8,128)S(1)} all-to-all(f32[8,264,128]{2,1,0:T(8,128)S(1)} %add.8), channel_id=1, replica_groups={{0,16,32,48,64,80,96,112},{8,24,40,56,72,88,104,120},{1,17,33,49,65,81,..., dimensions={0} | all-to-all | bytes 2162688 | tf_op jit(solution)/shard_map/all_to_all | solution.py:425
  34.2 0.0 copy-done.3
  34.2 0.8 centroids.1
  35.0 0.0 copy-start.1
  35.0 0.0 copy-start.2
  35.0 18.1 %all_to_all.26.own_ref = f32[8,256,128]{2,1,0:T(8,128)S(1)} all-to-all(f32[8,256,128]{2,1,0:T(8,128)S(1)} %get-tuple-element.14), channel_id=1, replica_groups={{0,16,32,48,64,80,96,112},{8,24,40,56,72,88,104,120},{1,17,33,49,65,81,..., dimensions={0} | all-to-all | bytes 2097152 | tf_op jit(solution)/shard_map/all_to_all | solution.py:427
  53.1 0.0 collective-permute-start.1
  53.1 2.7 %collective-permute-done.1.other_ref = f32[8,256,128]{2,1,0:T(8,128)S(1)} collective-permute-done((f32[8,256,128]{2,1,0:T(8,128)S(1)}, f32[8,256,128]{2,1,0:T(8,128)S(1)}, u32[]{:S(2)}, u32[]{:S(2)}) %collective-permute-start.1) | collective-permute-done | bytes 1048608 | tf_op jit(solution)/shard_map/ppermute | solution.py:404
  55.7 0.0 copy-done
  55.8 0.0 copy-done.1
  55.8 0.0 copy-done.2
  55.8 0.0 copy-start.4
  55.8 9.8 %residuals.1 = (f32[128,8192]{1,0:T(8,128)S(1)}, f32[16,24,128]{2,1,0:T(8,128)S(1)}) custom-call(s32[1]{0:T(128)} %bitcast.core_ref, s32[8192]{0:T(1024)S(1)} %copy-done.2, s32[8,8192]{1,0:T(8,128)S(1)} %bitcast.6, f32[8192,128]{1,0:T(8,128)S(1)} %copy-done, f32[8,256,128]{2,1,0:T(8,128)S(1)} %all_to_all.26.own_ref, ...), custom_call_target="tpu_custom_call" | custom-call | tf_op jit(solution)/shard_map/residuals/pallas_call | solution.py:267
  65.5 9.8 %all_to_all.27.part_ref = f32[16,24,128]{2,1,0:T(8,128)S(1)} all-to-all(f32[16,24,128]{2,1,0:T(8,128)S(1)} %get-tuple-element.15), channel_id=1, replica_groups=mesh['row'=16,'col'=8] {'row'}, dimensions={0} | all-to-all | bytes 393216 | tf_op jit(solution)/shard_map/all_to_all | solution.py:430
  75.3 0.0 copy-done.4
  75.3 0.8 codebook.1
  76.1 9.0 %all_to_all.28 = f32[16,16,128]{2,1,0:T(8,128)S(1)} all-to-all(f32[16,16,128]{2,1,0:T(8,128)S(1)} %get-tuple-element.17), channel_id=1, replica_groups=mesh['row'=16,'col'=8] {'row'}, dimensions={0} | all-to-all | bytes 262144 | tf_op jit(solution)/shard_map/all_to_all | solution.py:432
  85.1 3.1 %errors.1 = f32[8,64,128]{2,1,0:T(8,128)S(1)} custom-call(f32[256,128]{1,0:T(8,128)S(1)} %bitcast.8, s32[8,8192]{1,0:T(8,128)S(1)} %bitcast.7, f32[128,8192]{1,0:T(8,128)S(1)} %get-tuple-element.18.rest_ref), custom_call_target="tpu_custom_call" | custom-call | tf_op jit(solution)/shard_map/errors/pallas_call | solution.py:358
  88.2 16.4 %all_to_all.29 = f32[8,64,128]{2,1,0:T(8,128)S(1)} all-to-all(f32[8,64,128]{2,1,0:T(8,128)S(1)} %errors.1), channel_id=1, replica_groups=mesh['row'=16,'col'=8] {'col'}, dimensions={0} | all-to-all | bytes 524288 | tf_op jit(solution)/shard_map/all_to_all | solution.py:434
  104.7 0.6 multiply_bitcast_fusion
  (1 shorter events, 0.0 us)
Async XLA Ops:
  9.2 2.8 %collective-permute-start = (f32[8,264,128]{2,1,0:T(8,128)S(1)}, f32[8,264,128]{2,1,0:T(8,128)S(1)}, u32[]{:S(2)}, u32[]{:S(2)}) collective-permute-start(f32[8,264,128]{2,1,0:T(8,128)S(1)} %get-tuple-element.12), channel_id=1, source_target_pairs={{0,8},{8,0},{16,24},{24,16},{32,40},{40,32},{48,56},{56,48},{64,72... | collective-permute-start | bytes 3244040 | tf_op jit(solution)/shard_map/ppermute | solution.py:404
  12.0 22.2 %copy-start.3 = (f32[256,128]{1,0:T(8,128)S(1)}, f32[256,128]{1,0:T(8,128)}, u32[]{:S(2)}) copy-start(f32[256,128]{1,0:T(8,128)} %old_ref.2) | copy-start | bytes 393220
  12.1 43.6 %copy-start = (f32[8192,128]{1,0:T(8,128)S(1)}, f32[8192,128]{1,0:T(8,128)}, u32[]{:S(2)}) copy-start(f32[8192,128]{1,0:T(8,128)} %x_ref.1) | copy-start | bytes 12582916
  35.0 20.8 %copy-start.1 = (s32[8192,8]{0,1:T(8,128)S(1)}, s32[8192,8]{0,1:T(8,128)}, u32[]{:S(2)}) copy-start(s32[8192,8]{0,1:T(8,128)} %param.7) | copy-start | bytes 786436
  35.0 20.8 %copy-start.2 = (s32[8192]{0:T(1024)S(1)}, s32[8192]{0:T(1024)}, u32[]{:S(2)}) copy-start(s32[8192]{0:T(1024)} %ids_ref.1) | copy-start | bytes 98308
  53.1 2.7 %collective-permute-start.1 = (f32[8,256,128]{2,1,0:T(8,128)S(1)}, f32[8,256,128]{2,1,0:T(8,128)S(1)}, u32[]{:S(2)}, u32[]{:S(2)}) collective-permute-start(f32[8,256,128]{2,1,0:T(8,128)S(1)} %all_to_all.26.own_ref), channel_id=1, source_target_pairs={{0,8},{8,0},{16,24},{24,16},{32,40},{40,32},{48,56},{56,48},{64,72... | collective-permute-start | bytes 3145736 | tf_op jit(solution)/shard_map/ppermute | solution.py:404
  55.8 19.5 %copy-start.4 = (f32[16,128]{1,0:T(8,128)S(1)}, f32[16,128]{1,0:T(8,128)}, u32[]{:S(2)}) copy-start(f32[16,128]{1,0:T(8,128)} %old_ref.3) | copy-start | bytes 24580

commit v6 on v5

--- a/solution.py
+++ b/solution.py
@@ -14,7 +14,8 @@
 NACC = 8
 SLAB = 8
 K1LIM = 50 * 2**20
-RBLOCK = 1024
+RBLOCK = 256
+UNROLL = 8
 EBLOCK = 512
 EPAIRS = 2
 VLIM = 24 * 2**20
@@ -130,6 +131,41 @@
     )(core, ids, idv, x)
 
 
+def code_counts_kernel(codes_ref, out_ref):
+    subs, rows = codes_ref.shape
+    digit = lax.broadcasted_iota(jnp.int32, (SUB_DIM, CBLOCK), 0)
+    cc = jnp.zeros((LANES, LANES), jnp.float32)
+    for b in range(0, rows, CBLOCK):
+        left, right = [], []
+        for m in range(subs):
+            code = codes_ref[m : m + 1, b : b + CBLOCK]
+            left.append((lax.shift_right_logical(code, 4) == digit).astype(jnp.bfloat16))
+            right.append(((code & (SUB_DIM - 1)) == digit).astype(jnp.bfloat16))
+        cc += lax.dot_general(
+            jnp.concatenate(left, 0), jnp.concatenate(right, 0), NT, preferred_element_type=jnp.float32
+        )
+    r = lax.broadcasted_iota(jnp.int32, cc.shape, 0) // SUB_DIM
+    c = lax.broadcasted_iota(jnp.int32, cc.shape, 1) // SUB_DIM
+    cc = jnp.where(r == c, cc, 0.0)
+    total = cc[0:SUB_DIM, :]
+    for m in range(1, subs):
+        total = total + cc[m * SUB_DIM : (m + 1) * SUB_DIM, :]
+    out_ref[...] = total
+
+
+def code_counts(codes_t):
+    vmem = pl.BlockSpec(memory_space=pltpu.VMEM)
+    return pl.pallas_call(
+        code_counts_kernel,
+        in_specs=[vmem],
+        out_specs=vmem,
+        out_shape=jax.ShapeDtypeStruct((SUB_DIM, LANES), jnp.float32),
+        compiler_params=pltpu.CompilerParams(vmem_limit_bytes=8 * 2**20),
+        cost_estimate=pl.CostEstimate(flops=10**9, bytes_accessed=4 * 10**6, transcendentals=0),
+        name="code_counts",
+    )(codes_t)
+
+
 def centroid_kernel(prior, part_ref, old_ref, cent_ref, copies_ref):
     owned = old_ref.shape[0]
     total = part_ref[0]
@@ -166,7 +202,7 @@
 
 
 def resid_kernel(
-    core_ref, ids_ref, codes_ref, x_ref, own_ref, other_ref, rest_ref, sums_ref, ids, table, got0, got1, sumst, ccnt, sems
+    core_ref, ids_ref, codes_ref, x_ref, own_ref, other_ref, counts_ref, rest_ref, sums_ref, ids, table, got0, got1, sumst, sems
 ):
     block = got0.shape[0]
     rows = x_ref.shape[0]
@@ -184,7 +220,6 @@
         table[pl.ds(pl.multiple_of((2 * k + core) * owned, owned), owned), :] = own_ref[k]
         table[pl.ds(pl.multiple_of((2 * k + 1 - core) * owned, owned), owned), :] = other_ref[k]
     sumst[...] = jnp.zeros_like(sumst)
-    ccnt[...] = jnp.zeros_like(ccnt)
     fetch[0].wait()
 
     sublane = lax.broadcasted_iota(jnp.int32, (8, LANES), 0)
@@ -205,15 +240,6 @@
         hi = rest.astype(jnp.bfloat16)
         lo = (rest - hi.astype(jnp.float32)).astype(jnp.bfloat16)
         label = lax.broadcasted_iota(jnp.int32, (half, block), 0)
-        digit = lax.broadcasted_iota(jnp.int32, (SUB_DIM, block), 0)
-        left, right = [], []
-        for m in range(subs):
-            code = codes_ref[pl.ds(m, 1), here]
-            left.append((lax.shift_right_logical(code, 4) == digit).astype(jnp.bfloat16))
-            right.append(((code & (SUB_DIM - 1)) == digit).astype(jnp.bfloat16))
-        ccnt[...] += lax.dot_general(
-            jnp.concatenate(left, 0), jnp.concatenate(right, 0), NT, preferred_element_type=jnp.float32
-        )
         for p in range(subs // 2):
             left, right = [], []
             for m in (2 * p, 2 * p + 1):
@@ -236,37 +262,29 @@
     gather(0, got0)
     fetch[1].wait()
 
-    @pl.loop(0, rows // (2 * block))
+    @pl.loop(0, rows // (UNROLL * block))
     def _(i):
-        first = pl.multiple_of(2 * i * block, block)
-        second = pl.multiple_of(first + block, block)
-        third = pl.multiple_of(jnp.minimum(second + block, rows - block), block)
-        gather(second, got1)
-        work(first, got0)
-        gather(third, got0)
-        work(second, got1)
+        base = pl.multiple_of(i * UNROLL * block, block)
+        for u in range(UNROLL):
+            now, after = (got0, got1) if u % 2 == 0 else (got1, got0)
+            here = pl.multiple_of(base + u * block, block)
+            gather(pl.multiple_of(jnp.minimum(here + block, rows - block), block), after)
+            work(here, now)
 
     total = sumst[...].T
-    cc = ccnt[...]
-    r = lax.broadcasted_iota(jnp.int32, cc.shape, 0) // SUB_DIM
-    c = lax.broadcasted_iota(jnp.int32, cc.shape, 1) // SUB_DIM
-    cc = jnp.where(r == c, cc, 0.0)
-    crow = cc[0:SUB_DIM, :]
-    for m in range(1, subs):
-        crow = crow + cc[m * SUB_DIM : (m + 1) * SUB_DIM, :]
     fill = jnp.zeros((SLAB - 1, LANES), jnp.float32)
     for o in range(owners):
         sums_ref[o, 0:each, :] = total[o * each : (o + 1) * each, :]
-        sums_ref[o, each:slab, :] = jnp.concatenate([crow[o : o + 1, :], fill], 0)
-
-
-def residuals(core, ids, codes_t, x, own, other, owners, codes, block=RBLOCK):
+        sums_ref[o, each:slab, :] = jnp.concatenate([counts_ref[o : o + 1, :], fill], 0)
+
+
+def residuals(core, ids, codes_t, x, own, other, counts, owners, codes, block=RBLOCK):
     rows, width = x.shape
     pieces, owned, _ = own.shape
     vmem = pl.BlockSpec(memory_space=pltpu.VMEM)
     return pl.pallas_call(
         resid_kernel,
-        in_specs=[pl.BlockSpec(memory_space=pltpu.SMEM)] + [vmem] * 5,
+        in_specs=[pl.BlockSpec(memory_space=pltpu.SMEM)] + [vmem] * 6,
         out_specs=[vmem, vmem],
         out_shape=[
             jax.ShapeDtypeStruct((width, rows), jnp.float32),
@@ -278,12 +296,11 @@
             pltpu.VMEM((block, width), jnp.float32),
             pltpu.VMEM((block, width), jnp.float32),
             pltpu.VMEM((width, codes), jnp.float32),
-            pltpu.VMEM((LANES, LANES), jnp.float32),
             pltpu.SemaphoreType.DMA((2,)),
         ],
         compiler_params=pltpu.CompilerParams(vmem_limit_bytes=VLIM),
         name="residuals",
-    )(core, ids, codes_t, x, own, other)
+    )(core, ids, codes_t, x, own, other, counts)
 
 
 def book_bands(book_t, pair):
@@ -426,7 +443,7 @@
     centroids, copies = new_centroids(parts, old_centroids, list_prior)
     own = lax.all_to_all(copies, "row", 0, 0, axis_index_groups=same_core, tiled=True)
     other = swap(own, "row", n_row, 1)
-    rest, sums = residuals(core, list_ids, codes_t, passages, own, other, n_row, codes)
+    rest, sums = residuals(core, list_ids, codes_t, passages, own, other, code_counts(codes_t), n_row, codes)
     parts = lax.all_to_all(sums, "row", 0, 0, tiled=True)
     codebook, copies = new_codebook(parts, old_codebook, code_prior)
     book = lax.all_to_all(copies, "row", 0, 0, tiled=True).reshape(codes, width)

time: 106 us -> 105 us (level)
  transfers between devices with their start and end apart: 2 -> 2, of which waited for: 2 -> 2; matrix products, arithmetic and copies ran while one was open for 0% -> 0% of each run, Pallas kernels for 0% -> 1%
where the time goes in v6:
time: 105 us; the launch traced here: 104 us
  blocking collectives  75.3 us (72%)
  Pallas kernels  23 us (22%)
  waiting for transfers between devices  4.39 us (4%)
    all_to_all x1, blocking collectives, local(): lax.all_to_all(pair, 'row', 0, 0, axis_index_groups=same_core, tiled=True)  21.9 us
    all_to_all x1, blocking collectives, local(): lax.all_to_all(copies, 'row', 0, 0, axis_index_groups=same_core, tiled=True)  18.2 us
    all_to_all x1, blocking collectives, local(): err = lax.all_to_all(err, 'col', 0, 0, tiled=True)  16.4 us
    all_to_all x1, blocking collectives, local(): parts = lax.all_to_all(sums, 'row', 0, 0, tiled=True)  9.72 us
    all_to_all x1, blocking collectives, local(): book = lax.all_to_all(copies, 'row', 0, 0, tiled=True).reshape(codes, width)  9.02 us
    pallas_call x1, Pallas kernels, residuals(): pl.pallas_call(resid_kernel, in_specs=[pl.BlockSpec(memory_space=pltpu.SM...  8.74 us
    pallas_call x1, Pallas kernels, list_sums(): pl.pallas_call(sums_kernel, in_specs=[pl.BlockSpec(memory_space=pltpu.SME...  8.58 us
    ppermute x2, waiting for transfers between devices, swap(): return lax.ppermute(x, axis, [(i, i ^ bit) for i in range(n)])  4.39 us
  transfers between devices with their start and end apart: 2, of which 2 were waited for; matrix products, arithmetic and copies ran while one was open for 0% of the time, Pallas kernels for 1%

profile of v6, /device:TPU:0, one launch (start us, length us, event | category | flops | bytes accessed | tf_op | source)
XLA Modules:
  0.0 104.2 jit_solution(12344276156540281097)
XLA Ops:
  0.6 8.6 %list_sums.1 = (f32[8,264,128]{2,1,0:T(8,128)S(1)}, f32[8,264,128]{2,1,0:T(8,128)S(1)}) custom-call(s32[1]{0:T(128)} %bitcast.core_ref, s32[8192]{0:T(1024)} %ids_ref.1, s32[64,128]{1,0:T(8,128)} %bitcast.10, f32[8192,128]{1,0:T(8,128)} %x_ref.1), custom_call_target="tpu_custom_call" | custom-call | tf_op jit(solution)/shard_map/list_sums/pallas_call | solution.py:116
  9.2 0.1 collective-permute-start
  9.3 2.7 %collective-permute-done = f32[8,264,128]{2,1,0:T(8,128)S(1)} collective-permute-done((f32[8,264,128]{2,1,0:T(8,128)S(1)}, f32[8,264,128]{2,1,0:T(8,128)S(1)}, u32[]{:S(2)}, u32[]{:S(2)}) %collective-permute-start) | collective-permute-done | bytes 1081376 | tf_op jit(solution)/shard_map/ppermute | solution.py:421
  12.0 0.1 add.8
  12.1 0.0 copy-start.3
  12.1 21.9 %all_to_all.25.part_ref = f32[8,264,128]{2,1,0:T(8,128)S(1)} all-to-all(f32[8,264,128]{2,1,0:T(8,128)S(1)} %add.8), channel_id=1, replica_groups={{0,16,32,48,64,80,96,112},{8,24,40,56,72,88,104,120},{1,17,33,49,65,81,..., dimensions={0} | all-to-all | bytes 2162688 | tf_op jit(solution)/shard_map/all_to_all | solution.py:442
  34.0 0.0 copy-done.3
  34.0 0.8 centroids.1
  34.9 0.0 copy-start.1
  34.9 0.0 copy-start
  34.9 18.2 %all_to_all.26.own_ref = f32[8,256,128]{2,1,0:T(8,128)S(1)} all-to-all(f32[8,256,128]{2,1,0:T(8,128)S(1)} %get-tuple-element.14), channel_id=1, replica_groups={{0,16,32,48,64,80,96,112},{8,24,40,56,72,88,104,120},{1,17,33,49,65,81,..., dimensions={0} | all-to-all | bytes 2097152 | tf_op jit(solution)/shard_map/all_to_all | solution.py:444
  53.1 0.0 collective-permute-start.1
  53.1 0.0 copy-done.1
  53.1 0.0 copy-start.2
  53.1 0.9 code_counts.1.counts_ref
  54.0 0.0 copy-start.4
  54.0 1.7 %collective-permute-done.1.other_ref = f32[8,256,128]{2,1,0:T(8,128)S(1)} collective-permute-done((f32[8,256,128]{2,1,0:T(8,128)S(1)}, f32[8,256,128]{2,1,0:T(8,128)S(1)}, u32[]{:S(2)}, u32[]{:S(2)}) %collective-permute-start.1) | collective-permute-done | bytes 1048608 | tf_op jit(solution)/shard_map/ppermute | solution.py:421
  55.7 0.0 copy-done
  55.7 0.0 copy-done.2
  55.8 8.7 %residuals.1 = (f32[128,8192]{1,0:T(8,128)S(1)}, f32[16,24,128]{2,1,0:T(8,128)S(1)}) custom-call(s32[1]{0:T(128)} %bitcast.core_ref, s32[8192]{0:T(1024)S(1)} %copy-done.2, s32[8,8192]{1,0:T(8,128)S(1)} %bitcast.7, f32[8192,128]{1,0:T(8,128)S(1)} %copy-done, f32[8,256,128]{2,1,0:T(8,128)S(1)} %all_to_all.26.own_ref, ...), custom_call_target="tpu_custom_call" | custom-call | tf_op jit(solution)/shard_map/residuals/pallas_call | solution.py:285
  64.5 9.7 %all_to_all.27.part_ref = f32[16,24,128]{2,1,0:T(8,128)S(1)} all-to-all(f32[16,24,128]{2,1,0:T(8,128)S(1)} %get-tuple-element.15), channel_id=1, replica_groups=mesh['row'=16,'col'=8] {'row'}, dimensions={0} | all-to-all | bytes 393216 | tf_op jit(solution)/shard_map/all_to_all | solution.py:447
  74.2 0.0 copy-done.4
  74.2 0.8 codebook.1
  75.0 9.0 %all_to_all.28 = f32[16,16,128]{2,1,0:T(8,128)S(1)} all-to-all(f32[16,16,128]{2,1,0:T(8,128)S(1)} %get-tuple-element.17), channel_id=1, replica_groups=mesh['row'=16,'col'=8] {'row'}, dimensions={0} | all-to-all | bytes 262144 | tf_op jit(solution)/shard_map/all_to_all | solution.py:449
  84.0 3.1 %errors.1 = f32[8,64,128]{2,1,0:T(8,128)S(1)} custom-call(f32[256,128]{1,0:T(8,128)S(1)} %bitcast.9, s32[8,8192]{1,0:T(8,128)S(1)} %bitcast.8, f32[128,8192]{1,0:T(8,128)S(1)} %get-tuple-element.18.rest_ref), custom_call_target="tpu_custom_call" | custom-call | tf_op jit(solution)/shard_map/errors/pallas_call | solution.py:375
  87.2 16.4 %all_to_all.29 = f32[8,64,128]{2,1,0:T(8,128)S(1)} all-to-all(f32[8,64,128]{2,1,0:T(8,128)S(1)} %errors.1), channel_id=1, replica_groups=mesh['row'=16,'col'=8] {'col'}, dimensions={0} | all-to-all | bytes 524288 | tf_op jit(solution)/shard_map/all_to_all | solution.py:451
  103.6 0.6 multiply_bitcast_fusion
  (1 shorter events, 0.0 us)
Async XLA Ops:
  9.2 2.8 %collective-permute-start = (f32[8,264,128]{2,1,0:T(8,128)S(1)}, f32[8,264,128]{2,1,0:T(8,128)S(1)}, u32[]{:S(2)}, u32[]{:S(2)}) collective-permute-start(f32[8,264,128]{2,1,0:T(8,128)S(1)} %get-tuple-element.12), channel_id=1, source_target_pairs={{0,8},{8,0},{16,24},{24,16},{32,40},{40,32},{48,56},{56,48},{64,72... | collective-permute-start | bytes 3244040 | tf_op jit(solution)/shard_map/ppermute | solution.py:421
  12.1 21.9 %copy-start.3 = (f32[256,128]{1,0:T(8,128)S(1)}, f32[256,128]{1,0:T(8,128)}, u32[]{:S(2)}) copy-start(f32[256,128]{1,0:T(8,128)} %old_ref.2) | copy-start | bytes 393220
  34.9 18.2 %copy-start.1 = (s32[8192,8]{0,1:T(8,128)S(1)}, s32[8192,8]{0,1:T(8,128)}, u32[]{:S(2)}) copy-start(s32[8192,8]{0,1:T(8,128)} %param.7) | copy-start | bytes 786436
  34.9 20.9 %copy-start = (f32[8192,128]{1,0:T(8,128)S(1)}, f32[8192,128]{1,0:T(8,128)}, u32[]{:S(2)}) copy-start(f32[8192,128]{1,0:T(8,128)} %x_ref.1) | copy-start | bytes 12582916
  53.1 2.7 %collective-permute-start.1 = (f32[8,256,128]{2,1,0:T(8,128)S(1)}, f32[8,256,128]{2,1,0:T(8,128)S(1)}, u32[]{:S(2)}, u32[]{:S(2)}) collective-permute-start(f32[8,256,128]{2,1,0:T(8,128)S(1)} %all_to_all.26.own_ref), channel_id=1, source_target_pairs={{0,8},{8,0},{16,24},{24,16},{32,40},{40,32},{48,56},{56,48},{64,72... | collective-permute-start | bytes 3145736 | tf_op jit(solution)/shard_map/ppermute | solution.py:421
  53.1 2.7 %copy-start.2 = (s32[8192]{0:T(1024)S(1)}, s32[8192]{0:T(1024)}, u32[]{:S(2)}) copy-start(s32[8192]{0:T(1024)} %ids_ref.1) | copy-start | bytes 98308
  54.0 20.2 %copy-start.4 = (f32[16,128]{1,0:T(8,128)S(1)}, f32[16,128]{1,0:T(8,128)}, u32[]{:S(2)}) copy-start(f32[16,128]{1,0:T(8,128)} %old_ref.3) | copy-start | bytes 24580

commit v7 on v6

--- a/solution.py
+++ b/solution.py
@@ -7,7 +7,6 @@
 
 from jax.sharding import PartitionSpec as P
 
-HIGH = lax.Precision.HIGHEST
 D = 1024
 LANES = 128
 SUB_DIM = 16
@@ -202,14 +201,14 @@
 
 
 def resid_kernel(
-    core_ref, ids_ref, codes_ref, x_ref, own_ref, other_ref, counts_ref, rest_ref, sums_ref, ids, table, got0, got1, sumst, sems
+    core_ref, row_ref, ids_ref, codes_ref, x_ref, own_ref, other_ref, counts_ref, old_ref, rest_ref, keep_ref, send_ref, ids, table, got0, got1, sumst, tall, sems, *, prior
 ):
     block = got0.shape[0]
     rows = x_ref.shape[0]
     pieces, owned, _ = own_ref.shape
     subs = codes_ref.shape[0]
-    owners, slab, _ = sums_ref.shape
-    each = slab - SLAB
+    owners = counts_ref.shape[0]
+    each = old_ref.shape[0]
     half = owners * each // 2
     early, late = pl.ds(0, 2 * block), pl.ds(2 * block, rows - 2 * block)
     fetch = [pltpu.make_async_copy(ids_ref.at[p], ids.at[p], sems.at[n]) for n, p in enumerate((early, late))]
@@ -271,24 +270,30 @@
             gather(pl.multiple_of(jnp.minimum(here + block, rows - block), block), after)
             work(here, now)
 
-    total = sumst[...].T
-    fill = jnp.zeros((SLAB - 1, LANES), jnp.float32)
-    for o in range(owners):
-        sums_ref[o, 0:each, :] = total[o * each : (o + 1) * each, :]
-        sums_ref[o, each:slab, :] = jnp.concatenate([counts_ref[o : o + 1, :], fill], 0)
-
-
-def residuals(core, ids, codes_t, x, own, other, counts, owners, codes, block=RBLOCK):
+    tall[...] = sumst[...].T
+    mine = pl.ds(pl.multiple_of(row_ref[0] * each, each), each)
+    tall[mine, :] += prior * old_ref[...]
+    for out, parity in ((keep_ref, core), (send_ref, 1 - core)):
+        for k in range(owners // 2):
+            o = 2 * k + parity
+            out[k * each : (k + 1) * each, :] = tall[pl.ds(pl.multiple_of(o * each, each), each), :]
+            out[pl.ds(owners // 2 * each + k, 1), :] = counts_ref[pl.ds(o, 1), :]
+
+
+def residuals(core, row, ids, codes_t, x, own, other, counts, old, owners, prior, block=RBLOCK):
+    codes = owners * old.shape[0]
+    half = jax.ShapeDtypeStruct((codes // 2 + owners // 2, x.shape[1]), jnp.float32)
     rows, width = x.shape
     pieces, owned, _ = own.shape
     vmem = pl.BlockSpec(memory_space=pltpu.VMEM)
     return pl.pallas_call(
-        resid_kernel,
-        in_specs=[pl.BlockSpec(memory_space=pltpu.SMEM)] + [vmem] * 6,
-        out_specs=[vmem, vmem],
+        functools.partial(resid_kernel, prior=prior),
+        in_specs=[pl.BlockSpec(memory_space=pltpu.SMEM)] * 2 + [vmem] * 7,
+        out_specs=[vmem] * 3,
         out_shape=[
             jax.ShapeDtypeStruct((width, rows), jnp.float32),
-            jax.ShapeDtypeStruct((owners, codes // owners + SLAB, width), jnp.float32),
+            half,
+            half,
         ],
         scratch_shapes=[
             pltpu.SMEM((rows,), jnp.int32),
@@ -296,11 +301,12 @@
             pltpu.VMEM((block, width), jnp.float32),
             pltpu.VMEM((block, width), jnp.float32),
             pltpu.VMEM((width, codes), jnp.float32),
+            pltpu.VMEM((codes, width), jnp.float32),
             pltpu.SemaphoreType.DMA((2,)),
         ],
         compiler_params=pltpu.CompilerParams(vmem_limit_bytes=VLIM),
         name="residuals",
-    )(core, ids, codes_t, x, own, other, counts)
+    )(core, row, ids, codes_t, x, own, other, counts, old)
 
 
 def book_bands(book_t, pair):
@@ -317,9 +323,39 @@
     return jnp.concatenate(bands, 0)
 
 
-def errors_kernel(book_ref, codes_ref, rest_ref, out_ref, table, bands):
+def whole_book(prior, core_ref, own_ref, other_ref, each, book_ref, counts_ref):
+    owners = book_ref.shape[0] // each
+    core = core_ref[0]
+    for src, parity in ((own_ref, core), (other_ref, 1 - core)):
+        for k in range(owners // 2):
+            o = 2 * k + parity
+            book_ref[pl.ds(pl.multiple_of(o * each, each), each), :] = src[k * each : (k + 1) * each, :]
+            counts_ref[pl.ds(o, 1), :] = src[pl.ds(owners // 2 * each + k, 1), :]
+    lane = lax.broadcasted_iota(jnp.int32, (each, LANES), 1)
+    code = lax.broadcasted_iota(jnp.int32, (each, LANES), 0)
+    keep = (lane & (SUB_DIM - 1)) == code
+    whole = counts_ref[...].astype(jnp.int32)
+    digits = [lax.shift_right_logical(whole, 12), lax.shift_right_logical(whole, 6) & 63, whole & 63]
+    picked = jnp.concatenate(
+        [
+            jnp.concatenate([jnp.where(keep, d[o : o + 1, :], 0) for o in range(owners)], 0).astype(jnp.bfloat16)
+            for d in digits
+        ],
+        1,
+    )
+    r = lax.broadcasted_iota(jnp.int32, (LANES, LANES), 0) // SUB_DIM
+    c = lax.broadcasted_iota(jnp.int32, (LANES, LANES), 1) // SUB_DIM
+    ones = jnp.concatenate([jnp.where(r == c, w, 0.0).astype(jnp.bfloat16) for w in (4096.0, 64.0, 1.0)], 0)
+    spread = jnp.dot(picked, ones, preferred_element_type=jnp.float32)
+    book_ref[...] = book_ref[...] / (spread + prior)
+
+
+def errors_kernel(core_ref, row_ref, own_ref, other_ref, codes_ref, rest_ref, out_ref, mine_ref, table, bands, book_ref, counts_ref, *, prior):
     subs, rows = codes_ref.shape
     half = book_ref.shape[0] // 2
+    each = mine_ref.shape[0]
+    whole_book(prior, core_ref, own_ref, other_ref, each, book_ref, counts_ref)
+    mine_ref[...] = book_ref[pl.ds(pl.multiple_of(row_ref[0] * each, each), each), :]
     by_product = bands.shape[0]
     looked_up = subs - 2 * by_product
 
@@ -368,53 +404,27 @@
                 out_ref[k, at : at + 1, :] = row
 
 
-def errors(book, codes_t, rest, copies):
+def errors(core, row, own, other, codes_t, rest, copies, owned, owners, prior):
     width, rows = rest.shape
-    codes = book.shape[0]
+    codes = owned * owners
     vmem = pl.BlockSpec(memory_space=pltpu.VMEM)
     return pl.pallas_call(
-        errors_kernel,
-        in_specs=[vmem] * 3,
-        out_specs=vmem,
-        out_shape=jax.ShapeDtypeStruct((copies, rows // LANES, LANES), jnp.float32),
+        functools.partial(errors_kernel, prior=prior),
+        in_specs=[pl.BlockSpec(memory_space=pltpu.SMEM)] * 2 + [vmem] * 4,
+        out_specs=[vmem] * 2,
+        out_shape=[
+            jax.ShapeDtypeStruct((copies, rows // LANES, LANES), jnp.float32),
+            jax.ShapeDtypeStruct((owned, width), jnp.float32),
+        ],
         scratch_shapes=[
             pltpu.VMEM((width, codes), jnp.float32),
             pltpu.VMEM((EPAIRS, LANES, codes), jnp.bfloat16),
+            pltpu.VMEM((codes, width), jnp.float32),
+            pltpu.VMEM((owners, width), jnp.float32),
         ],
         compiler_params=pltpu.CompilerParams(vmem_limit_bytes=24 * 2**20),
         name="errors",
-    )(book, codes_t, rest)
-
-
-def book_kernel(prior, part_ref, old_ref, book_ref, copies_ref):
-    total = part_ref[0]
-    for k in range(1, part_ref.shape[0]):
-        total = total + part_ref[k]
-    shape = old_ref.shape
-    row = jnp.broadcast_to(total[shape[0] : shape[0] + 1, :], shape)
-    lane = lax.broadcasted_iota(jnp.int32, shape, 1)
-    code = lax.broadcasted_iota(jnp.int32, shape, 0)
-    picked = jnp.where(lane % SUB_DIM == code, row, 0.0)
-    r = lax.broadcasted_iota(jnp.int32, (LANES, LANES), 0) // SUB_DIM
-    c = lax.broadcasted_iota(jnp.int32, (LANES, LANES), 1) // SUB_DIM
-    ones = (r == c).astype(jnp.float32)
-    counts = jnp.dot(picked, ones, precision=HIGH, preferred_element_type=jnp.float32)
-    book = (total[: shape[0], :] + prior * old_ref[...]) / (counts + prior)
-    book_ref[...] = book
-    for k in range(copies_ref.shape[0]):
-        copies_ref[k] = book
-
-
-def new_codebook(parts, old, prior):
-    return pl.pallas_call(
-        functools.partial(book_kernel, prior),
-        out_shape=[
-            jax.ShapeDtypeStruct(old.shape, jnp.float32),
-            jax.ShapeDtypeStruct((parts.shape[0],) + old.shape, jnp.float32),
-        ],
-        compiler_params=pltpu.CompilerParams(vmem_limit_bytes=4 * 2**20),
-        name="codebook",
-    )(parts, old)
+    )(core, row, own, other, codes_t, rest)
 
 
 def swap(x, axis, n, bit):
@@ -434,6 +444,7 @@
     code_prior = float(total // codes)
     pieces = n_row // 2
     same_core = [[2 * k + c for k in range(pieces)] for c in range(2)]
+    row = lax.axis_index("row").astype(jnp.int32).reshape(1)
     core = (lax.axis_index("row") % 2).astype(jnp.int32).reshape(1)
     codes_t = code_ids.T
 
@@ -443,11 +454,17 @@
     centroids, copies = new_centroids(parts, old_centroids, list_prior)
     own = lax.all_to_all(copies, "row", 0, 0, axis_index_groups=same_core, tiled=True)
     other = swap(own, "row", n_row, 1)
-    rest, sums = residuals(core, list_ids, codes_t, passages, own, other, code_counts(codes_t), n_row, codes)
-    parts = lax.all_to_all(sums, "row", 0, 0, tiled=True)
-    codebook, copies = new_codebook(parts, old_codebook, code_prior)
-    book = lax.all_to_all(copies, "row", 0, 0, tiled=True).reshape(codes, width)
-    err = errors(book, codes_t, rest, n_col)
+    rest, keep, send = residuals(
+        core, row, list_ids, codes_t, passages, own, other, code_counts(codes_t), old_codebook, n_row, code_prior
+    )
+    half = keep + swap(send, "row", n_row, 1)
+    bit = n_row // 2
+    while bit > 1:
+        half = half + swap(half, "row", n_row, bit)
+        bit //= 2
+    err, codebook = errors(
+        core, row, half, swap(half, "row", n_row, 1), codes_t, rest, n_col, owned_codes, n_row, code_prior
+    )
     err = lax.all_to_all(err, "col", 0, 0, tiled=True)
     return centroids, codebook, jnp.sum(err, axis=0).reshape(rows) / D
 

time: 105 us -> 103 us (0.981)
  blocking collectives: 75.3 us -> 56.6 us
  waiting for transfers between devices: 4.39 us -> 18.7 us
  starting transfers between devices: 0.09 us -> 3.08 us
    all_to_all x2 -> x0, blocking collectives: 18.7 us -> none  [the longest x1 9.72 us: local(): parts = lax.all_to_all(sums, 'row', 0, 0, tiled=True)]
    ppermute x2 -> x7, waiting for transfers between devices: 4.39 us -> 18.7 us  [swap(): return lax.ppermute(x, axis, [(i, i ^ bit) for i in range(n)])]
    ppermute x2 -> x7, starting transfers between devices: 0.09 us -> 3.08 us  [swap(): return lax.ppermute(x, axis, [(i, i ^ bit) for i in range(n)])]
    pallas_call x3 -> x2, Pallas kernels: 12.6 us -> 12.1 us  [the longest x1 8.73 us: residuals(): pl.pallas_call(functools.partial(resid_kernel, prior=prior), in_specs=[pl...]
  transfers between devices with their start and end apart: 2 -> 7, of which waited for: 2 -> 7; matrix products, arithmetic and copies ran while one was open for 0% -> 0% of each run, Pallas kernels for 1% -> 1%
where the time goes in v7:
time: 103 us; the launch traced here: 102 us
  blocking collectives  56.6 us (55%)
  Pallas kernels  22.4 us (22%)
  waiting for transfers between devices  18.7 us (18%)
  starting transfers between devices  3.08 us (3%)
    all_to_all x1, blocking collectives, local(): lax.all_to_all(pair, 'row', 0, 0, axis_index_groups=same_core, tiled=True)  21.9 us
    ppermute x7, waiting for transfers between devices, swap(): return lax.ppermute(x, axis, [(i, i ^ bit) for i in range(n)])  18.7 us
    all_to_all x1, blocking collectives, local(): lax.all_to_all(copies, 'row', 0, 0, axis_index_groups=same_core, tiled=True)  18.2 us
    all_to_all x1, blocking collectives, local(): err = lax.all_to_all(err, 'col', 0, 0, tiled=True)  16.5 us
    pallas_call x1, Pallas kernels, residuals(): pl.pallas_call(functools.partial(resid_kernel, prior=prior), in_specs=[pl...  8.73 us
    pallas_call x1, Pallas kernels, list_sums(): pl.pallas_call(sums_kernel, in_specs=[pl.BlockSpec(memory_space=pltpu.SME...  8.59 us
    pallas_call x1, Pallas kernels, errors(): pl.pallas_call(functools.partial(errors_kernel, prior=prior), in_specs=[p...  3.32 us
    ppermute x7, starting transfers between devices, swap(): return lax.ppermute(x, axis, [(i, i ^ bit) for i in range(n)])  3.08 us
  transfers between devices with their start and end apart: 7, of which 7 were waited for; matrix products, arithmetic and copies ran while one was open for 0% of the time, Pallas kernels for 1%

profile of v7, /device:TPU:0, one launch (start us, length us, event | category | flops | bytes accessed | tf_op | source)
XLA Modules:
  0.0 102.4 jit_solution(5204568812695234077)
XLA Ops:
  0.6 8.6 %list_sums.1 = (f32[8,264,128]{2,1,0:T(8,128)S(1)}, f32[8,264,128]{2,1,0:T(8,128)S(1)}) custom-call(s32[1]{0:T(128)} %bitcast.core_ref, s32[8192]{0:T(1024)} %ids_ref.1, s32[64,128]{1,0:T(8,128)} %bitcast.9, f32[8192,128]{1,0:T(8,128)} %x_ref.1), custom_call_target="tpu_custom_call" | custom-call | tf_op jit(solution)/shard_map/list_sums/pallas_call | solution.py:115
  9.2 0.1 collective-permute-start
  9.3 2.7 %collective-permute-done = f32[8,264,128]{2,1,0:T(8,128)S(1)} collective-permute-done((f32[8,264,128]{2,1,0:T(8,128)S(1)}, f32[8,264,128]{2,1,0:T(8,128)S(1)}, u32[]{:S(2)}, u32[]{:S(2)}) %collective-permute-start) | collective-permute-done | bytes 1081376 | tf_op jit(solution)/shard_map/ppermute | solution.py:431
  12.0 0.1 add.20
  12.1 0.0 copy-start.3
  12.2 21.9 %all_to_all.15.part_ref = f32[8,264,128]{2,1,0:T(8,128)S(1)} all-to-all(f32[8,264,128]{2,1,0:T(8,128)S(1)} %add.20), channel_id=1, replica_groups={{0,16,32,48,64,80,96,112},{8,24,40,56,72,88,104,120},{1,17,33,49,65,81,..., dimensions={0} | all-to-all | bytes 2162688 | tf_op jit(solution)/shard_map/all_to_all | solution.py:453
  34.0 0.0 copy-done.3
  34.0 0.8 centroids.1
  34.9 0.0 copy-start.1
  34.9 0.0 copy-start
  34.9 18.2 %all_to_all.16.own_ref = f32[8,256,128]{2,1,0:T(8,128)S(1)} all-to-all(f32[8,256,128]{2,1,0:T(8,128)S(1)} %get-tuple-element.15), channel_id=1, replica_groups={{0,16,32,48,64,80,96,112},{8,24,40,56,72,88,104,120},{1,17,33,49,65,81,..., dimensions={0} | all-to-all | bytes 2097152 | tf_op jit(solution)/shard_map/all_to_all | solution.py:455
  53.1 0.0 collective-permute-start.1
  53.1 0.0 copy-done.1
  53.1 0.0 copy-start.2
  53.1 0.0 copy-start.4
  53.1 0.9 code_counts.1.counts_ref
  54.1 1.7 %collective-permute-done.1.other_ref = f32[8,256,128]{2,1,0:T(8,128)S(1)} collective-permute-done((f32[8,256,128]{2,1,0:T(8,128)S(1)}, f32[8,256,128]{2,1,0:T(8,128)S(1)}, u32[]{:S(2)}, u32[]{:S(2)}) %collective-permute-start.1) | collective-permute-done | bytes 1048608 | tf_op jit(solution)/shard_map/ppermute | solution.py:431
  55.8 0.0 copy-done
  55.8 0.0 copy-done.2
  55.8 0.0 copy-done.4
  55.8 8.7 %residuals.1 = (f32[128,8192]{1,0:T(8,128)S(1)}, f32[136,128]{1,0:T(8,128)S(1)}, f32[136,128]{1,0:T(8,128)S(1)}) custom-call(s32[1]{0:T(128)} %bitcast.core_ref, s32[1]{0:T(128)} %bitcast.2.row_ref, s32[8192]{0:T(1024)S(1)} %copy-done.2, s32[8,8192]{1,0:T(8,128)S(1)} %bitcast.7, f32[8192,128]{1,0:T(8,128)S(1)} %copy-done, ...), custom_call_target="tpu_custom_call" | custom-call | tf_op jit(solution)/shard_map/residuals/pallas_call | solution.py:289
  64.5 0.2 collective-permute-start.2
  64.7 1.1 %collective-permute-done.2 = f32[136,128]{1,0:T(8,128)S(1)} collective-permute-done((f32[136,128]{1,0:T(8,128)S(1)}, f32[136,128]{1,0:T(8,128)S(1)}, u32[]{:S(2)}, u32[]{:S(2)}) %collective-permute-start.2) | collective-permute-done | bytes 69664 | tf_op jit(solution)/shard_map/ppermute | solution.py:431
  65.9 0.6 collective-permute-start.3
  66.5 3.8 %collective-permute-done.3 = f32[136,128]{1,0:T(8,128)S(1)} collective-permute-done((f32[136,128]{1,0:T(8,128)S(1)}, f32[136,128]{1,0:T(8,128)S(1)}, u32[]{:S(2)}, u32[]{:S(2)}) %collective-permute-start.3) | collective-permute-done | bytes 69664 | tf_op jit(solution)/shard_map/ppermute | solution.py:431
  70.3 1.0 collective-permute-start.4
  71.2 4.9 %collective-permute-done.4 = f32[136,128]{1,0:T(8,128)S(1)} collective-permute-done((f32[136,128]{1,0:T(8,128)S(1)}, f32[136,128]{1,0:T(8,128)S(1)}, u32[]{:S(2)}, u32[]{:S(2)}) %collective-permute-start.4) | collective-permute-done | bytes 69664 | tf_op jit(solution)/shard_map/ppermute | solution.py:431
  76.2 1.1 %collective-permute-start.5 = (f32[136,128]{1,0:T(8,128)S(1)}, f32[136,128]{1,0:T(8,128)S(1)}, u32[]{:S(2)}, u32[]{:S(2)}) collective-permute-start(f32[136,128]{1,0:T(8,128)S(1)} %add.23), channel_id=1, source_target_pairs={{0,16},{8,24},{16,0},{24,8},{32,48},{40,56},{48,32},{56,40},{64,80... | collective-permute-start | bytes 208904 | tf_op jit(solution)/shard_map/ppermute | solution.py:431
  77.3 3.3 %collective-permute-done.5 = f32[136,128]{1,0:T(8,128)S(1)} collective-permute-done((f32[136,128]{1,0:T(8,128)S(1)}, f32[136,128]{1,0:T(8,128)S(1)}, u32[]{:S(2)}, u32[]{:S(2)}) %collective-permute-start.5) | collective-permute-done | bytes 69664 | tf_op jit(solution)/shard_map/ppermute | solution.py:431
  80.6 0.1 collective-permute-start.6
  80.7 1.2 %collective-permute-done.6.other_ref = f32[136,128]{1,0:T(8,128)S(1)} collective-permute-done((f32[136,128]{1,0:T(8,128)S(1)}, f32[136,128]{1,0:T(8,128)S(1)}, u32[]{:S(2)}, u32[]{:S(2)}) %collective-permute-start.6) | collective-permute-done | bytes 69664 | tf_op jit(solution)/shard_map/ppermute | solution.py:431
  81.9 3.3 %errors.1 = (f32[8,64,128]{2,1,0:T(8,128)S(1)}, f32[16,128]{1,0:T(8,128)}) custom-call(s32[1]{0:T(128)} %bitcast.core_ref, s32[1]{0:T(128)} %bitcast.2.row_ref, f32[136,128]{1,0:T(8,128)S(1)} %add.24.own_ref, f32[136,128]{1,0:T(8,128)S(1)} %collective-permute-done.6.other_ref, s32[8,8192]{1,0:T(8,128)S(1)} %bitcast.8, f32[128,8192]{1,0:T(8,128)S(1)} %get-tuple-element.18.rest_ref), custom_call_target="tpu_custom_call" | custom-call | tf_op jit(solution)/shard_map/errors/pallas_call | solution.py:411
  85.2 16.5 %all_to_all.17 = f32[8,64,128]{2,1,0:T(8,128)S(1)} all-to-all(f32[8,64,128]{2,1,0:T(8,128)S(1)} %get-tuple-element.20), channel_id=1, replica_groups=mesh['row'=16,'col'=8] {'col'}, dimensions={0} | all-to-all | bytes 524288 | tf_op jit(solution)/shard_map/all_to_all | solution.py:468
  101.8 0.6 multiply_bitcast_fusion
  (5 shorter events, 0.1 us)
Async XLA Ops:
  9.2 2.8 %collective-permute-start = (f32[8,264,128]{2,1,0:T(8,128)S(1)}, f32[8,264,128]{2,1,0:T(8,128)S(1)}, u32[]{:S(2)}, u32[]{:S(2)}) collective-permute-start(f32[8,264,128]{2,1,0:T(8,128)S(1)} %get-tuple-element.13), channel_id=1, source_target_pairs={{0,8},{8,0},{16,24},{24,16},{32,40},{40,32},{48,56},{56,48},{64,72... | collective-permute-start | bytes 3244040 | tf_op jit(solution)/shard_map/ppermute | solution.py:431
  12.1 21.9 %copy-start.3 = (f32[256,128]{1,0:T(8,128)S(1)}, f32[256,128]{1,0:T(8,128)}, u32[]{:S(2)}) copy-start(f32[256,128]{1,0:T(8,128)} %old_ref.2) | copy-start | bytes 393220
  34.9 18.2 %copy-start.1 = (s32[8192,8]{0,1:T(8,128)S(1)}, s32[8192,8]{0,1:T(8,128)}, u32[]{:S(2)}) copy-start(s32[8192,8]{0,1:T(8,128)} %param.7) | copy-start | bytes 786436
  34.9 20.9 %copy-start = (f32[8192,128]{1,0:T(8,128)S(1)}, f32[8192,128]{1,0:T(8,128)}, u32[]{:S(2)}) copy-start(f32[8192,128]{1,0:T(8,128)} %x_ref.1) | copy-start | bytes 12582916
  53.1 2.7 %collective-permute-start.1 = (f32[8,256,128]{2,1,0:T(8,128)S(1)}, f32[8,256,128]{2,1,0:T(8,128)S(1)}, u32[]{:S(2)}, u32[]{:S(2)}) collective-permute-start(f32[8,256,128]{2,1,0:T(8,128)S(1)} %all_to_all.16.own_ref), channel_id=1, source_target_pairs={{0,8},{8,0},{16,24},{24,16},{32,40},{40,32},{48,56},{56,48},{64,72... | collective-permute-start | bytes 3145736 | tf_op jit(solution)/shard_map/ppermute | solution.py:431
  53.1 2.7 %copy-start.2 = (s32[8192]{0:T(1024)S(1)}, s32[8192]{0:T(1024)}, u32[]{:S(2)}) copy-start(s32[8192]{0:T(1024)} %ids_ref.1) | copy-start | bytes 98308
  53.1 2.7 %copy-start.4 = (f32[16,128]{1,0:T(8,128)S(1)}, f32[16,128]{1,0:T(8,128)}, u32[]{:S(2)}) copy-start(f32[16,128]{1,0:T(8,128)} %old_ref.3) | copy-start | bytes 24580
  64.5 1.3 %collective-permute-start.2 = (f32[136,128]{1,0:T(8,128)S(1)}, f32[136,128]{1,0:T(8,128)S(1)}, u32[]{:S(2)}, u32[]{:S(2)}) collective-permute-start(f32[136,128]{1,0:T(8,128)S(1)} %get-tuple-element.17), channel_id=1, source_target_pairs={{0,8},{8,0},{16,24},{24,16},{32,40},{40,32},{48,56},{56,48},{64,72... | collective-permute-start | bytes 208904 | tf_op jit(solution)/shard_map/ppermute | solution.py:431
  65.9 4.4 %collective-permute-start.3 = (f32[136,128]{1,0:T(8,128)S(1)}, f32[136,128]{1,0:T(8,128)S(1)}, u32[]{:S(2)}, u32[]{:S(2)}) collective-permute-start(f32[136,128]{1,0:T(8,128)S(1)} %add.21), channel_id=1, source_target_pairs={{0,64},{8,72},{16,80},{24,88},{32,96},{40,104},{48,112},{56,120},{... | collective-permute-start | bytes 208904 | tf_op jit(solution)/shard_map/ppermute | solution.py:431
  70.3 5.9 %collective-permute-start.4 = (f32[136,128]{1,0:T(8,128)S(1)}, f32[136,128]{1,0:T(8,128)S(1)}, u32[]{:S(2)}, u32[]{:S(2)}) collective-permute-start(f32[136,128]{1,0:T(8,128)S(1)} %add.22), channel_id=1, source_target_pairs={{0,32},{8,40},{16,48},{24,56},{32,0},{40,8},{48,16},{56,24},{64,96... | collective-permute-start | bytes 208904 | tf_op jit(solution)/shard_map/ppermute | solution.py:431
  76.2 4.4 %collective-permute-start.5 = (f32[136,128]{1,0:T(8,128)S(1)}, f32[136,128]{1,0:T(8,128)S(1)}, u32[]{:S(2)}, u32[]{:S(2)}) collective-permute-start(f32[136,128]{1,0:T(8,128)S(1)} %add.23), channel_id=1, source_target_pairs={{0,16},{8,24},{16,0},{24,8},{32,48},{40,56},{48,32},{56,40},{64,80... | collective-permute-start | bytes 208904 | tf_op jit(solution)/shard_map/ppermute | solution.py:431
  80.6 1.3 %collective-permute-start.6 = (f32[136,128]{1,0:T(8,128)S(1)}, f32[136,128]{1,0:T(8,128)S(1)}, u32[]{:S(2)}, u32[]{:S(2)}) collective-permute-start(f32[136,128]{1,0:T(8,128)S(1)} %add.24.own_ref), channel_id=1, source_target_pairs={{0,8},{8,0},{16,24},{24,16},{32,40},{40,32},{48,56},{56,48},{64,72... | collective-permute-start | bytes 208904 | tf_op jit(solution)/shard_map/ppermute | solution.py:431

commit v8 on v7

--- a/solution.py
+++ b/solution.py
@@ -431,6 +431,14 @@
     return lax.ppermute(x, axis, [(i, i ^ bit) for i in range(n)])
 
 
+def turned(x, axis, n, ring, step):
+    def there(i):
+        y, at, core = i // (2 * ring), i // 2 % ring, i % 2
+        return (y * ring + (at + step) % ring) * 2 + core
+
+    return lax.ppermute(x, axis, [(i, there(i)) for i in range(n)])
+
+
 def local(passages, list_ids, code_ids, old_centroids, old_codebook):
     rows, width = passages.shape
     n_row = lax.axis_size("row")
@@ -458,10 +466,9 @@
         core, row, list_ids, codes_t, passages, own, other, code_counts(codes_t), old_codebook, n_row, code_prior
     )
     half = keep + swap(send, "row", n_row, 1)
-    bit = n_row // 2
-    while bit > 1:
-        half = half + swap(half, "row", n_row, bit)
-        bit //= 2
+    half = half + swap(half, "row", n_row, n_row // 2)
+    ring = n_row // 4
+    half = half + sum(turned(half, "row", n_row, ring, step) for step in range(1, ring))
     err, codebook = errors(
         core, row, half, swap(half, "row", n_row, 1), codes_t, rest, n_col, owned_codes, n_row, code_prior
     )

time: 103 us -> 101 us (0.981)
  waiting for transfers between devices: 18.7 us -> 16 us
    ppermute x7 -> x5, waiting for transfers between devices: 18.7 us -> 10.5 us  [swap(): return lax.ppermute(x, axis, [(i, i ^ bit) for i in range(n)])]
    ppermute x0 -> x3, waiting for transfers between devices: none -> 5.52 us  [turned(): return lax.ppermute(x, axis, [(i, there(i)) for i in range(n)])]
    ppermute x0 -> x3, starting transfers between devices: none -> 3.04 us  [turned(): return lax.ppermute(x, axis, [(i, there(i)) for i in range(n)])]
    ppermute x7 -> x5, starting transfers between devices: 3.08 us -> 1.04 us  [swap(): return lax.ppermute(x, axis, [(i, i ^ bit) for i in range(n)])]
  transfers between devices with their start and end apart: 7 -> 8, of which waited for: 7 -> 8; matrix products, arithmetic and copies ran while one was open for 0% -> 0% of each run, Pallas kernels for 1% -> 1%
where the time goes in v8:
time: 101 us
  blocking collectives  56.6 us (56%)
  Pallas kernels  22.4 us (22%)
  waiting for transfers between devices  16 us (16%)
  starting transfers between devices  4.07 us (4%)
    all_to_all x1, blocking collectives, local(): lax.all_to_all(pair, 'row', 0, 0, axis_index_groups=same_core, tiled=True)  21.9 us
    all_to_all x1, blocking collectives, local(): lax.all_to_all(copies, 'row', 0, 0, axis_index_groups=same_core, tiled=True)  18.2 us
    all_to_all x1, blocking collectives, local(): err = lax.all_to_all(err, 'col', 0, 0, tiled=True)  16.5 us
    ppermute x5, waiting for transfers between devices, swap(): return lax.ppermute(x, axis, [(i, i ^ bit) for i in range(n)])  10.5 us
    pallas_call x1, Pallas kernels, residuals(): pl.pallas_call(functools.partial(resid_kernel, prior=prior), in_specs=[pl...  8.74 us
    pallas_call x1, Pallas kernels, list_sums(): pl.pallas_call(sums_kernel, in_specs=[pl.BlockSpec(memory_space=pltpu.SME...  8.57 us
    ppermute x3, waiting for transfers between devices, turned(): return lax.ppermute(x, axis, [(i, there(i)) for i in range(n)])  5.52 us
    pallas_call x1, Pallas kernels, errors(): pl.pallas_call(functools.partial(errors_kernel, prior=prior), in_specs=[p...  3.32 us
  transfers between devices with their start and end apart: 8, of which 8 were waited for; matrix products, arithmetic and copies ran while one was open for 0% of the time, Pallas kernels for 1%

profile of v8, /device:TPU:0, one launch (start us, length us, event | category | flops | bytes accessed | tf_op | source)
XLA Modules:
  0.0 100.7 jit_solution(10894143804407932365)
XLA Ops:
  0.6 8.6 %list_sums.1 = (f32[8,264,128]{2,1,0:T(8,128)S(1)}, f32[8,264,128]{2,1,0:T(8,128)S(1)}) custom-call(s32[1]{0:T(128)} %bitcast.core_ref, s32[8192]{0:T(1024)} %ids_ref.1, s32[64,128]{1,0:T(8,128)} %bitcast.9, f32[8192,128]{1,0:T(8,128)} %x_ref.1), custom_call_target="tpu_custom_call" | custom-call | tf_op jit(solution)/shard_map/list_sums/pallas_call | solution.py:115
  9.2 0.1 collective-permute-start
  9.3 2.7 %collective-permute-done = f32[8,264,128]{2,1,0:T(8,128)S(1)} collective-permute-done((f32[8,264,128]{2,1,0:T(8,128)S(1)}, f32[8,264,128]{2,1,0:T(8,128)S(1)}, u32[]{:S(2)}, u32[]{:S(2)}) %collective-permute-start) | collective-permute-done | bytes 1081376 | tf_op jit(solution)/shard_map/ppermute | solution.py:431
  12.0 0.1 add.23
  12.1 0.0 copy-start.3
  12.1 21.9 %all_to_all.15.part_ref = f32[8,264,128]{2,1,0:T(8,128)S(1)} all-to-all(f32[8,264,128]{2,1,0:T(8,128)S(1)} %add.23), channel_id=1, replica_groups={{0,16,32,48,64,80,96,112},{8,24,40,56,72,88,104,120},{1,17,33,49,65,81,..., dimensions={0} | all-to-all | bytes 2162688 | tf_op jit(solution)/shard_map/all_to_all | solution.py:461
  34.0 0.0 copy-done.3
  34.0 0.8 centroids.1
  34.9 0.0 copy-start.1
  34.9 0.0 copy-start
  34.9 18.2 %all_to_all.16.own_ref = f32[8,256,128]{2,1,0:T(8,128)S(1)} all-to-all(f32[8,256,128]{2,1,0:T(8,128)S(1)} %get-tuple-element.15), channel_id=1, replica_groups={{0,16,32,48,64,80,96,112},{8,24,40,56,72,88,104,120},{1,17,33,49,65,81,..., dimensions={0} | all-to-all | bytes 2097152 | tf_op jit(solution)/shard_map/all_to_all | solution.py:463
  53.1 0.0 collective-permute-start.1
  53.1 0.0 copy-done.1
  53.1 0.0 copy-start.2
  53.1 0.0 copy-start.4
  53.1 0.9 code_counts.1.counts_ref
  54.1 1.7 %collective-permute-done.1.other_ref = f32[8,256,128]{2,1,0:T(8,128)S(1)} collective-permute-done((f32[8,256,128]{2,1,0:T(8,128)S(1)}, f32[8,256,128]{2,1,0:T(8,128)S(1)}, u32[]{:S(2)}, u32[]{:S(2)}) %collective-permute-start.1) | collective-permute-done | bytes 1048608 | tf_op jit(solution)/shard_map/ppermute | solution.py:431
  55.7 0.0 copy-done
  55.8 0.0 copy-done.2
  55.8 0.0 copy-done.4
  55.8 8.7 %residuals.1 = (f32[128,8192]{1,0:T(8,128)S(1)}, f32[136,128]{1,0:T(8,128)S(1)}, f32[136,128]{1,0:T(8,128)S(1)}) custom-call(s32[1]{0:T(128)} %bitcast.core_ref, s32[1]{0:T(128)} %bitcast.2.row_ref, s32[8192]{0:T(1024)S(1)} %copy-done.2, s32[8,8192]{1,0:T(8,128)S(1)} %bitcast.7, f32[8192,128]{1,0:T(8,128)S(1)} %copy-done, ...), custom_call_target="tpu_custom_call" | custom-call | tf_op jit(solution)/shard_map/residuals/pallas_call | solution.py:289
  64.5 0.2 collective-permute-start.2
  64.7 1.1 %collective-permute-done.2 = f32[136,128]{1,0:T(8,128)S(1)} collective-permute-done((f32[136,128]{1,0:T(8,128)S(1)}, f32[136,128]{1,0:T(8,128)S(1)}, u32[]{:S(2)}, u32[]{:S(2)}) %collective-permute-start.2) | collective-permute-done | bytes 69664 | tf_op jit(solution)/shard_map/ppermute | solution.py:431
  65.9 0.6 collective-permute-start.3
  66.5 3.8 %collective-permute-done.3 = f32[136,128]{1,0:T(8,128)S(1)} collective-permute-done((f32[136,128]{1,0:T(8,128)S(1)}, f32[136,128]{1,0:T(8,128)S(1)}, u32[]{:S(2)}, u32[]{:S(2)}) %collective-permute-start.3) | collective-permute-done | bytes 69664 | tf_op jit(solution)/shard_map/ppermute | solution.py:431
  70.3 1.2 %collective-permute-start.6 = (f32[136,128]{1,0:T(8,128)S(1)}, f32[136,128]{1,0:T(8,128)S(1)}, u32[]{:S(2)}, u32[]{:S(2)}) collective-permute-start(f32[136,128]{1,0:T(8,128)S(1)} %add.25), channel_id=1, source_target_pairs={{0,48},{8,56},{16,0},{24,8},{32,16},{40,24},{48,32},{56,40},{64,11... | collective-permute-start | bytes 208904 | tf_op jit(solution)/shard_map/ppermute | solution.py:439
  71.4 1.9 %collective-permute-start.5 = (f32[136,128]{1,0:T(8,128)S(1)}, f32[136,128]{1,0:T(8,128)S(1)}, u32[]{:S(2)}, u32[]{:S(2)}) collective-permute-start(f32[136,128]{1,0:T(8,128)S(1)} %add.25), channel_id=1, source_target_pairs={{0,32},{8,40},{16,48},{24,56},{32,0},{40,8},{48,16},{56,24},{64,96... | collective-permute-start | bytes 208904 | tf_op jit(solution)/shard_map/ppermute | solution.py:439
  73.3 0.0 collective-permute-start.4
  73.3 1.3 %collective-permute-done.6 = f32[136,128]{1,0:T(8,128)S(1)} collective-permute-done((f32[136,128]{1,0:T(8,128)S(1)}, f32[136,128]{1,0:T(8,128)S(1)}, u32[]{:S(2)}, u32[]{:S(2)}) %collective-permute-start.6) | collective-permute-done | bytes 69664 | tf_op jit(solution)/shard_map/ppermute | solution.py:439
  74.6 2.6 %collective-permute-done.5 = f32[136,128]{1,0:T(8,128)S(1)} collective-permute-done((f32[136,128]{1,0:T(8,128)S(1)}, f32[136,128]{1,0:T(8,128)S(1)}, u32[]{:S(2)}, u32[]{:S(2)}) %collective-permute-start.5) | collective-permute-done | bytes 69664 | tf_op jit(solution)/shard_map/ppermute | solution.py:439
  77.2 1.6 %collective-permute-done.4 = f32[136,128]{1,0:T(8,128)S(1)} collective-permute-done((f32[136,128]{1,0:T(8,128)S(1)}, f32[136,128]{1,0:T(8,128)S(1)}, u32[]{:S(2)}, u32[]{:S(2)}) %collective-permute-start.4) | collective-permute-done | bytes 69664 | tf_op jit(solution)/shard_map/ppermute | solution.py:439
  78.8 0.1 collective-permute-start.7
  78.9 1.2 %collective-permute-done.7.other_ref = f32[136,128]{1,0:T(8,128)S(1)} collective-permute-done((f32[136,128]{1,0:T(8,128)S(1)}, f32[136,128]{1,0:T(8,128)S(1)}, u32[]{:S(2)}, u32[]{:S(2)}) %collective-permute-start.7) | collective-permute-done | bytes 69664 | tf_op jit(solution)/shard_map/ppermute | solution.py:431
  80.2 3.3 %errors.1 = (f32[8,64,128]{2,1,0:T(8,128)S(1)}, f32[16,128]{1,0:T(8,128)}) custom-call(s32[1]{0:T(128)} %bitcast.core_ref, s32[1]{0:T(128)} %bitcast.2.row_ref, f32[136,128]{1,0:T(8,128)S(1)} %add_add_fusion.own_ref, f32[136,128]{1,0:T(8,128)S(1)} %collective-permute-done.7.other_ref, s32[8,8192]{1,0:T(8,128)S(1)} %bitcast.8, ...), custom_call_target="tpu_custom_call" | custom-call | tf_op jit(solution)/shard_map/errors/pallas_call | solution.py:411
  83.5 16.5 %all_to_all.17 = f32[8,64,128]{2,1,0:T(8,128)S(1)} all-to-all(f32[8,64,128]{2,1,0:T(8,128)S(1)} %get-tuple-element.20), channel_id=1, replica_groups=mesh['row'=16,'col'=8] {'col'}, dimensions={0} | all-to-all | bytes 524288 | tf_op jit(solution)/shard_map/all_to_all | solution.py:475
  100.1 0.6 multiply_bitcast_fusion
  (4 shorter events, 0.1 us)
Async XLA Ops:
  9.2 2.8 %collective-permute-start = (f32[8,264,128]{2,1,0:T(8,128)S(1)}, f32[8,264,128]{2,1,0:T(8,128)S(1)}, u32[]{:S(2)}, u32[]{:S(2)}) collective-permute-start(f32[8,264,128]{2,1,0:T(8,128)S(1)} %get-tuple-element.13), channel_id=1, source_target_pairs={{0,8},{8,0},{16,24},{24,16},{32,40},{40,32},{48,56},{56,48},{64,72... | collective-permute-start | bytes 3244040 | tf_op jit(solution)/shard_map/ppermute | solution.py:431
  12.1 21.9 %copy-start.3 = (f32[256,128]{1,0:T(8,128)S(1)}, f32[256,128]{1,0:T(8,128)}, u32[]{:S(2)}) copy-start(f32[256,128]{1,0:T(8,128)} %old_ref.2) | copy-start | bytes 393220
  34.9 18.2 %copy-start.1 = (s32[8192,8]{0,1:T(8,128)S(1)}, s32[8192,8]{0,1:T(8,128)}, u32[]{:S(2)}) copy-start(s32[8192,8]{0,1:T(8,128)} %param.7) | copy-start | bytes 786436
  34.9 20.9 %copy-start = (f32[8192,128]{1,0:T(8,128)S(1)}, f32[8192,128]{1,0:T(8,128)}, u32[]{:S(2)}) copy-start(f32[8192,128]{1,0:T(8,128)} %x_ref.1) | copy-start | bytes 12582916
  53.1 2.7 %collective-permute-start.1 = (f32[8,256,128]{2,1,0:T(8,128)S(1)}, f32[8,256,128]{2,1,0:T(8,128)S(1)}, u32[]{:S(2)}, u32[]{:S(2)}) collective-permute-start(f32[8,256,128]{2,1,0:T(8,128)S(1)} %all_to_all.16.own_ref), channel_id=1, source_target_pairs={{0,8},{8,0},{16,24},{24,16},{32,40},{40,32},{48,56},{56,48},{64,72... | collective-permute-start | bytes 3145736 | tf_op jit(solution)/shard_map/ppermute | solution.py:431
  53.1 2.7 %copy-start.2 = (s32[8192]{0:T(1024)S(1)}, s32[8192]{0:T(1024)}, u32[]{:S(2)}) copy-start(s32[8192]{0:T(1024)} %ids_ref.1) | copy-start | bytes 98308
  53.1 2.7 %copy-start.4 = (f32[16,128]{1,0:T(8,128)S(1)}, f32[16,128]{1,0:T(8,128)}, u32[]{:S(2)}) copy-start(f32[16,128]{1,0:T(8,128)} %old_ref.3) | copy-start | bytes 24580
  64.5 1.3 %collective-permute-start.2 = (f32[136,128]{1,0:T(8,128)S(1)}, f32[136,128]{1,0:T(8,128)S(1)}, u32[]{:S(2)}, u32[]{:S(2)}) collective-permute-start(f32[136,128]{1,0:T(8,128)S(1)} %get-tuple-element.17), channel_id=1, source_target_pairs={{0,8},{8,0},{16,24},{24,16},{32,40},{40,32},{48,56},{56,48},{64,72... | collective-permute-start | bytes 208904 | tf_op jit(solution)/shard_map/ppermute | solution.py:431
  65.9 4.4 %collective-permute-start.3 = (f32[136,128]{1,0:T(8,128)S(1)}, f32[136,128]{1,0:T(8,128)S(1)}, u32[]{:S(2)}, u32[]{:S(2)}) collective-permute-start(f32[136,128]{1,0:T(8,128)S(1)} %add.24), channel_id=1, source_target_pairs={{0,64},{8,72},{16,80},{24,88},{32,96},{40,104},{48,112},{56,120},{... | collective-permute-start | bytes 208904 | tf_op jit(solution)/shard_map/ppermute | solution.py:431
  70.3 4.4 %collective-permute-start.6 = (f32[136,128]{1,0:T(8,128)S(1)}, f32[136,128]{1,0:T(8,128)S(1)}, u32[]{:S(2)}, u32[]{:S(2)}) collective-permute-start(f32[136,128]{1,0:T(8,128)S(1)} %add.25), channel_id=1, source_target_pairs={{0,48},{8,56},{16,0},{24,8},{32,16},{40,24},{48,32},{56,40},{64,11... | collective-permute-start | bytes 208904 | tf_op jit(solution)/shard_map/ppermute | solution.py:439
  71.4 5.8 %collective-permute-start.5 = (f32[136,128]{1,0:T(8,128)S(1)}, f32[136,128]{1,0:T(8,128)S(1)}, u32[]{:S(2)}, u32[]{:S(2)}) collective-permute-start(f32[136,128]{1,0:T(8,128)S(1)} %add.25), channel_id=1, source_target_pairs={{0,32},{8,40},{16,48},{24,56},{32,0},{40,8},{48,16},{56,24},{64,96... | collective-permute-start | bytes 208904 | tf_op jit(solution)/shard_map/ppermute | solution.py:439
  73.3 5.5 %collective-permute-start.4 = (f32[136,128]{1,0:T(8,128)S(1)}, f32[136,128]{1,0:T(8,128)S(1)}, u32[]{:S(2)}, u32[]{:S(2)}) collective-permute-start(f32[136,128]{1,0:T(8,128)S(1)} %add.25), channel_id=1, source_target_pairs={{0,16},{8,24},{16,32},{24,40},{32,48},{40,56},{48,0},{56,8},{64,80... | collective-permute-start | bytes 208904 | tf_op jit(solution)/shard_map/ppermute | solution.py:439
  78.8 1.3 %collective-permute-start.7 = (f32[136,128]{1,0:T(8,128)S(1)}, f32[136,128]{1,0:T(8,128)S(1)}, u32[]{:S(2)}, u32[]{:S(2)}) collective-permute-start(f32[136,128]{1,0:T(8,128)S(1)} %add_add_fusion.own_ref), channel_id=1, source_target_pairs={{0,8},{8,0},{16,24},{24,16},{32,40},{40,32},{48,56},{56,48},{64,72... | collective-permute-start | bytes 208904 | tf_op jit(solution)/shard_map/ppermute | solution.py:431

commit v9 on v8

--- a/solution.py
+++ b/solution.py
@@ -465,8 +465,8 @@
     rest, keep, send = residuals(
         core, row, list_ids, codes_t, passages, own, other, code_counts(codes_t), old_codebook, n_row, code_prior
     )
-    half = keep + swap(send, "row", n_row, 1)
-    half = half + swap(half, "row", n_row, n_row // 2)
+    far = n_row // 2
+    half = keep + swap(send, "row", n_row, 1) + swap(keep, "row", n_row, far) + swap(send, "row", n_row, far + 1)
     ring = n_row // 4
     half = half + sum(turned(half, "row", n_row, ring, step) for step in range(1, ring))
     err, codebook = errors(

time: 101 us -> 101 us (level)
  waiting for transfers between devices: 16 us -> 14.3 us
  starting transfers between devices: 4.07 us -> 5.43 us
    ppermute x5 -> x6, waiting for transfers between devices: 10.5 us -> 8.55 us  [swap(): return lax.ppermute(x, axis, [(i, i ^ bit) for i in range(n)])]
    ppermute x5 -> x6, starting transfers between devices: 1.04 us -> 2.39 us  [swap(): return lax.ppermute(x, axis, [(i, i ^ bit) for i in range(n)])]
  transfers between devices with their start and end apart: 8 -> 9, of which waited for: 8 -> 7; matrix products, arithmetic and copies ran while one was open for 0% -> 0% of each run, Pallas kernels for 1% -> 1%
where the time goes in v9:
time: 101 us; the launch traced here: 100 us
  blocking collectives  56.7 us (56%)
  Pallas kernels  22.4 us (22%)
  waiting for transfers between devices  14.3 us (14%)
  starting transfers between devices  5.43 us (5%)
    all_to_all x1, blocking collectives, local(): lax.all_to_all(pair, 'row', 0, 0, axis_index_groups=same_core, tiled=True)  21.9 us
    all_to_all x1, blocking collectives, local(): lax.all_to_all(copies, 'row', 0, 0, axis_index_groups=same_core, tiled=True)  18.2 us
    all_to_all x1, blocking collectives, local(): err = lax.all_to_all(err, 'col', 0, 0, tiled=True)  16.5 us
    pallas_call x1, Pallas kernels, residuals(): pl.pallas_call(functools.partial(resid_kernel, prior=prior), in_specs=[pl...  8.73 us
    pallas_call x1, Pallas kernels, list_sums(): pl.pallas_call(sums_kernel, in_specs=[pl.BlockSpec(memory_space=pltpu.SME...  8.57 us
    ppermute x6, waiting for transfers between devices, swap(): return lax.ppermute(x, axis, [(i, i ^ bit) for i in range(n)])  8.55 us
    ppermute x3, waiting for transfers between devices, turned(): return lax.ppermute(x, axis, [(i, there(i)) for i in range(n)])  5.74 us
    pallas_call x1, Pallas kernels, errors(): pl.pallas_call(functools.partial(errors_kernel, prior=prior), in_specs=[p...  3.32 us
  transfers between devices with their start and end apart: 9, of which 7 were waited for; matrix products, arithmetic and copies ran while one was open for 0% of the time, Pallas kernels for 1%

profile of v9, /device:TPU:0, one launch (start us, length us, event | category | flops | bytes accessed | tf_op | source)
XLA Modules:
  0.0 100.3 jit_solution(12068809310386020190)
XLA Ops:
  0.6 8.6 %list_sums.1 = (f32[8,264,128]{2,1,0:T(8,128)S(1)}, f32[8,264,128]{2,1,0:T(8,128)S(1)}) custom-call(s32[1]{0:T(128)} %bitcast.core_ref, s32[8192]{0:T(1024)} %ids_ref.1, s32[64,128]{1,0:T(8,128)} %bitcast.9, f32[8192,128]{1,0:T(8,128)} %x_ref.1), custom_call_target="tpu_custom_call" | custom-call | tf_op jit(solution)/shard_map/list_sums/pallas_call | solution.py:115
  9.2 0.1 collective-permute-start
  9.3 2.7 %collective-permute-done = f32[8,264,128]{2,1,0:T(8,128)S(1)} collective-permute-done((f32[8,264,128]{2,1,0:T(8,128)S(1)}, f32[8,264,128]{2,1,0:T(8,128)S(1)}, u32[]{:S(2)}, u32[]{:S(2)}) %collective-permute-start) | collective-permute-done | bytes 1081376 | tf_op jit(solution)/shard_map/ppermute | solution.py:431
  12.0 0.1 add.26
  12.1 0.0 copy-start.3
  12.1 21.9 %all_to_all.15.part_ref = f32[8,264,128]{2,1,0:T(8,128)S(1)} all-to-all(f32[8,264,128]{2,1,0:T(8,128)S(1)} %add.26), channel_id=1, replica_groups={{0,16,32,48,64,80,96,112},{8,24,40,56,72,88,104,120},{1,17,33,49,65,81,..., dimensions={0} | all-to-all | bytes 2162688 | tf_op jit(solution)/shard_map/all_to_all | solution.py:461
  34.0 0.0 copy-done.3
  34.0 0.8 centroids.1
  34.9 0.0 copy-start.1
  34.9 0.0 copy-start
  34.9 18.2 %all_to_all.16.own_ref = f32[8,256,128]{2,1,0:T(8,128)S(1)} all-to-all(f32[8,256,128]{2,1,0:T(8,128)S(1)} %get-tuple-element.15), channel_id=1, replica_groups={{0,16,32,48,64,80,96,112},{8,24,40,56,72,88,104,120},{1,17,33,49,65,81,..., dimensions={0} | all-to-all | bytes 2097152 | tf_op jit(solution)/shard_map/all_to_all | solution.py:463
  53.1 0.0 collective-permute-start.1
  53.1 0.0 copy-done.1
  53.1 0.0 copy-start.2
  53.1 0.0 copy-start.4
  53.1 0.9 code_counts.1.counts_ref
  54.1 1.7 %collective-permute-done.1.other_ref = f32[8,256,128]{2,1,0:T(8,128)S(1)} collective-permute-done((f32[8,256,128]{2,1,0:T(8,128)S(1)}, f32[8,256,128]{2,1,0:T(8,128)S(1)}, u32[]{:S(2)}, u32[]{:S(2)}) %collective-permute-start.1) | collective-permute-done | bytes 1048608 | tf_op jit(solution)/shard_map/ppermute | solution.py:431
  55.8 0.0 copy-done
  55.8 0.0 copy-done.2
  55.8 0.0 copy-done.4
  55.8 8.7 %residuals.1 = (f32[128,8192]{1,0:T(8,128)S(1)}, f32[136,128]{1,0:T(8,128)S(1)}, f32[136,128]{1,0:T(8,128)S(1)}) custom-call(s32[1]{0:T(128)} %bitcast.core_ref, s32[1]{0:T(128)} %bitcast.2.row_ref, s32[8192]{0:T(1024)S(1)} %copy-done.2, s32[8,8192]{1,0:T(8,128)S(1)} %bitcast.7, f32[8192,128]{1,0:T(8,128)S(1)} %copy-done, ...), custom_call_target="tpu_custom_call" | custom-call | tf_op jit(solution)/shard_map/residuals/pallas_call | solution.py:289
  64.5 0.6 collective-permute-start.3
  65.2 0.9 collective-permute-start.4
  66.1 0.6 collective-permute-start.2
  66.7 2.9 %collective-permute-done.3 = f32[136,128]{1,0:T(8,128)S(1)} collective-permute-done((f32[136,128]{1,0:T(8,128)S(1)}, f32[136,128]{1,0:T(8,128)S(1)}, u32[]{:S(2)}, u32[]{:S(2)}) %collective-permute-start.3) | collective-permute-done | bytes 69664 | tf_op jit(solution)/shard_map/ppermute | solution.py:431
  69.6 0.0 collective-permute-done.4
  69.6 0.0 collective-permute-done.2
  69.7 1.5 %collective-permute-start.7 = (f32[136,128]{1,0:T(8,128)S(1)}, f32[136,128]{1,0:T(8,128)S(1)}, u32[]{:S(2)}, u32[]{:S(2)}) collective-permute-start(f32[136,128]{1,0:T(8,128)S(1)} %add_add_fusion.1), channel_id=1, source_target_pairs={{0,48},{8,56},{16,0},{24,8},{32,16},{40,24},{48,32},{56,40},{64,11... | collective-permute-start | bytes 208904 | tf_op jit(solution)/shard_map/ppermute | solution.py:439
  71.1 1.6 %collective-permute-start.6 = (f32[136,128]{1,0:T(8,128)S(1)}, f32[136,128]{1,0:T(8,128)S(1)}, u32[]{:S(2)}, u32[]{:S(2)}) collective-permute-start(f32[136,128]{1,0:T(8,128)S(1)} %add_add_fusion.1), channel_id=1, source_target_pairs={{0,32},{8,40},{16,48},{24,56},{32,0},{40,8},{48,16},{56,24},{64,96... | collective-permute-start | bytes 208904 | tf_op jit(solution)/shard_map/ppermute | solution.py:439
  72.7 0.0 collective-permute-start.5
  72.7 2.0 %collective-permute-done.7 = f32[136,128]{1,0:T(8,128)S(1)} collective-permute-done((f32[136,128]{1,0:T(8,128)S(1)}, f32[136,128]{1,0:T(8,128)S(1)}, u32[]{:S(2)}, u32[]{:S(2)}) %collective-permute-start.7) | collective-permute-done | bytes 69664 | tf_op jit(solution)/shard_map/ppermute | solution.py:439
  74.7 2.7 %collective-permute-done.6 = f32[136,128]{1,0:T(8,128)S(1)} collective-permute-done((f32[136,128]{1,0:T(8,128)S(1)}, f32[136,128]{1,0:T(8,128)S(1)}, u32[]{:S(2)}, u32[]{:S(2)}) %collective-permute-start.6) | collective-permute-done | bytes 69664 | tf_op jit(solution)/shard_map/ppermute | solution.py:439
  77.4 1.0 %collective-permute-done.5 = f32[136,128]{1,0:T(8,128)S(1)} collective-permute-done((f32[136,128]{1,0:T(8,128)S(1)}, f32[136,128]{1,0:T(8,128)S(1)}, u32[]{:S(2)}, u32[]{:S(2)}) %collective-permute-start.5) | collective-permute-done | bytes 69664 | tf_op jit(solution)/shard_map/ppermute | solution.py:439
  78.5 0.1 collective-permute-start.8
  78.6 1.2 %collective-permute-done.8.other_ref = f32[136,128]{1,0:T(8,128)S(1)} collective-permute-done((f32[136,128]{1,0:T(8,128)S(1)}, f32[136,128]{1,0:T(8,128)S(1)}, u32[]{:S(2)}, u32[]{:S(2)}) %collective-permute-start.8) | collective-permute-done | bytes 69664 | tf_op jit(solution)/shard_map/ppermute | solution.py:431
  79.8 3.3 %errors.1 = (f32[8,64,128]{2,1,0:T(8,128)S(1)}, f32[16,128]{1,0:T(8,128)}) custom-call(s32[1]{0:T(128)} %bitcast.core_ref, s32[1]{0:T(128)} %bitcast.2.row_ref, f32[136,128]{1,0:T(8,128)S(1)} %add_add_fusion.own_ref, f32[136,128]{1,0:T(8,128)S(1)} %collective-permute-done.8.other_ref, s32[8,8192]{1,0:T(8,128)S(1)} %bitcast.8, ...), custom_call_target="tpu_custom_call" | custom-call | tf_op jit(solution)/shard_map/errors/pallas_call | solution.py:411
  83.1 16.5 %all_to_all.17 = f32[8,64,128]{2,1,0:T(8,128)S(1)} all-to-all(f32[8,64,128]{2,1,0:T(8,128)S(1)} %get-tuple-element.20), channel_id=1, replica_groups=mesh['row'=16,'col'=8] {'col'}, dimensions={0} | all-to-all | bytes 524288 | tf_op jit(solution)/shard_map/all_to_all | solution.py:475
  99.7 0.6 multiply_bitcast_fusion
  (3 shorter events, 0.1 us)
Async XLA Ops:
  9.2 2.8 %collective-permute-start = (f32[8,264,128]{2,1,0:T(8,128)S(1)}, f32[8,264,128]{2,1,0:T(8,128)S(1)}, u32[]{:S(2)}, u32[]{:S(2)}) collective-permute-start(f32[8,264,128]{2,1,0:T(8,128)S(1)} %get-tuple-element.13), channel_id=1, source_target_pairs={{0,8},{8,0},{16,24},{24,16},{32,40},{40,32},{48,56},{56,48},{64,72... | collective-permute-start | bytes 3244040 | tf_op jit(solution)/shard_map/ppermute | solution.py:431
  12.1 21.9 %copy-start.3 = (f32[256,128]{1,0:T(8,128)S(1)}, f32[256,128]{1,0:T(8,128)}, u32[]{:S(2)}) copy-start(f32[256,128]{1,0:T(8,128)} %old_ref.2) | copy-start | bytes 393220
  34.9 18.2 %copy-start.1 = (s32[8192,8]{0,1:T(8,128)S(1)}, s32[8192,8]{0,1:T(8,128)}, u32[]{:S(2)}) copy-start(s32[8192,8]{0,1:T(8,128)} %param.7) | copy-start | bytes 786436
  34.9 20.9 %copy-start = (f32[8192,128]{1,0:T(8,128)S(1)}, f32[8192,128]{1,0:T(8,128)}, u32[]{:S(2)}) copy-start(f32[8192,128]{1,0:T(8,128)} %x_ref.1) | copy-start | bytes 12582916
  53.1 2.7 %collective-permute-start.1 = (f32[8,256,128]{2,1,0:T(8,128)S(1)}, f32[8,256,128]{2,1,0:T(8,128)S(1)}, u32[]{:S(2)}, u32[]{:S(2)}) collective-permute-start(f32[8,256,128]{2,1,0:T(8,128)S(1)} %all_to_all.16.own_ref), channel_id=1, source_target_pairs={{0,8},{8,0},{16,24},{24,16},{32,40},{40,32},{48,56},{56,48},{64,72... | collective-permute-start | bytes 3145736 | tf_op jit(solution)/shard_map/ppermute | solution.py:431
  53.1 2.7 %copy-start.2 = (s32[8192]{0:T(1024)S(1)}, s32[8192]{0:T(1024)}, u32[]{:S(2)}) copy-start(s32[8192]{0:T(1024)} %ids_ref.1) | copy-start | bytes 98308
  53.1 2.7 %copy-start.4 = (f32[16,128]{1,0:T(8,128)S(1)}, f32[16,128]{1,0:T(8,128)}, u32[]{:S(2)}) copy-start(f32[16,128]{1,0:T(8,128)} %old_ref.3) | copy-start | bytes 24580
  64.5 5.1 %collective-permute-start.3 = (f32[136,128]{1,0:T(8,128)S(1)}, f32[136,128]{1,0:T(8,128)S(1)}, u32[]{:S(2)}, u32[]{:S(2)}) collective-permute-start(f32[136,128]{1,0:T(8,128)S(1)} %get-tuple-element.16), channel_id=1, source_target_pairs={{0,64},{8,72},{16,80},{24,88},{32,96},{40,104},{48,112},{56,120},{... | collective-permute-start | bytes 208904 | tf_op jit(solution)/shard_map/ppermute | solution.py:431
  65.2 4.5 %collective-permute-start.4 = (f32[136,128]{1,0:T(8,128)S(1)}, f32[136,128]{1,0:T(8,128)S(1)}, u32[]{:S(2)}, u32[]{:S(2)}) collective-permute-start(f32[136,128]{1,0:T(8,128)S(1)} %get-tuple-element.17), channel_id=1, source_target_pairs={{0,72},{8,64},{16,88},{24,80},{32,104},{40,96},{48,120},{56,112},{... | collective-permute-start | bytes 208904 | tf_op jit(solution)/shard_map/ppermute | solution.py:431
  66.1 3.6 %collective-permute-start.2 = (f32[136,128]{1,0:T(8,128)S(1)}, f32[136,128]{1,0:T(8,128)S(1)}, u32[]{:S(2)}, u32[]{:S(2)}) collective-permute-start(f32[136,128]{1,0:T(8,128)S(1)} %get-tuple-element.17), channel_id=1, source_target_pairs={{0,8},{8,0},{16,24},{24,16},{32,40},{40,32},{48,56},{56,48},{64,72... | collective-permute-start | bytes 208904 | tf_op jit(solution)/shard_map/ppermute | solution.py:431
  69.7 5.0 %collective-permute-start.7 = (f32[136,128]{1,0:T(8,128)S(1)}, f32[136,128]{1,0:T(8,128)S(1)}, u32[]{:S(2)}, u32[]{:S(2)}) collective-permute-start(f32[136,128]{1,0:T(8,128)S(1)} %add_add_fusion.1), channel_id=1, source_target_pairs={{0,48},{8,56},{16,0},{24,8},{32,16},{40,24},{48,32},{56,40},{64,11... | collective-permute-start | bytes 208904 | tf_op jit(solution)/shard_map/ppermute | solution.py:439
  71.1 6.3 %collective-permute-start.6 = (f32[136,128]{1,0:T(8,128)S(1)}, f32[136,128]{1,0:T(8,128)S(1)}, u32[]{:S(2)}, u32[]{:S(2)}) collective-permute-start(f32[136,128]{1,0:T(8,128)S(1)} %add_add_fusion.1), channel_id=1, source_target_pairs={{0,32},{8,40},{16,48},{24,56},{32,0},{40,8},{48,16},{56,24},{64,96... | collective-permute-start | bytes 208904 | tf_op jit(solution)/shard_map/ppermute | solution.py:439
  72.7 5.7 %collective-permute-start.5 = (f32[136,128]{1,0:T(8,128)S(1)}, f32[136,128]{1,0:T(8,128)S(1)}, u32[]{:S(2)}, u32[]{:S(2)}) collective-permute-start(f32[136,128]{1,0:T(8,128)S(1)} %add_add_fusion.1), channel_id=1, source_target_pairs={{0,16},{8,24},{16,32},{24,40},{32,48},{40,56},{48,0},{56,8},{64,80... | collective-permute-start | bytes 208904 | tf_op jit(solution)/shard_map/ppermute | solution.py:439
  78.5 1.3 %collective-permute-start.8 = (f32[136,128]{1,0:T(8,128)S(1)}, f32[136,128]{1,0:T(8,128)S(1)}, u32[]{:S(2)}, u32[]{:S(2)}) collective-permute-start(f32[136,128]{1,0:T(8,128)S(1)} %add_add_fusion.own_ref), channel_id=1, source_target_pairs={{0,8},{8,0},{16,24},{24,16},{32,40},{40,32},{48,56},{56,48},{64,72... | collective-permute-start | bytes 208904 | tf_op jit(solution)/shard_map/ppermute | solution.py:431
